TPU v7x, 32 devices: a whole 2x2x4 slice. The times are simulated.
32 devices in a mesh: island: 8 (over y, x, core), fsdp: 4 (over z).
Axes of the slice: x: 2, y: 2, z: 4, core: 2. Of those that a mesh axis runs over, the one named last changes fastest.
Arguments:
- tokens: bfloat16 [16384, 2048], P(('island', 'fsdp')), may hold values from -6 to 6
- cotangent: bfloat16 [16384, 2048], P(('island', 'fsdp')), may hold values from -0.125 to 0.125
- norm_gain: float32 [8, 2048], P('island'), may hold values from 0.5 to 1.5
- qkv_weight: bfloat16 [8, 2048, 1536], P('island', 'fsdp'), may hold values from -0.125 to 0.125
- out_weight: bfloat16 [8, 1024, 2048], P('island', 'fsdp'), may hold values from -0.1875 to 0.1875
- gain_first: float32 [8, 2048], P('island'), may hold values from -2 to 2
- gain_second: float32 [8, 2048], P('island'), may hold values from 0.01 to 1
- qkv_first: float32 [8, 2048, 1536], P('island', 'fsdp'), may hold values from -2 to 2
- qkv_second: float32 [8, 2048, 1536], P('island', 'fsdp'), may hold values from 0.01 to 1
- out_first: float32 [8, 1024, 2048], P('island', 'fsdp'), may hold values from -2 to 2
- out_second: float32 [8, 1024, 2048], P('island', 'fsdp'), may hold values from 0.01 to 1
- gain_global: float32 [2048], replicated, may hold values from 0.5 to 1.5
- gain_momentum: float32 [2048], replicated, may hold values from -1 to 1
- qkv_global: float32 [2048, 1536], P('fsdp', 'island'), may hold values from -0.125 to 0.125
- qkv_momentum: float32 [2048, 1536], P('fsdp', 'island'), may hold values from -0.1 to 0.1
- out_global: float32 [1024, 2048], P('fsdp', 'island'), may hold values from -0.1875 to 0.1875
- out_momentum: float32 [1024, 2048], P('fsdp', 'island'), may hold values from -0.1 to 0.1
Outputs:
- gain_next: float32 [8, 2048], P('island')
- qkv_next: bfloat16 [8, 2048, 1536], P('island', 'fsdp')
- out_next: bfloat16 [8, 1024, 2048], P('island', 'fsdp')
- gain_first_next: float32 [8, 2048], P('island')
- gain_second_next: float32 [8, 2048], P('island')
- qkv_first_next: float32 [8, 2048, 1536], P('island', 'fsdp')
- qkv_second_next: float32 [8, 2048, 1536], P('island', 'fsdp')
- out_first_next: float32 [8, 1024, 2048], P('island', 'fsdp')
- out_second_next: float32 [8, 1024, 2048], P('island', 'fsdp')
- gain_global_next: float32 [2048], replicated
- gain_momentum_next: float32 [2048], replicated
- qkv_global_next: float32 [2048, 1536], P('fsdp', 'island')
- qkv_momentum_next: float32 [2048, 1536], P('fsdp', 'island')
- out_global_next: float32 [1024, 2048], P('fsdp', 'island')
- out_momentum_next: float32 [1024, 2048], P('fsdp', 'island')
All inputs are finite; a program needn't handle non-finite values.
Results may differ from a plain program's by a relative error of at most 0.01.
Values may be sent and summed in bfloat16 or wider, within the bound.
No kernel may reach another device: no remote copies, remote signals or barrier semaphores. Data moves between devices by JAX's collectives and lax.ppermute only.
A program may use at most 192 MiB of HBM per device.

v0:
```python
import jax
import jax.numpy as jnp
from jax import lax
from jax.sharding import PartitionSpec as P

HEADS = 16
KV_HEADS = 4
HEAD_DIM = 64


BETA_ONE = 0.9
BETA_TWO = 0.95
ADAM_EPS = 1e-08
INNER_RATE = 0.001
WEIGHT_DECAY = 0.1
STEP_COUNT = 100.0
OUTER_RATE = 0.7
OUTER_MOMENTUM = 0.9
MIXING = 0.5
NORM_EPS = 1e-05
ROPE_BASE = 500000.0


def rotary(heads, positions):
    half = heads.shape[-1] // 2
    freqs = ROPE_BASE ** (-jnp.arange(half, dtype=jnp.float32) / half)
    angles = positions[:, None] * freqs[None, :]
    cosine = jnp.cos(angles)[:, None, :]
    sine = jnp.sin(angles)[:, None, :]
    first = heads[..., :half]
    second = heads[..., half:]
    return jnp.concatenate(
        [first * cosine - second * sine, first * sine + second * cosine], axis=-1
    )


def attend_part(seq, gain, wqkv):
    length = seq.shape[0]
    wide = seq.astype(jnp.float32)
    factor = lax.rsqrt(jnp.mean(wide * wide, axis=-1, keepdims=True) + NORM_EPS)
    normed = (wide * factor * gain).astype(jnp.bfloat16)
    mixed = jnp.dot(normed, wqkv, preferred_element_type=jnp.float32)
    qwidth = HEADS * HEAD_DIM
    kwidth = KV_HEADS * HEAD_DIM
    queries = mixed[:, :qwidth].reshape(length, HEADS, HEAD_DIM)
    keys = mixed[:, qwidth : qwidth + kwidth].reshape(length, KV_HEADS, HEAD_DIM)
    values = mixed[:, qwidth + kwidth :].reshape(length, KV_HEADS, HEAD_DIM).astype(jnp.bfloat16)
    positions = jnp.arange(length, dtype=jnp.float32)
    queries = rotary(queries, positions).astype(jnp.bfloat16)
    keys = rotary(keys, positions).astype(jnp.bfloat16)
    queries = queries.reshape(length, KV_HEADS, HEADS // KV_HEADS, HEAD_DIM)
    scores = jnp.einsum(
        "qkgd,skd->kgqs", queries, keys, preferred_element_type=jnp.float32
    ) * HEAD_DIM ** (-0.5)
    causal = positions[:, None] >= positions[None, :]
    scores = jnp.where(causal, scores, -1e30)
    weights = jax.nn.softmax(scores, axis=-1).astype(jnp.bfloat16)
    attended = jnp.einsum("kgqs,skd->qkgd", weights, values, preferred_element_type=jnp.float32)
    return attended.astype(jnp.bfloat16).reshape(length, qwidth)


def project_out(attended, wout):
    return jnp.dot(attended, wout, preferred_element_type=jnp.float32)


def sequence_grads(seq, cot, gain, wqkv, wout):

    def loss(gain_in, qkv_in, out_in):
        return jnp.sum(
            project_out(attend_part(seq, gain_in, qkv_in), out_in) * cot.astype(jnp.float32)
        )

    return jax.grad(loss, argnums=(0, 1, 2))(gain, wqkv, wout)


def adamw(param, grad, first, second, decay):
    wide = param.astype(jnp.float32)
    first_next = BETA_ONE * first + (1.0 - BETA_ONE) * grad
    second_next = BETA_TWO * second + (1.0 - BETA_TWO) * grad * grad
    update = (
        first_next
        / (1.0 - BETA_ONE**STEP_COUNT)
        / (jnp.sqrt(second_next / (1.0 - BETA_TWO**STEP_COUNT)) + ADAM_EPS)
    )
    return (wide - INNER_RATE * (update + decay * wide), first_next, second_next)


def nesterov(global_value, momentum, average):
    delta = global_value - average
    momentum_next = OUTER_MOMENTUM * momentum + delta
    return (global_value - OUTER_RATE * (delta + OUTER_MOMENTUM * momentum_next), momentum_next)


def inner_step(tokens, cotangent, gain, local_qkv, local_out, moments):
    full_qkv, full_out = (
        lax.all_gather(local_qkv, "fsdp", axis=0, tiled=True),
        lax.all_gather(local_out, "fsdp", axis=0, tiled=True),
    )
    g_gain, g_qkv, g_out = sequence_grads(tokens, cotangent, gain, full_qkv, full_out)
    sum_qkv, sum_out = (
        lax.psum_scatter(
            g_qkv.astype(jnp.float32).astype(jnp.bfloat16), "fsdp", scatter_dimension=0, tiled=True
        ).astype(jnp.float32),
        lax.psum_scatter(
            g_out.astype(jnp.float32).astype(jnp.bfloat16), "fsdp", scatter_dimension=0, tiled=True
        ).astype(jnp.float32),
    )
    sum_gain = lax.psum(g_gain, "fsdp")
    gain_state = adamw(gain, sum_gain, moments[0], moments[1], 0.0)
    qkv_state = adamw(local_qkv, sum_qkv, moments[2], moments[3], WEIGHT_DECAY)
    out_state = adamw(local_out, sum_out, moments[4], moments[5], WEIGHT_DECAY)
    return (gain_state, qkv_state, out_state)


def outer_sync(gain, local_qkv, local_out, outer_state):
    islands = lax.axis_size("island")
    scale = 1.0 / islands
    qkv_total, out_total = (
        lax.psum_scatter(
            local_qkv.astype(jnp.float32).astype(jnp.bfloat16),
            "island",
            scatter_dimension=1,
            tiled=True,
        ).astype(jnp.float32),
        lax.psum_scatter(
            local_out.astype(jnp.float32).astype(jnp.bfloat16),
            "island",
            scatter_dimension=1,
            tiled=True,
        ).astype(jnp.float32),
    )
    gain_total = lax.psum(gain, "island")
    gain_global, gain_momentum, qkv_global, qkv_momentum, out_global, out_momentum = outer_state
    gain_pair = nesterov(gain_global, gain_momentum, gain_total * scale)
    qkv_pair = nesterov(qkv_global, qkv_momentum, qkv_total * scale)
    out_pair = nesterov(out_global, out_momentum, out_total * scale)
    qkv_whole, out_whole = (
        lax.all_gather(qkv_pair[0].astype(jnp.bfloat16), "island", axis=1, tiled=True).astype(
            jnp.float32
        ),
        lax.all_gather(out_pair[0].astype(jnp.bfloat16), "island", axis=1, tiled=True).astype(
            jnp.float32
        ),
    )
    return (gain_pair, qkv_pair, out_pair, qkv_whole, out_whole)


def shards(
    tokens,
    cotangent,
    norm_gain,
    qkv_weight,
    out_weight,
    gain_first,
    gain_second,
    qkv_first,
    qkv_second,
    out_first,
    out_second,
    gain_global,
    gain_momentum,
    qkv_global,
    qkv_momentum,
    out_global,
    out_momentum,
):
    gain = norm_gain[0]
    local_qkv = qkv_weight[0]
    local_out = out_weight[0]
    moments = (
        gain_first[0],
        gain_second[0],
        qkv_first[0],
        qkv_second[0],
        out_first[0],
        out_second[0],
    )
    outer_state = (gain_global, gain_momentum, qkv_global, qkv_momentum, out_global, out_momentum)
    stepped = inner_step(tokens, cotangent, gain, local_qkv, local_out, moments)
    synced = outer_sync(gain, local_qkv, local_out, outer_state)
    gain_state, qkv_state, out_state = stepped
    gain_pair, qkv_pair, out_pair, qkv_whole, out_whole = synced
    gain_next = MIXING * gain_state[0] + (1.0 - MIXING) * gain_pair[0]
    qkv_next = (MIXING * qkv_state[0] + (1.0 - MIXING) * qkv_whole).astype(jnp.bfloat16)
    out_next = (MIXING * out_state[0] + (1.0 - MIXING) * out_whole).astype(jnp.bfloat16)
    return (
        gain_next[None],
        qkv_next[None],
        out_next[None],
        gain_state[1][None],
        gain_state[2][None],
        qkv_state[1][None],
        qkv_state[2][None],
        out_state[1][None],
        out_state[2][None],
        gain_pair[0],
        gain_pair[1],
        qkv_pair[0],
        qkv_pair[1],
        out_pair[0],
        out_pair[1],
    )


def solution(mesh):
    placed = (
        P(("island", "fsdp"), None),
        P(("island", "fsdp"), None),
        P("island", None),
        P("island", "fsdp", None),
        P("island", "fsdp", None),
        P("island", None),
        P("island", None),
        P("island", "fsdp", None),
        P("island", "fsdp", None),
        P("island", "fsdp", None),
        P("island", "fsdp", None),
        P(),
        P(),
        P("fsdp", "island"),
        P("fsdp", "island"),
        P("fsdp", "island"),
        P("fsdp", "island"),
    )
    return jax.shard_map(
        shards,
        mesh=mesh,
        in_specs=placed,
        out_specs=(
            P("island", None),
            P("island", "fsdp", None),
            P("island", "fsdp", None),
            P("island", None),
            P("island", None),
            P("island", "fsdp", None),
            P("island", "fsdp", None),
            P("island", "fsdp", None),
            P("island", "fsdp", None),
            P(),
            P(),
            P("fsdp", "island"),
            P("fsdp", "island"),
            P("fsdp", "island"),
            P("fsdp", "island"),
        ),
        check_vma=False,
    )
```

profile of v0, /device:TPU:22, one launch (start us, length us, event | category | flops | bytes accessed | tf_op | source)
XLA Modules:
  0.0 479.5 jit_solution(6653459383477240818)
XLA Ops:
  8.1 2.7 copy.81
  10.9 0.7 reduce-scatter.11.cloned.1.call-update
  11.6 0.5 all-gather.11.cloned.1.call-update
  12.2 0.5 all-gather.13.cloned.1.call-update
  13.2 38.1 %reduce-scatter.13.cloned.1.call-done = bf16[192,512]{1,0:T(8,128)(2,1)} async-done(((bf16[1536,512]{1,0:T(8,128)(2,1)}), bf16[192,512]{1,0:T(8,128)(2,1)}) %reduce-scatter.13.cloned.1.call-update) | async-done | bytes 196624
  51.3 1.1 copy.82
  52.4 1.2 fusion.69
  53.6 1.8 copy.70
  55.7 2.1 fusion.17
  58.1 32.4 %reduce-scatter.11.cloned.1.call-done = bf16[256,256]{1,0:T(8,128)(2,1)} async-done(((bf16[256,2048]{1,0:T(8,128)(2,1)}), bf16[256,256]{1,0:T(8,128)(2,1)}) %reduce-scatter.11.cloned.1.call-update) | async-done | bytes 131088 | tf_op jit(solution)/shard_map/reduce_scatter | solution.py:125
  90.5 1.8 fusion.68
  92.6 1.2 all-gather.11.cloned.1.call-done
  93.8 5.5 %fusion.43 = bf16[512,1024]{1,0:T(8,128)(2,1)} fusion(bf16[512,2048]{1,0:T(8,128)(2,1)S(1)} %copy-done, bf16[1,1024,2048]{2,1,0:T(8,128)(2,1)} %all-gather.11.cloned.1.call-done), kind=kOutput, calls=%fused_computation.63 | convolution fusion | flops 2148007936 | bytes 7340032 | tf_op jit(solution)/shard_map/transpose(jvp())/dot_general | solution.py:63
  99.3 1.5 copy.62
  100.8 107.9 %all-gather.13.cloned.1.call-done = bf16[1,2048,1536]{2,1,0:T(8,128)(2,1)} async-done(((bf16[1,512,1536]{2,1,0:T(8,128)(2,1)}), bf16[1,2048,1536]{2,1,0:T(8,128)(2,1)}) %all-gather.13.cloned.1.call-update) | async-done | bytes 6291472 | tf_op jit(solution)/shard_map/all_gather | solution.py:96
  208.7 6.3 %fusion.11 = f32[512,1536]{1,0:T(8,128)S(1)} fusion(bf16[1,2048,1536]{2,1,0:T(8,128)(2,1)} %all-gather.13.cloned.1.call-done, bf16[512,2048]{1,0:T(8,128)(2,1)} %param.17, f32[2048]{0:T(1024)S(1)} %bitcast.182, f32[512]{0:T(512)S(1)} %add_rsqrt_fusion), kind=kOutput, calls=%fused_computation.18 | convolution fusion | flops 3225419776 | bytes 11544576 | tf_op jit(solution)/shard_map/jvp()/dot_general | solution.py:42
  215.0 1.5 slice.32
  216.5 0.8 slice.29
  217.3 0.7 slice.45
  218.0 2.9 copy.64
  221.0 2.0 copy.63
  223.0 1.9 subtract_convert_fusion
  225.1 8.0 %fusion.7 = (f32[4,4,512]{2,1,0:T(4,128)}, f32[4,512,512,4]{2,1,3,0:T(8,128)}) fusion(pred[512,512]{0,1:T(8,128)(4,1)S(1)} %iota_compare_fusion.1, bf16[512,4,4,32]{0,3,2,1:T(8,128)(2,1)S(1)} %bitcast.167, bf16[512,4,4,32]{0,3,2,1:T(8,128)(2,1)S(1)} %bitcast.165, bf16[512,4,32]{0,2,1:T(8,128)(2,1)S(1)} %get-tuple-element.86, ...), kind=kOutput, calls=%fused_computation.12 | convolution fusion | flops 552067072 | bytes 18382848 | tf_op jit(solution)/shard_map/jvp(qkgd,skd->kgqs)/dot_general | solution.py:52
  233.1 9.8 %fusion.8 = f32[4,4,512]{2,1,0:T(4,128)} fusion(f32[4,512,512,4]{2,1,3,0:T(8,128)} %get-tuple-element.90, f32[4,4,512]{2,1,0:T(4,128)} %get-tuple-element.89, pred[512,512]{0,1:T(8,128)(4,1)S(1)} %iota_compare_fusion.1), kind=kLoop, calls=%fused_computation.13 | loop fusion | flops 16769024 | bytes 17104896 | tf_op jit(solution)/shard_map/jvp()/reduce_sum | solution.py:57
  243.0 1.4 multiply_divide_fusion
  244.3 1.8 copy.66
  246.1 16.7 %divide_convert_fusion = (bf16[4,4,512,512]{2,3,1,0:T(8,128)(2,1)}, f32[4,4,512]{2,1,0:T(4,128)}, bf16[4,4,512,512]{2,3,1,0:T(8,128)(2,1)}) fusion(f32[4,512,512,4]{2,1,3,0:T(8,128)} %get-tuple-element.90, f32[4,4,512]{2,1,0:T(4,128)} %fusion.8, f32[4,4,512]{2,1,0:T(4,128)} %get-tuple-element.89, pred[512,512]{0,1:T(8,128)(4,1)S(1)} %iota_compare_fusion.1, ...), kind=kOutput, calls=%fused_computation.10 | convolution fusion | flops 578805760 | bytes 35258368 | tf_op jit(solution)/shard_map/transpose(jvp(kgqs,skd->qkgd))/dot_general | solution.py:58
  262.8 4.9 %convolution_convert_fusion.3 = bf16[4,64,4,512]{3,1,2,0:T(8,128)(2,1)S(1)} fusion(bf16[512,4,64,1]{0,2,3,1:T(8,128)(2,1)S(1)} %bitcast.174, bf16[4,4,512,512]{2,3,1,0:T(8,128)(2,1)} %get-tuple-element.70), kind=kOutput, calls=%fused_computation.60 | convolution fusion | flops 537395200 | bytes 9699328 | tf_op jit(solution)/shard_map/jvp(kgqs,skd->qkgd)/dot_general | solution.py:58
  267.8 4.3 convolution_convert_fusion.2
  272.9 11.9 %fusion.4 = bf16[4,512,512,4]{2,1,3,0:T(8,128)(2,1)S(1)} fusion(bf16[4,4,512,512]{2,3,1,0:T(8,128)(2,1)} %get-tuple-element.91, f32[4,512,512,4]{2,1,3,0:T(8,128)} %get-tuple-element.90, f32[4,512,4]{1,2,0:T(4,128)S(1)} %bitcast.181, f32[4,512,4]{1,2,0:T(4,128)S(1)} %negate_bitcast_fusion, f32[4,512,4]{1,2,0:T(4,128)S(1)} %bitcast.177, ...), kind=kLoop, calls=%fused_computation.6 | loop fusion | flops 41943040 | bytes 33914880 | tf_op jit(solution)/shard_map/transpose(jvp())/mul | solution.py:52
  284.9 2.6 fusion.50
  287.6 0.8 pad_add_fusion.6
  288.5 2.9 fusion.42
  291.4 1.9 multiply_add_fusion.1
  293.5 1.0 copy-done.3
  294.5 2.6 fusion.51
  297.2 6.8 %convolution_convert_fusion = bf16[2048,1536]{1,0:T(8,128)(2,1)} fusion(f32[512,1024]{0,1:T(8,128)S(1)} %bitcast.170, f32[512,256]{0,1:T(8,128)S(1)} %bitcast.176, bf16[512,256]{0,1:T(8,128)(2,1)S(1)} %bitcast.178, bf16[512,2048]{1,0:T(8,128)(2,1)S(1)} %copy-done.10, f32[2048]{0:T(1024)S(1)} %bitcast.183, f32[512]{0:T(512)S(1)} %add_rsqrt_fusion), kind=kOutput, calls=%fused_computation.14 | convolution fusion | flops 3230924800 | bytes 11282432 | tf_op jit(solution)/shard_map/transpose(jvp())/dot_general | solution.py:42
  304.0 11.2 %psum.15 = f32[2048]{0:T(1024)S(1)} all-reduce(f32[2048]{0:T(1024)S(1)} %bitcast.184), channel_id=1, replica_groups=mesh['island'=8,'fsdp'=4] {'island'}, use_global_device_ids=true, to_apply=%region_6.7 | all-reduce | flops 2048 | bytes 16384 | tf_op jit(solution)/shard_map/psum | solution.py:132
  315.3 0.9 copy.73
  316.3 0.9 copy.74
  317.2 2.6 copy.71
  319.8 8.2 %fusion.16 = f32[2048]{0:T(1024)S(1)} fusion(bf16[512,2048]{1,0:T(8,128)(2,1)} %param.17, f32[512]{0:T(512)S(1)} %add_rsqrt_fusion, bf16[1,2048,1536]{2,1,0:T(8,128)(2,1)} %all-gather.13.cloned.1.call-done, f32[512,1024]{0,1:T(8,128)} %bitcast.171, f32[512,256]{0,1:T(8,128)} %bitcast.175, bf16[512,256]{0,1:T(8,128)(2,1)S(1)} %bitcast.179), kind=kOutput, calls=%fused_computation.26 | convolution fusion | flops 3229874176 | bytes 11282432 | tf_op jit(solution)/shard_map/transpose(jvp())/dot_general | solution.py:42
  328.0 10.2 %psum.14 = f32[2048]{0:T(1024)S(1)} all-reduce(f32[2048]{0:T(1024)S(1)} %fusion.16), channel_id=1, replica_groups=mesh['island'=8,'fsdp'=4] {'fsdp'}, use_global_device_ids=true, to_apply=%region_5.6 | all-reduce | flops 2048 | bytes 16384 | tf_op jit(solution)/shard_map/psum | solution.py:108
  338.2 0.6 add_multiply_fusion
  338.8 11.1 %reduce-scatter.9.cloned.1.call-done = bf16[256,2048]{1,0:T(8,128)(2,1)} async-done(((bf16[1024,2048]{1,0:T(8,128)(2,1)}), bf16[256,2048]{1,0:T(8,128)(2,1)}) %reduce-scatter.9.cloned.1.call-update) | async-done | bytes 1048592 | tf_op jit(solution)/shard_map/reduce_scatter | solution.py:104
  349.9 7.2 %fusion.53 = (f32[1,256,2048]{2,1,0:T(8,128)}, bf16[1,256,2048]{2,1,0:T(8,128)(2,1)}, f32[1,256,2048]{2,1,0:T(8,128)}) fusion(bf16[256,2048]{1,0:T(8,128)(2,1)} %reduce-scatter.9.cloned.1.call-done, f32[1,256,2048]{2,1,0:T(8,128)} %param.27, bf16[256,2048]{1,0:T(8,128)(2,1)} %all-gather.9.cloned.1.call-done, f32[1,256,2048]{2,1,0:T(8,128)} %param.26, ...), kind=kLoop, calls=%fused_computation.71 | loop fusion | flops 11010048 | bytes 12582912 | tf_op jit(solution)/shard_map/broadcast_in_dim | solution.py:195
  357.1 106.4 %reduce-scatter.7.cloned.1.call-done = bf16[512,1536]{1,0:T(8,128)(2,1)} async-done(((bf16[2048,1536]{1,0:T(8,128)(2,1)}), bf16[512,1536]{1,0:T(8,128)(2,1)}) %reduce-scatter.7.cloned.1.call-update) | async-done | bytes 1572880 | tf_op jit(solution)/shard_map/reduce_scatter | solution.py:101
  463.5 8.5 %fusion.40 = (f32[1,512,1536]{2,1,0:T(8,128)}, bf16[1,512,1536]{2,1,0:T(8,128)(2,1)}, f32[1,512,1536]{2,1,0:T(8,128)}) fusion(bf16[512,1536]{1,0:T(8,128)(2,1)} %reduce-scatter.7.cloned.1.call-done, f32[1,512,1536]{2,1,0:T(8,128)} %param.25, bf16[512,1536]{1,0:T(8,128)(2,1)} %copy.71, f32[1,512,1536]{2,1,0:T(8,128)} %param.24, bf16[1,512,1536]{2,1,0:T(8,128)(2,1)} %param.20), kind=kLoop, calls=%fused_computation.58 | loop fusion | flops 16515072 | bytes 18874368 | tf_op jit(solution)/shard_map/broadcast_in_dim | solution.py:193
  (94 shorter events, 2.7 us)
Async XLA Ops:
  8.0 85.8 %copy-start = (bf16[512,2048]{1,0:T(8,128)(2,1)S(1)}, bf16[512,2048]{1,0:T(8,128)(2,1)}, u32[]{:S(2)}) copy-start(bf16[512,2048]{1,0:T(8,128)(2,1)} %param.18) | copy-start | bytes 6291460
  8.0 43.3 %reduce-scatter.13.cloned.1.call-start = ((), (), s32[]{:S(2)}) async-start(), calls=%async_computation.11 | async-start | bytes 1769472
  10.8 2.0 copy-start.19
  10.8 2.2 copy-start.20
  10.8 79.7 %reduce-scatter.11.cloned.1.call-start = ((), (), s32[]{:S(2)}) async-start(), calls=%async_computation.7 | async-start | bytes 1179648 | tf_op jit(solution)/shard_map/reduce_scatter | solution.py:125
  11.6 82.2 %all-gather.11.cloned.1.call-start = ((), (), s32[]{:S(2)}) async-start(), calls=%async_computation.9 | async-start | bytes 5242880 | tf_op jit(solution)/shard_map/all_gather | solution.py:97
  12.2 196.5 %all-gather.13.cloned.1.call-start = ((), (), s32[]{:S(2)}) async-start(), calls=%async_computation.10 | async-start | bytes 7864320 | tf_op jit(solution)/shard_map/all_gather | solution.py:96
  12.8 304.4 %all-gather.7.cloned.1.call-start = ((), (), s32[]{:S(2)}) async-start(), calls=%async_computation.5 | async-start | bytes 1769472 | tf_op jit(solution)/shard_map/all_gather | solution.py:138
  53.6 36.9 %copy-start.22 = (f32[256,256]{1,0:T(8,128)S(1)}, f32[256,256]{1,0:T(8,128)}, u32[]{:S(2)}) copy-start(f32[256,256]{1,0:T(8,128)} %param.32) | copy-start | bytes 786436
  53.6 36.9 %copy-start.23 = (f32[256,256]{1,0:T(8,128)S(1)}, f32[256,256]{1,0:T(8,128)}, u32[]{:S(2)}) copy-start(f32[256,256]{1,0:T(8,128)} %param.33) | copy-start | bytes 786436
  55.4 283.4 %all-gather.9.cloned.1.call-start = ((), (), s32[]{:S(2)}) async-start(), calls=%async_computation.8 | async-start | bytes 1179648 | tf_op jit(solution)/shard_map/all_gather | solution.py:141
  92.4 116.3 %copy-start.25 = (f32[1,2048]{1,0:T(1,128)S(1)}, f32[1,2048]{1,0:T(1,128)}, u32[]{:S(2)}) copy-start(f32[1,2048]{1,0:T(1,128)} %param.19) | copy-start | bytes 24580
  92.4 257.5 %reduce-scatter.9.cloned.1.call-start = ((), (), s32[]{:S(2)}) async-start(), calls=%async_computation.6 | async-start | bytes 5242880 | tf_op jit(solution)/shard_map/reduce_scatter | solution.py:104
  100.8 145.3 %copy-start.2 = (bf16[512,1024]{0,1:T(8,128)(2,1)}, bf16[512,1024]{0,1:T(8,128)(2,1)S(1)}, u32[]{:S(2)}) copy-start(bf16[512,1024]{0,1:T(8,128)(2,1)S(1)} %copy.62) | copy-start | bytes 3145732
  223.0 2.0 copy-start.11
  224.9 8.2 %copy-start.6 = (bf16[512,16,32]{0,2,1:T(8,128)(2,1)}, bf16[512,16,32]{0,2,1:T(8,128)(2,1)S(1)}, u32[]{:S(2)}) copy-start(bf16[512,16,32]{0,2,1:T(8,128)(2,1)S(1)} %get-tuple-element.80) | copy-start | bytes 1572868
  225.0 8.2 %copy-start.8 = (bf16[512,16,32]{0,2,1:T(8,128)(2,1)}, bf16[512,16,32]{0,2,1:T(8,128)(2,1)S(1)}, u32[]{:S(2)}) copy-start(bf16[512,16,32]{0,2,1:T(8,128)(2,1)S(1)} %get-tuple-element.81) | copy-start | bytes 1572868
  225.1 8.1 %copy-start.14 = (bf16[512,4,32]{0,2,1:T(8,128)(2,1)}, bf16[512,4,32]{0,2,1:T(8,128)(2,1)S(1)}, u32[]{:S(2)}) copy-start(bf16[512,4,32]{0,2,1:T(8,128)(2,1)S(1)} %get-tuple-element.85) | copy-start | bytes 393220
  225.1 8.0 %copy-start.16 = (bf16[512,4,32]{0,2,1:T(8,128)(2,1)}, bf16[512,4,32]{0,2,1:T(8,128)(2,1)S(1)}, u32[]{:S(2)}) copy-start(bf16[512,4,32]{0,2,1:T(8,128)(2,1)S(1)} %get-tuple-element.86) | copy-start | bytes 393220
  246.1 16.7 %copy-start.13 = (bf16[512,256]{0,1:T(8,128)(2,1)S(1)}, bf16[512,256]{0,1:T(8,128)(2,1)}, u32[]{:S(2)}) copy-start(bf16[512,256]{0,1:T(8,128)(2,1)} %copy.66) | copy-start | bytes 786436
  272.1 0.8 copy-start.26
  272.1 0.8 copy-start.21
  272.1 0.8 copy-start.24
  272.1 191.4 %reduce-scatter.7.cloned.1.call-start = ((), (), s32[]{:S(2)}) async-start(), calls=%async_computation.4 | async-start | bytes 7864320 | tf_op jit(solution)/shard_map/reduce_scatter | solution.py:101
  272.9 11.9 %copy-start.7 = (bf16[512,16,32]{0,2,1:T(8,128)(2,1)S(1)}, bf16[512,16,32]{0,2,1:T(8,128)(2,1)}, u32[]{:S(2)}) copy-start(bf16[512,16,32]{0,2,1:T(8,128)(2,1)} %copy-done.6) | copy-start | bytes 1572868
  272.9 11.9 %copy-start.9 = (bf16[512,16,32]{0,2,1:T(8,128)(2,1)S(1)}, bf16[512,16,32]{0,2,1:T(8,128)(2,1)}, u32[]{:S(2)}) copy-start(bf16[512,16,32]{0,2,1:T(8,128)(2,1)} %copy-done.8) | copy-start | bytes 1572868
  284.9 3.6 copy-start.15
  284.9 3.6 copy-start.17
  287.6 5.9 %slice-start = ((s8[8388608]{0:T(1024)(128)(4,1)}), s8[4194304]{0:T(1024)(128)(4,1)S(1)}, s32[]{:S(2)}) async-start(s8[8388608]{0:T(1024)(128)(4,1)} %bitcast.156), calls=%async_computation.12 | async-start | bytes 8388608
  288.5 5.0 %slice-start.1 = ((s8[8388608]{0:T(1024)(128)(4,1)}), s8[4194304]{0:T(1024)(128)(4,1)S(1)}, s32[]{:S(2)}) async-start(s8[8388608]{0:T(1024)(128)(4,1)} %bitcast.156), calls=%async_computation.13 | async-start | bytes 8388608
  293.3 1.2 copy-start.3
  294.5 2.7 copy-start.12
  294.5 2.7 copy-start.10
  294.5 2.7 copy-start.18
  304.0 11.3 %copy-start.29 = (f32[1,2048]{1,0:T(1,128)S(1)}, f32[1,2048]{1,0:T(1,128)}, u32[]{:S(2)}) copy-start(f32[1,2048]{1,0:T(1,128)} %param.22) | copy-start | bytes 24580
  304.0 11.3 %copy-start.30 = (f32[1,2048]{1,0:T(1,128)S(1)}, f32[1,2048]{1,0:T(1,128)}, u32[]{:S(2)}) copy-start(f32[1,2048]{1,0:T(1,128)} %param.23) | copy-start | bytes 24580
  304.0 11.3 %copy-start.5 = (f32[512,192]{1,0:T(8,128)S(1)}, f32[512,192]{1,0:T(8,128)}, u32[]{:S(2)}) copy-start(f32[512,192]{1,0:T(8,128)} %get-tuple-element.64) | copy-start | bytes 1179652
  304.0 12.3 %copy-start.4 = (f32[512,192]{1,0:T(8,128)S(1)}, f32[512,192]{1,0:T(8,128)}, u32[]{:S(2)}) copy-start(f32[512,192]{1,0:T(8,128)} %get-tuple-element.82) | copy-start | bytes 1179652
  319.8 18.4 %copy-start.27 = (f32[2048]{0:T(1024)S(1)}, f32[2048]{0:T(1024)}, u32[]{:S(2)}) copy-start(f32[2048]{0:T(1024)} %param.28) | copy-start | bytes 24580
  319.8 18.4 %copy-start.28 = (f32[2048]{0:T(1024)S(1)}, f32[2048]{0:T(1024)}, u32[]{:S(2)}) copy-start(f32[2048]{0:T(1024)} %param.29) | copy-start | bytes 24580
  319.8 30.2 %copy-start.1 = (bf16[1,256,2048]{2,1,0:T(8,128)(2,1)S(1)}, bf16[1,256,2048]{2,1,0:T(8,128)(2,1)}, u32[]{:S(2)}) copy-start(bf16[1,256,2048]{2,1,0:T(8,128)(2,1)} %param.21) | copy-start | bytes 3145732
Sparse Core Ops, SparseCore 0:
  12.7 38.5 reduce-scatter.12
  54.5 35.9 reduce-scatter.10
Sparse Core Ops, SparseCore 1:
  13.6 80.1 all-gather.10
  95.2 113.4 all-gather.12
  210.4 24.6 all-gather.6
  237.0 23.4 all-gather.8
  272.2 77.6 reduce-scatter.8
  352.4 111.1 reduce-scatter.6
where the time goes:
time: 481 us; the launch traced here: 480 us
  waiting for transfers between devices  299 us (62%)
  matrix products  69 us (14%)
  other arithmetic  50.3 us (10%)
  local copies, waits for them, and re-layouts  23.4 us (5%)
  blocking collectives  21.5 us (4%)
  between operations  16 us (3%)
    all_gather x1, waiting for transfers between devices, inner_step(): lax.all_gather(local_qkv, 'fsdp', axis=0, tiled=True)  108 us
    reduce_scatter x1, waiting for transfers between devices, inner_step(): lax.psum_scatter(g_qkv.astype(jnp.float32).astype(jnp.bfloat16), 'fsdp',...  106 us
    unnamed x9, waiting for transfers between devices  39.9 us
    reduce_scatter x1, waiting for transfers between devices, outer_sync(): lax.psum_scatter(local_out.astype(jnp.float32).astype(jnp.bfloat16), 'isl...  32.4 us
    dot_general x3, matrix products, attend_part(): jnp.einsum('kgqs,skd->qkgd', weights, values, preferred_element_type=jnp....  24.3 us
    dot_general x3, matrix products, attend_part(): mixed = jnp.dot(normed, wqkv, preferred_element_type=jnp.float32)  21.2 us
    dot_general x3, matrix products, attend_part(): jnp.einsum('qkgd,skd->kgqs', queries, keys, preferred_element_type=jnp.fl...  13.6 us
    mul x1, other arithmetic, attend_part(): jnp.einsum('qkgd,skd->kgqs', queries, keys, preferred_element_type=jnp.fl...  11.9 us
  transfers between devices with their start and end apart: 8, of which 6 were waited for; matrix products, arithmetic and copies ran while one was open for 27% of the time, Pallas kernels for 0%

commit v1 on v0

v1 whole, which is shorter than its diff:
```python
import functools

import jax
import jax.numpy as jnp
from jax import lax
from jax.experimental import pallas as pl
from jax.experimental.pallas import tpu as pltpu
from jax.sharding import PartitionSpec as P

HEADS = 16
KV_HEADS = 4
HEAD_DIM = 64
GROUP = HEADS // KV_HEADS
QG = GROUP * HEAD_DIM
CG = QG + 2 * HEAD_DIM

BETA_ONE = 0.9
BETA_TWO = 0.95
ADAM_EPS = 1e-08
INNER_RATE = 0.001
WEIGHT_DECAY = 0.1
STEP_COUNT = 100.0
OUTER_RATE = 0.7
OUTER_MOMENTUM = 0.9
MIXING = 0.5
NORM_EPS = 1e-05
ROPE_BASE = 500000.0
VMEM_LIMIT = 50 * 1024 * 1024

ORDER = (1, 0, 3, 2)
F32 = jnp.float32
BF16 = jnp.bfloat16
NN = (((1,), (0,)), ((), ()))
NT = (((1,), (1,)), ((), ()))


def mm(a, b, dims=NN):
    return lax.dot_general(a, b, dims, preferred_element_type=F32)


def rope_tables(length):
    half = HEAD_DIM // 2
    freqs = ROPE_BASE ** (-jnp.arange(half, dtype=F32) / half)
    angles = jnp.arange(length, dtype=F32)[:, None] * freqs[None, :]
    cosine = jnp.cos(angles)
    sine = jnp.sin(angles)
    zero = jnp.zeros_like(sine)
    one = jnp.ones_like(sine)
    c = jnp.concatenate([cosine] * 6 + [one] * 2, axis=1)
    above = jnp.concatenate([zero, sine] * 3 + [zero] * 2, axis=1)
    below = jnp.concatenate([-sine, zero] * 3 + [zero] * 2, axis=1)
    return jnp.stack([c, above, below])


def turn(x, tab, at, sign):
    c = tab[0, :, at : at + 128]
    above = tab[1, :, at : at + 128]
    below = tab[2, :, at : at + 128]
    side = pltpu.roll(x, 32, 1) * above + pltpu.roll(x, 96, 1) * below
    return x * c + sign * side


def group_kernel(spec, idx_ref, normed, normed_t, cot, tab, gain_in, *refs):
    n, q_keys, o_keys, owners = spec
    q_cand = refs[: len(q_keys)]
    o_cand = refs[len(q_keys) : len(q_keys) + len(o_keys)]
    gq_ref, go_ref, gain_ref, wq, wo, q_sem, o_sem = refs[len(q_keys) + len(o_keys) :]
    me = idx_ref[0]
    rows = wq.shape[0] // n
    orows = wo.shape[0] // len(owners)
    plans = []
    for at, delta in enumerate(q_keys):
        src = me - delta
        here = jnp.logical_and(src >= 0, src < n)
        plans.append((here, q_cand[at], wq, src, rows, q_sem.at[at]))
    for at, delta in enumerate(o_keys):
        src = me - delta
        here = jnp.logical_and(src >= owners[0], src <= owners[-1])
        plans.append((here, o_cand[at], wo, src - owners[0], orows, o_sem.at[at]))

    def copy_of(plan):
        _, src_ref, dst, at, size, sem = plan
        start = pl.multiple_of(at * size, size)
        return pltpu.make_async_copy(src_ref, dst.at[pl.ds(start, size)], sem)

    for plan in plans:
        @pl.when(plan[0])
        def _(plan=plan):
            copy_of(plan).start()
    for plan in plans:
        @pl.when(plan[0])
        def _(plan=plan):
            copy_of(plan).wait()

    length = normed.shape[0]
    mixed = mm(normed[...], wq[...])
    datt = mm(cot[...], wo[...], NT).astype(BF16)
    kv = turn(mixed[:, QG:], tab, 128, 1.0).astype(BF16).astype(F32)
    lane = lax.broadcasted_iota(jnp.int32, kv.shape, 1)
    left = lane < HEAD_DIM
    k_left = jnp.where(left, kv, 0.0)
    v_right = jnp.where(left, 0.0, kv)
    keys = (k_left.astype(BF16), pltpu.roll(k_left, HEAD_DIM, 1).astype(BF16))
    values = (pltpu.roll(v_right, HEAD_DIM, 1).astype(BF16), v_right.astype(BF16))

    step = length // 2
    dk_t = [[None] * 2 for _ in range(2)]
    dv_t = [[None] * 2 for _ in range(2)]
    row = lax.broadcasted_iota(jnp.int32, (step, step), 0)
    col = lax.broadcasted_iota(jnp.int32, (step, step), 1)
    causal = row >= col

    def added(total, part):
        return part if total is None else total + part

    att_t = []
    dm = []
    for pair in range(QG // 128):
        qf = turn(mixed[:, pair * 128 : pair * 128 + 128], tab, 0, 1.0).astype(BF16).astype(F32) * HEAD_DIM**-0.5
        q = qf.astype(BF16)
        q_t = qf.T.astype(BF16)
        da = datt[:, pair * 128 : pair * 128 + 128]
        da_t = da.astype(F32).T.astype(BF16)
        att = [None] * 2
        dq = [None] * 2
        for half in range(2):
            key = keys[half]
            value = values[half]
            for blk in range(2):
                r0 = blk * step
                nk = r0 + step
                s = mm(q[r0 : r0 + step], key[:nk], NT)
                last = jnp.where(causal, s[:, r0:], -1e30)
                s = last if blk == 0 else jnp.concatenate([s[:, :r0], last], axis=1)
                top = jnp.max(s, axis=1, keepdims=True)
                e = jnp.exp(s - top)
                p = e * (1.0 / jnp.sum(e, axis=1, keepdims=True))
                pb = p.astype(BF16)
                att[blk] = added(att[blk], mm(pb, value[:nk]))
                dp = mm(da[r0 : r0 + step], value[:nk], NT)
                ds = (p * (dp - jnp.sum(p * dp, axis=1, keepdims=True))).astype(BF16)
                dq[blk] = added(dq[blk], mm(ds, key[:nk]))
                dv = mm(da_t[:, r0 : r0 + step], pb)
                dk = mm(q_t[:, r0 : r0 + step], ds)
                for kb in range(blk + 1):
                    cut = slice(kb * step, kb * step + step)
                    dv_t[half][kb] = added(dv_t[half][kb], dv[:, cut])
                    dk_t[half][kb] = added(dk_t[half][kb], dk[:, cut])
        att = jnp.concatenate(att, axis=0).astype(BF16).astype(F32)
        att_t.append(att.T.astype(BF16))
        dq = jnp.concatenate(dq, axis=0) * HEAD_DIM**-0.5
        dm.append(turn(dq, tab, 0, -1.0).astype(BF16))
    go_ref[...] = mm(jnp.concatenate(att_t, axis=0), cot[...]).astype(BF16)
    d_kv = []
    for kb in range(2):
        dk = dk_t[0][kb][:HEAD_DIM] + dk_t[1][kb][HEAD_DIM:]
        dv = dv_t[0][kb][:HEAD_DIM] + dv_t[1][kb][HEAD_DIM:]
        d_kv.append(jnp.concatenate([dk, dv], axis=0).T)
    dm.append(turn(jnp.concatenate(d_kv, axis=0), tab, 128, -1.0).astype(BF16))
    dm = jnp.concatenate(dm, axis=1)
    ones = jnp.ones((8, CG), BF16)
    block = 512
    for at in range(wq.shape[0] // block):
        cut = slice(at * block, at * block + block)
        g = mm(normed_t[cut, :], dm)
        gq_ref[cut, :] = g.astype(BF16)
        prod = g * wq[cut, :].astype(F32)
        high = prod.astype(BF16)
        low = (prod - high.astype(F32)).astype(BF16)
        gain_ref[:, cut] = gain_in[:, cut] + mm(ones, high, NT) + mm(ones, low, NT)


def group_step(n, owners, idx, normed, normed_t, cot, tab, gain_in, q_cand, o_cand):
    q_keys = tuple(q_cand)
    o_keys = tuple(o_cand)
    width = normed.shape[1]
    orows = o_cand[0].shape[0] * len(owners)
    whole = pl.BlockSpec(memory_space=pltpu.VMEM)
    hbm = pl.BlockSpec(memory_space=pl.ANY)
    return pl.pallas_call(
        functools.partial(group_kernel, (n, q_keys, o_keys, owners)),
        out_shape=(
            jax.ShapeDtypeStruct((width, CG), BF16),
            jax.ShapeDtypeStruct((orows, width), BF16),
            jax.ShapeDtypeStruct((8, width), F32),
        ),
        in_specs=[pl.BlockSpec(memory_space=pltpu.SMEM)] + [whole] * 5 + [hbm] * (len(q_keys) + len(o_keys)),
        out_specs=(whole, whole, whole),
        scratch_shapes=[
            pltpu.VMEM((width, CG), BF16),
            pltpu.VMEM((orows, width), BF16),
            pltpu.SemaphoreType.DMA((len(q_keys),)),
            pltpu.SemaphoreType.DMA((len(o_keys),)),
        ],
        compiler_params=pltpu.CompilerParams(vmem_limit_bytes=VMEM_LIMIT),
        cost_estimate=pl.CostEstimate(flops=4_000_000_000, bytes_accessed=12_000_000, transcendentals=1_000_000),
    )(idx, normed, normed_t, cot, tab, gain_in, *q_cand.values(), *o_cand.values())


def adam(wide, grad, first, second, decay):
    first_next = BETA_ONE * first + (1.0 - BETA_ONE) * grad
    second_next = BETA_TWO * second + (1.0 - BETA_TWO) * grad * grad
    update = (
        first_next
        / (1.0 - BETA_ONE**STEP_COUNT)
        / (jnp.sqrt(second_next / (1.0 - BETA_TWO**STEP_COUNT)) + ADAM_EPS)
    )
    return (wide - INNER_RATE * (update + decay * wide), first_next, second_next)


def mixed_step(w, grad, first, second, outer):
    stepped, first_next, second_next = adam(w.astype(F32), grad, first, second, WEIGHT_DECAY)
    new = (MIXING * stepped + (1.0 - MIXING) * outer.astype(F32)).astype(BF16)
    return new, first_next, second_next


def qkv_adam_kernel(idx_ref, *refs):
    parts = refs[: 3 * KV_HEADS]
    w, first, second, outer, new, first_next, second_next = refs[3 * KV_HEADS :]
    grads = []
    for g in range(KV_HEADS):
        own, down, up = parts[3 * g : 3 * g + 3]
        grads.append(own[...].astype(F32) + down[...].astype(F32) + up[...].astype(F32))
    grad = jnp.concatenate(
        [x[:, :QG] for x in grads]
        + [x[:, QG : QG + HEAD_DIM] for x in grads]
        + [x[:, QG + HEAD_DIM :] for x in grads],
        axis=1,
    )
    new[...], first_next[...], second_next[...] = mixed_step(
        w[...], grad, first[...], second[...], outer[...]
    )


def qkv_adam(idx, parts, w, first, second, outer):
    rows, width = w.shape
    block = 128
    steps = rows // block
    own = pl.BlockSpec((block, CG), lambda i, idx: (idx[0] * steps + i, 0))
    part = pl.BlockSpec((block, CG), lambda i, idx: (i, 0))
    full = pl.BlockSpec((block, width), lambda i, idx: (i, 0))
    return pl.pallas_call(
        qkv_adam_kernel,
        out_shape=(
            jax.ShapeDtypeStruct((rows, width), BF16),
            jax.ShapeDtypeStruct((rows, width), F32),
            jax.ShapeDtypeStruct((rows, width), F32),
        ),
        grid_spec=pltpu.PrefetchScalarGridSpec(
            num_scalar_prefetch=1,
            grid=(steps,),
            in_specs=[own, part, part] * KV_HEADS + [full] * 4,
            out_specs=(full, full, full),
        ),
        compiler_params=pltpu.CompilerParams(vmem_limit_bytes=VMEM_LIMIT),
        cost_estimate=pl.CostEstimate(flops=20_000_000, bytes_accessed=20_000_000, transcendentals=0),
    )(idx, *parts, w, first, second, outer)


def out_adam_kernel(parts_n, *refs):
    parts = refs[:parts_n]
    w, first, second, outer, new, first_next, second_next = refs[parts_n:]
    grad = parts[0][...].astype(F32)
    for part in parts[1:]:
        grad = grad + part[...].astype(F32)
    new[...], first_next[...], second_next[...] = mixed_step(
        w[...], grad, first[...], second[...], outer[...]
    )


def out_adam(parts, w, first, second, outer):
    rows, width = w.shape
    block = 64
    full = pl.BlockSpec((block, width), lambda i: (i, 0))
    return pl.pallas_call(
        functools.partial(out_adam_kernel, len(parts)),
        out_shape=(
            jax.ShapeDtypeStruct((rows, width), BF16),
            jax.ShapeDtypeStruct((rows, width), F32),
            jax.ShapeDtypeStruct((rows, width), F32),
        ),
        grid=(rows // block,),
        in_specs=[full] * (len(parts) + 4),
        out_specs=(full, full, full),
        compiler_params=pltpu.CompilerParams(vmem_limit_bytes=VMEM_LIMIT),
        cost_estimate=pl.CostEstimate(flops=20_000_000, bytes_accessed=14_000_000, transcendentals=0),
    )(*parts, w, first, second, outer)


def nesterov(global_value, momentum, average):
    delta = global_value - average
    momentum_next = OUTER_MOMENTUM * momentum + delta
    return (global_value - OUTER_RATE * (delta + OUTER_MOMENTUM * momentum_next), momentum_next)


def after(x, *others):
    return lax.optimization_barrier((x, *others))[0]


def line_gather(x, n, owners, first=None):
    got = {0: x}
    for way in (1, -1):
        held = x
        for s in range(1, n):
            pairs = [(i, i + way) for i in range(n) if 0 <= i + way < n and (i - way * (s - 1)) in owners]
            if not pairs:
                break
            held = lax.ppermute(held, "fsdp", pairs)
            got[way * s] = held
    return got


def line_reduce(blocks, n, owners, me):
    ends = []
    for way in (1, -1):
        held = None
        for s in range(1, n):
            if way < 0:
                dest = {i: s + i - n for i in range(n)}
            else:
                dest = {i: i + n - s for i in range(n)}
            pairs = [(i, i + way) for i in range(n) if 0 <= i + way < n and dest[i] in owners
                     and 0 <= dest[i] < n and (dest[i] - i) * way > 0]
            if not pairs:
                continue
            at = (me + (s - n) if way < 0 else me + (n - s)) - owners[0]
            block = lax.dynamic_index_in_dim(blocks, jnp.clip(at, 0, len(owners) - 1), 0, keepdims=False)
            if held is not None:
                block = (block.astype(F32) + held.astype(F32)).astype(BF16)
            held = lax.ppermute(block, "fsdp", pairs)
        ends.append(held)
    return ends


def all_sum(x, axis, n):
    k = 1
    while k < n:
        x = x + lax.ppermute(x, axis, [(i, i ^ k) for i in range(n)])
        k *= 2
    return x


def shards(
    tokens,
    cotangent,
    norm_gain,
    qkv_weight,
    out_weight,
    gain_first,
    gain_second,
    qkv_first,
    qkv_second,
    out_first,
    out_second,
    gain_global,
    gain_momentum,
    qkv_global,
    qkv_momentum,
    out_global,
    out_momentum,
):
    n = lax.axis_size("fsdp")
    islands = lax.axis_size("island")
    me = lax.axis_index("fsdp")
    idx = me[None].astype(jnp.int32)
    gain = norm_gain[0]
    w_qkv = qkv_weight[0]
    w_out = out_weight[0]
    rows, qkv_width = w_qkv.shape
    length, width = tokens.shape
    qw = HEADS * HEAD_DIM
    kw = KV_HEADS * HEAD_DIM
    per = n // KV_HEADS

    gathered = []
    previous = ()
    for g in ORDER:
        own = jnp.concatenate(
            [
                w_qkv[:, g * QG : (g + 1) * QG],
                w_qkv[:, qw + g * HEAD_DIM : qw + (g + 1) * HEAD_DIM],
                w_qkv[:, qw + kw + g * HEAD_DIM : qw + kw + (g + 1) * HEAD_DIM],
            ],
            axis=1,
        )
        out_own = w_out
        if previous:
            own, out_own = lax.optimization_barrier((own, out_own, *previous))[:2]
        owners = tuple(range(g * per, (g + 1) * per))
        q_cand = line_gather(own, n, tuple(range(n)))
        o_cand = line_gather(out_own, n, owners)
        previous = (q_cand[1], q_cand[-1])
        gathered.append((g, owners, q_cand, o_cand))

    wide = tokens.astype(F32)
    factor = lax.rsqrt(jnp.mean(wide * wide, axis=-1, keepdims=True) + NORM_EPS)
    normed = (wide * factor * gain).astype(BF16)
    normed_t = normed.T
    tab = rope_tables(length)

    gain_sum = jnp.zeros((8, width), F32)
    q_parts = [None] * KV_HEADS
    out_parts = []
    own_out = None
    for g, owners, q_cand, o_cand in gathered:
        g_qkv, g_out, gain_sum = group_step(
            n, owners, idx, normed, normed_t, cotangent, tab, gain_sum, q_cand, o_cand
        )
        up, down = line_reduce(g_qkv.reshape(n, rows, CG), n, tuple(range(n)), me)
        q_parts[g] = (g_qkv, down, up)
        blocks = g_out.reshape(per, g_out.shape[0] // per, width)
        ends = line_reduce(blocks, n, owners, me)
        out_parts += [x for x in ends if x is not None]
        mine = lax.dynamic_index_in_dim(blocks, jnp.clip(me - owners[0], 0, per - 1), 0, keepdims=False)
        here = jnp.logical_and(me >= owners[0], me <= owners[-1])
        own_out = mine if own_out is None else jnp.where(here, mine, own_out)

    gain_grad = all_sum(gain_sum[0], "fsdp", n) / gain
    gain_step, gain_first_next, gain_second_next = adam(gain, gain_grad, gain_first[0], gain_second[0], 0.0)

    scale = 1.0 / islands
    qkv_total = lax.psum_scatter(w_qkv, "island", scatter_dimension=1, tiled=True).astype(F32)
    out_total = lax.psum_scatter(w_out, "island", scatter_dimension=1, tiled=True).astype(F32)
    gain_total = all_sum(gain, "island", islands)
    gain_pair = nesterov(gain_global, gain_momentum, gain_total * scale)
    qkv_pair = nesterov(qkv_global, qkv_momentum, qkv_total * scale)
    out_pair = nesterov(out_global, out_momentum, out_total * scale)
    qkv_whole = lax.all_gather(qkv_pair[0].astype(BF16), "island", axis=1, tiled=True)
    out_whole = lax.all_gather(out_pair[0].astype(BF16), "island", axis=1, tiled=True)

    out_state = out_adam([own_out] + out_parts, w_out, out_first[0], out_second[0], out_whole)
    flat = [x for part in q_parts for x in part]
    qkv_state = qkv_adam(idx, flat, w_qkv, qkv_first[0], qkv_second[0], qkv_whole)
    gain_next = MIXING * gain_step + (1.0 - MIXING) * gain_pair[0]
    return (
        gain_next[None],
        qkv_state[0][None],
        out_state[0][None],
        gain_first_next[None],
        gain_second_next[None],
        qkv_state[1][None],
        qkv_state[2][None],
        out_state[1][None],
        out_state[2][None],
        gain_pair[0],
        gain_pair[1],
        qkv_pair[0],
        qkv_pair[1],
        out_pair[0],
        out_pair[1],
    )


def solution(mesh):
    placed = (
        P(("island", "fsdp"), None),
        P(("island", "fsdp"), None),
        P("island", None),
        P("island", "fsdp", None),
        P("island", "fsdp", None),
        P("island", None),
        P("island", None),
        P("island", "fsdp", None),
        P("island", "fsdp", None),
        P("island", "fsdp", None),
        P("island", "fsdp", None),
        P(),
        P(),
        P("fsdp", "island"),
        P("fsdp", "island"),
        P("fsdp", "island"),
        P("fsdp", "island"),
    )
    return jax.shard_map(
        shards,
        mesh=mesh,
        in_specs=placed,
        out_specs=(
            P("island", None),
            P("island", "fsdp", None),
            P("island", "fsdp", None),
            P("island", None),
            P("island", None),
            P("island", "fsdp", None),
            P("island", "fsdp", None),
            P("island", "fsdp", None),
            P("island", "fsdp", None),
            P(),
            P(),
            P("fsdp", "island"),
            P("fsdp", "island"),
            P("fsdp", "island"),
            P("fsdp", "island"),
        ),
        check_vma=False,
    )
```

time: 481 us -> 510 us (1.060); the launches traced: 480 us -> 501 us
  starting transfers between devices: 0.52 us -> 218 us
  waiting for transfers between devices: 299 us -> 92.4 us
  Pallas kernels: 0 us -> 84 us
  matrix products: 69 us -> 0 us
  local copies, waits for them, and re-layouts: 23.4 us -> 51.4 us
  blocking collectives: 21.5 us -> 0 us
  other arithmetic: 50.3 us -> 39.3 us
    ppermute x0 -> x77, starting transfers between devices: none -> 217 us  [the longest x36 127 us: line_reduce(): held = lax.ppermute(block, 'fsdp', pairs)]
    reduce_scatter x3 -> x1, waiting for transfers between devices: 150 us -> 0.02 us  [shards(): lax.psum_scatter(w_out, 'island', scatter_dimension=1, tiled=True)]
    all_gather x4 -> x2, waiting for transfers between devices: 109 us -> 0.02 us  [the longest x1 0.02 us: shards(): lax.all_gather(out_pair[0].astype(BF16), 'island', axis=1, tiled=True)]
    ppermute x0 -> x77, waiting for transfers between devices: none -> 92.2 us  [the longest x36 45.3 us: line_reduce(): held = lax.ppermute(block, 'fsdp', pairs)]
    pallas_call x0 -> x6, Pallas kernels: none -> 84 us  [the longest x4 66.8 us: group_step(): pl.pallas_call(functools.partial(group_kernel, (n, q_keys, o_keys, owners...]
    dot_general x11 -> x0, matrix products: 69 us -> none  [the longest x3 24.3 us: attend_part(): jnp.einsum('kgqs,skd->qkgd', weights, values, preferred_element_type=jnp....]
    unnamed x9 -> x5, waiting for transfers between devices: 39.9 us -> 0.09 us
    psum x2 -> x0, blocking collectives: 21.5 us -> none  [the longest x1 11.2 us: outer_sync(): gain_total = lax.psum(gain, 'island')]
  transfers between devices with their start and end apart: 8 -> 81, of which waited for: 6 -> 14; matrix products, arithmetic and copies ran while one was open for 27% -> 15% of each run, Pallas kernels for 0% -> 15%
where the time goes in v1:
time: 510 us; the launch traced here: 501 us
  starting transfers between devices  218 us (43%)
  waiting for transfers between devices  92.4 us (18%)
  Pallas kernels  84 us (16%)
  local copies, waits for them, and re-layouts  51.4 us (10%)
  other arithmetic  39.3 us (8%)
  between operations  15.9 us (3%)
    ppermute x36, starting transfers between devices, line_reduce(): held = lax.ppermute(block, 'fsdp', pairs)  127 us
    ppermute x36, starting transfers between devices, line_gather(): held = lax.ppermute(held, 'fsdp', pairs)  86.2 us
    pallas_call x4, Pallas kernels, group_step(): pl.pallas_call(functools.partial(group_kernel, (n, q_keys, o_keys, owners...  66.8 us
    ppermute x36, waiting for transfers between devices, line_reduce(): held = lax.ppermute(block, 'fsdp', pairs)  45.3 us
    ppermute x36, waiting for transfers between devices, line_gather(): held = lax.ppermute(held, 'fsdp', pairs)  43.7 us
    unnamed x155, local copies, waits for them, and re-layouts  28.3 us
    convert_element_type x18, other arithmetic, line_reduce(): block = (block.astype(F32) + held.astype(F32)).astype(BF16)  16.1 us
  transfers between devices with their start and end apart: 81, of which 14 were waited for; matrix products, arithmetic and copies ran while one was open for 15% of the time, Pallas kernels for 15%

profile of v1, /device:TPU:22, one launch (start us, length us, event | category | flops | bytes accessed | tf_op | source)
XLA Modules:
  0.0 500.6 jit_solution(5650475629561976245)
XLA Ops:
  7.2 2.7 copy.54
  12.0 3.5 collective-permute-start
  21.0 4.0 copy.42
  25.9 3.1 collective-permute-start.1
  36.9 3.9 collective-permute-start.12
  40.9 15.9 %collective-permute-done.1.refs_2_ = bf16[512,384]{1,0:T(8,128)(2,1)S(1)} collective-permute-done((bf16[512,384]{1,0:T(8,128)(2,1)S(1)}, bf16[512,384]{1,0:T(8,128)(2,1)S(1)}, u32[]{:S(2)}, u32[]{:S(2)}) %collective-permute-start.1) | collective-permute-done | bytes 393248 | tf_op jit(solution)/shard_map/ppermute | solution.py:308
  59.0 3.5 fusion.2
  70.1 5.6 %collective-permute-start.13 = (bf16[512,384]{1,0:T(8,128)(2,1)S(1)}, bf16[512,384]{1,0:T(8,128)(2,1)S(1)}, u32[]{:S(2)}, u32[]{:S(2)}) collective-permute-start(bf16[512,384]{1,0:T(8,128)(2,1)S(1)} %collective-permute-done.12.refs_4_), channel_id=1, source_target_pairs={{1,0},{2,1},{5,4},{6,5},{9,8},{10,9},{13,12},{14,13},{17,16},{18,1... | collective-permute-start | bytes 1179656 | tf_op jit(solution)/shard_map/ppermute | solution.py:308
  84.8 3.9 collective-permute-start.21
  88.8 2.9 collective-permute-start.7
  93.0 3.5 fusion.32.normed_t
  111.3 13.5 %collective-permute-done.11.refs_3_ = bf16[512,384]{1,0:T(8,128)(2,1)S(1)} collective-permute-done((bf16[512,384]{1,0:T(8,128)(2,1)S(1)}, bf16[512,384]{1,0:T(8,128)(2,1)S(1)}, u32[]{:S(2)}, u32[]{:S(2)}) %collective-permute-start.11) | collective-permute-done | bytes 393248 | tf_op jit(solution)/shard_map/ppermute | solution.py:308
  126.1 2.6 pad_maximum_fusion.tab
  128.7 6.3 %collective-permute-start.22 = (bf16[512,384]{1,0:T(8,128)(2,1)S(1)}, bf16[512,384]{1,0:T(8,128)(2,1)}, u32[]{:S(2)}, u32[]{:S(2)}) collective-permute-start(bf16[512,384]{1,0:T(8,128)(2,1)S(1)} %copy-done.16), channel_id=1, source_target_pairs={{1,0},{2,1},{5,4},{6,5},{9,8},{10,9},{13,12},{14,13},{17,16},{18,1... | collective-permute-start | bytes 1179656 | tf_op jit(solution)/shard_map/ppermute | solution.py:308
  135.1 4.1 copy.46.normed
  141.1 3.9 collective-permute-start.30
  148.1 16.7 %shard_map.280 = (bf16[2048,384]{1,0:T(8,128)(2,1)}, bf16[256,2048]{1,0:T(8,128)(2,1)S(1)}, f32[8,2048]{1,0:T(8,128)S(1)}) custom-call(s32[1]{0:T(128)} %bitcast.4.idx_ref, bf16[512,2048]{1,0:T(8,128)(2,1)} %copy.46.normed, bf16[2048,512]{1,0:T(8,128)(2,1)} %fusion.32.normed_t, bf16[512,2048]{1,0:T(8,128)(2,1)} %cot.7, f32[3,512,256]{2,1,0:T(8,128)} %pad_maximum_fusion.tab, ...), custom_call_target="tpu_custom_call" | custom-call | flops 4000000000 | bytes 12000000 | tf_op jit(solution)/shard_map/pallas_call | solution.py:180
  164.8 2.6 collective-permute-start.20
  178.0 6.5 %collective-permute-start.17 = (bf16[256,2048]{1,0:T(8,128)(2,1)}, bf16[256,2048]{1,0:T(8,128)(2,1)}, u32[]{:S(2)}, u32[]{:S(2)}) collective-permute-start(bf16[256,2048]{1,0:T(8,128)(2,1)} %collective-permute-done.16.refs_9_), channel_id=1, source_target_pairs={{2,3},{6,7},{10,11},{14,15},{18,19},{22,23},{26,27},{30,31}} | collective-permute-start | bytes 3145736 | tf_op jit(solution)/shard_map/ppermute | solution.py:308
  188.3 7.2 %collective-permute-done.51 = bf16[512,384]{1,0:T(8,128)(2,1)} collective-permute-done((bf16[512,384]{1,0:T(8,128)(2,1)S(1)}, bf16[512,384]{1,0:T(8,128)(2,1)}, u32[]{:S(2)}, u32[]{:S(2)}) %collective-permute-start.51) | collective-permute-done | bytes 393248 | tf_op jit(solution)/shard_map/ppermute | solution.py:330
  198.9 2.4 fusion.16
  202.9 11.0 %collective-permute-done.34.refs_9_ = bf16[256,2048]{1,0:T(8,128)(2,1)} collective-permute-done((bf16[256,2048]{1,0:T(8,128)(2,1)}, bf16[256,2048]{1,0:T(8,128)(2,1)}, u32[]{:S(2)}, u32[]{:S(2)}) %collective-permute-start.34) | collective-permute-done | bytes 1048608 | tf_op jit(solution)/shard_map/ppermute | solution.py:308
  215.9 4.0 collective-permute-start.31
  220.6 2.6 add_convert_fusion.1
  223.2 17.0 %shard_map.281 = (bf16[2048,384]{1,0:T(8,128)(2,1)}, bf16[256,2048]{1,0:T(8,128)(2,1)S(1)}, f32[8,2048]{1,0:T(8,128)S(1)}) custom-call(s32[1]{0:T(128)} %bitcast.4.idx_ref, bf16[512,2048]{1,0:T(8,128)(2,1)} %copy.46.normed, bf16[2048,512]{1,0:T(8,128)(2,1)} %fusion.32.normed_t, bf16[512,2048]{1,0:T(8,128)(2,1)} %cot.7, f32[3,512,256]{2,1,0:T(8,128)} %pad_maximum_fusion.tab, ...), custom_call_target="tpu_custom_call" | custom-call | flops 4000000000 | bytes 12000000 | tf_op jit(solution)/shard_map/pallas_call | solution.py:180
  244.3 2.5 collective-permute-start.48
  246.9 16.6 %shard_map.282 = (bf16[2048,384]{1,0:T(8,128)(2,1)}, bf16[256,2048]{1,0:T(8,128)(2,1)S(1)}, f32[8,2048]{1,0:T(8,128)S(1)}) custom-call(s32[1]{0:T(128)} %bitcast.4.idx_ref, bf16[512,2048]{1,0:T(8,128)(2,1)} %copy.46.normed, bf16[2048,512]{1,0:T(8,128)(2,1)} %fusion.32.normed_t, bf16[512,2048]{1,0:T(8,128)(2,1)} %cot.7, f32[3,512,256]{2,1,0:T(8,128)} %pad_maximum_fusion.tab, ...), custom_call_target="tpu_custom_call" | custom-call | flops 4000000000 | bytes 12000000 | tf_op jit(solution)/shard_map/pallas_call | solution.py:180
  267.8 16.6 %shard_map.283 = (bf16[2048,384]{1,0:T(8,128)(2,1)}, bf16[256,2048]{1,0:T(8,128)(2,1)}, f32[8,2048]{1,0:T(8,128)S(1)}) custom-call(s32[1]{0:T(128)} %bitcast.4.idx_ref, bf16[512,2048]{1,0:T(8,128)(2,1)} %copy.46.normed, bf16[2048,512]{1,0:T(8,128)(2,1)} %fusion.32.normed_t, bf16[512,2048]{1,0:T(8,128)(2,1)} %cot.7, f32[3,512,256]{2,1,0:T(8,128)} %pad_maximum_fusion.tab, ...), custom_call_target="tpu_custom_call" | custom-call | flops 4000000000 | bytes 12000000 | tf_op jit(solution)/shard_map/pallas_call | solution.py:180
  289.2 3.2 collective-permute-start.36
  292.5 3.3 collective-permute-done.36
  300.2 19.2 %collective-permute-start.42 = (bf16[512,384]{1,0:T(8,128)(2,1)S(1)}, bf16[512,384]{1,0:T(8,128)(2,1)S(1)}, u32[]{:S(2)}, u32[]{:S(2)}) collective-permute-start(bf16[512,384]{1,0:T(8,128)(2,1)S(1)} %get-tuple-element.116), channel_id=1, source_target_pairs={{2,1},{3,2},{6,5},{7,6},{10,9},{11,10},{14,13},{15,14},{18,17},{19... | collective-permute-start | bytes 1179656 | tf_op jit(solution)/shard_map/ppermute | solution.py:330
  330.2 21.7 %collective-permute-start.69 = (bf16[256,2048]{1,0:T(8,128)(2,1)S(1)}, bf16[256,2048]{1,0:T(8,128)(2,1)S(1)}, u32[]{:S(2)}, u32[]{:S(2)}) collective-permute-start(bf16[256,2048]{1,0:T(8,128)(2,1)S(1)} %fusion.3), channel_id=1, source_target_pairs={{2,1},{6,5},{10,9},{14,13},{18,17},{22,21},{26,25},{30,29}} | collective-permute-start | bytes 3145736 | tf_op jit(solution)/shard_map/ppermute | solution.py:330
  352.0 6.8 %collective-permute-start.54 = (bf16[512,384]{1,0:T(8,128)(2,1)S(1)}, bf16[512,384]{1,0:T(8,128)(2,1)S(1)}, u32[]{:S(2)}, u32[]{:S(2)}) collective-permute-start(bf16[512,384]{1,0:T(8,128)(2,1)S(1)} %get-tuple-element.108), channel_id=1, source_target_pairs={{2,1},{3,2},{6,5},{7,6},{10,9},{11,10},{14,13},{15,14},{18,17},{19... | collective-permute-start | bytes 1179656 | tf_op jit(solution)/shard_map/ppermute | solution.py:330
  363.0 2.6 add_convert_fusion
  365.6 6.3 %collective-permute-done.54 = bf16[512,384]{1,0:T(8,128)(2,1)S(1)} collective-permute-done((bf16[512,384]{1,0:T(8,128)(2,1)S(1)}, bf16[512,384]{1,0:T(8,128)(2,1)S(1)}, u32[]{:S(2)}, u32[]{:S(2)}) %collective-permute-start.54) | collective-permute-done | bytes 393248 | tf_op jit(solution)/shard_map/ppermute | solution.py:330
  372.3 3.8 collective-permute-done.60
  378.1 25.5 %collective-permute-start.49 = (bf16[512,384]{1,0:T(8,128)(2,1)S(1)}, bf16[512,384]{1,0:T(8,128)(2,1)S(1)}, u32[]{:S(2)}, u32[]{:S(2)}) collective-permute-start(bf16[512,384]{1,0:T(8,128)(2,1)S(1)} %fusion.18), channel_id=1, source_target_pairs={{1,0},{2,1},{3,2},{5,4},{6,5},{7,6},{9,8},{10,9},{11,10},{13,12},{... | collective-permute-start | bytes 1179656 | tf_op jit(solution)/shard_map/ppermute | solution.py:330
  403.8 4.4 collective-permute-start.46
  409.5 18.6 %collective-permute-done.52.refs_5_ = bf16[512,384]{1,0:T(8,128)(2,1)S(1)} collective-permute-done((bf16[512,384]{1,0:T(8,128)(2,1)S(1)}, bf16[512,384]{1,0:T(8,128)(2,1)S(1)}, u32[]{:S(2)}, u32[]{:S(2)}) %collective-permute-start.52) | collective-permute-done | bytes 393248 | tf_op jit(solution)/shard_map/ppermute | solution.py:330
  430.0 3.9 collective-permute-start.58
  436.7 3.2 collective-permute-start.55
  444.0 2.9 collective-permute-start.67
  453.4 4.1 collective-permute-done.61.refs_10_
  458.2 2.8 collective-permute-start.73
  465.6 2.4 select_select_fusion.refs_0_
  468.7 2.6 copy.51.refs_15_
  476.3 9.5 %shard_map.284 = (bf16[512,1536]{1,0:T(8,128)(2,1)}, f32[512,1536]{1,0:T(8,128)}, f32[512,1536]{1,0:T(8,128)}) custom-call(s32[1]{0:T(128)} %bitcast.4.idx_ref, bf16[2048,384]{1,0:T(8,128)(2,1)} %get-tuple-element.49.refs_0_, bf16[512,384]{1,0:T(8,128)(2,1)S(1)} %copy-done.33, bf16[512,384]{1,0:T(8,128)(2,1)S(1)} %copy-done.31, ...), custom_call_target="tpu_custom_call" | custom-call | flops 20000000 | bytes 20000000 | tf_op jit(solution)/shard_map/pallas_call | solution.py:242
  485.9 7.7 %shard_map.285 = (bf16[256,2048]{1,0:T(8,128)(2,1)}, f32[256,2048]{1,0:T(8,128)}, f32[256,2048]{1,0:T(8,128)}) custom-call(bf16[256,2048]{1,0:T(8,128)(2,1)S(1)} %copy-done, bf16[256,2048]{1,0:T(8,128)(2,1)S(1)} %copy-done.4, bf16[256,2048]{1,0:T(8,128)(2,1)} %collective-permute-done.67.refs_2_, bf16[256,2048]{1,0:T(8,128)(2,1)} %collective-permute-done.70.refs_3_, ...), custom_call_target="tpu_custom_call" | custom-call | flops 20000000 | bytes 14000000 | tf_op jit(solution)/shard_map/pallas_call | solution.py:275
  (335 shorter events, 141.8 us)
Async XLA Ops:
  7.2 68.7 %reduce-scatter.7.cloned.1.call-start = ((), (), s32[]{:S(2)}) async-start(), calls=%async_computation.5 | async-start | bytes 1769472
  10.0 186.2 %reduce-scatter.5.cloned.1.call-start = ((), (), s32[]{:S(2)}) async-start(), calls=%async_computation.3 | async-start | bytes 1179648 | tf_op jit(solution)/shard_map/reduce_scatter | solution.py:423
  15.5 453.2 %all-gather.3.cloned.1.call-start = ((), (), s32[]{:S(2)}) async-start(), calls=%async_computation.2 | async-start | bytes 1769472 | tf_op jit(solution)/shard_map/all_gather | solution.py:428
  17.9 52.2 %collective-permute-start.6 = (bf16[256,2048]{1,0:T(8,128)(2,1)}, bf16[256,2048]{1,0:T(8,128)(2,1)}, u32[]{:S(2)}, u32[]{:S(2)}) collective-permute-start(bf16[256,2048]{1,0:T(8,128)(2,1)} %bitcast.10.refs_7_), channel_id=1, source_target_pairs={{1,2},{5,6},{9,10},{13,14},{17,18},{21,22},{25,26},{29,30}} | collective-permute-start | bytes 3145736 | tf_op jit(solution)/shard_map/ppermute | solution.py:308
  19.2 57.7 %collective-permute-start.8 = (bf16[256,2048]{1,0:T(8,128)(2,1)}, bf16[256,2048]{1,0:T(8,128)(2,1)}, u32[]{:S(2)}, u32[]{:S(2)}) collective-permute-start(bf16[256,2048]{1,0:T(8,128)(2,1)} %bitcast.10.refs_7_), channel_id=1, source_target_pairs={{1,0},{5,4},{9,8},{13,12},{17,16},{21,20},{25,24},{29,28}} | collective-permute-start | bytes 3145736 | tf_op jit(solution)/shard_map/ppermute | solution.py:308
  25.9 30.9 %collective-permute-start.1 = (bf16[512,384]{1,0:T(8,128)(2,1)S(1)}, bf16[512,384]{1,0:T(8,128)(2,1)S(1)}, u32[]{:S(2)}, u32[]{:S(2)}) collective-permute-start(bf16[512,384]{1,0:T(8,128)(2,1)S(1)} %collective-permute-done.refs_1_), channel_id=1, source_target_pairs={{1,2},{2,3},{5,6},{6,7},{9,10},{10,11},{13,14},{14,15},{17,18},{18... | collective-permute-start | bytes 1179656 | tf_op jit(solution)/shard_map/ppermute | solution.py:308
  34.8 31.9 %collective-permute-start.9 = (bf16[512,384]{1,0:T(8,128)(2,1)S(1)}, bf16[512,384]{1,0:T(8,128)(2,1)S(1)}, u32[]{:S(2)}, u32[]{:S(2)}) collective-permute-start(bf16[512,384]{1,0:T(8,128)(2,1)S(1)} %pad_maximum_fusion.2.refs_0_), channel_id=1, source_target_pairs={{0,1},{1,2},{2,3},{4,5},{5,6},{6,7},{8,9},{9,10},{10,11},{12,13},{... | collective-permute-start | bytes 1179656 | tf_op jit(solution)/shard_map/ppermute | solution.py:308
  36.9 31.2 %collective-permute-start.12 = (bf16[512,384]{1,0:T(8,128)(2,1)S(1)}, bf16[512,384]{1,0:T(8,128)(2,1)S(1)}, u32[]{:S(2)}, u32[]{:S(2)}) collective-permute-start(bf16[512,384]{1,0:T(8,128)(2,1)S(1)} %pad_maximum_fusion.2.refs_0_), channel_id=1, source_target_pairs={{1,0},{2,1},{3,2},{5,4},{6,5},{7,6},{9,8},{10,9},{11,10},{13,12},{... | collective-permute-start | bytes 1179656 | tf_op jit(solution)/shard_map/ppermute | solution.py:308
  77.0 32.9 %collective-permute-start.15 = (bf16[256,2048]{1,0:T(8,128)(2,1)}, bf16[256,2048]{1,0:T(8,128)(2,1)}, u32[]{:S(2)}, u32[]{:S(2)}) collective-permute-start(bf16[256,2048]{1,0:T(8,128)(2,1)} %bitcast.10.refs_7_), channel_id=1, source_target_pairs={{0,1},{4,5},{8,9},{12,13},{16,17},{20,21},{24,25},{28,29}} | collective-permute-start | bytes 3145736 | tf_op jit(solution)/shard_map/ppermute | solution.py:308
  82.8 403.0 %all-gather.5.cloned.1.call-start = ((), (), s32[]{:S(2)}) async-start(), calls=%async_computation.4 | async-start | bytes 1179648 | tf_op jit(solution)/shard_map/all_gather | solution.py:429
  88.8 52.3 %collective-permute-start.7 = (bf16[256,2048]{1,0:T(8,128)(2,1)}, bf16[256,2048]{1,0:T(8,128)(2,1)}, u32[]{:S(2)}, u32[]{:S(2)}) collective-permute-start(bf16[256,2048]{1,0:T(8,128)(2,1)} %collective-permute-done.6.refs_8_), channel_id=1, source_target_pairs={{2,3},{6,7},{10,11},{14,15},{18,19},{22,23},{26,27},{30,31}} | collective-permute-start | bytes 3145736 | tf_op jit(solution)/shard_map/ppermute | solution.py:308
  91.7 33.1 %collective-permute-start.11 = (bf16[512,384]{1,0:T(8,128)(2,1)S(1)}, bf16[512,384]{1,0:T(8,128)(2,1)S(1)}, u32[]{:S(2)}, u32[]{:S(2)}) collective-permute-start(bf16[512,384]{1,0:T(8,128)(2,1)S(1)} %collective-permute-done.10.refs_2_), channel_id=1, source_target_pairs={{2,3},{6,7},{10,11},{14,15},{18,19},{22,23},{26,27},{30,31}} | collective-permute-start | bytes 1179656 | tf_op jit(solution)/shard_map/ppermute | solution.py:308
  96.5 32.2 %collective-permute-start.14 = (bf16[512,384]{1,0:T(8,128)(2,1)S(1)}, bf16[512,384]{1,0:T(8,128)(2,1)}, u32[]{:S(2)}, u32[]{:S(2)}) collective-permute-start(bf16[512,384]{1,0:T(8,128)(2,1)S(1)} %collective-permute-done.13.refs_5_), channel_id=1, source_target_pairs={{1,0},{5,4},{9,8},{13,12},{17,16},{21,20},{25,24},{29,28}} | collective-permute-start | bytes 1179656 | tf_op jit(solution)/shard_map/ppermute | solution.py:308
  98.7 40.5 %collective-permute-start.19 = (bf16[512,384]{1,0:T(8,128)(2,1)S(1)}, bf16[512,384]{1,0:T(8,128)(2,1)}, u32[]{:S(2)}, u32[]{:S(2)}) collective-permute-start(bf16[512,384]{1,0:T(8,128)(2,1)S(1)} %collective-permute-done.18.refs_1_), channel_id=1, source_target_pairs={{1,2},{2,3},{5,6},{6,7},{9,10},{10,11},{13,14},{14,15},{17,18},{18... | collective-permute-start | bytes 1179656 | tf_op jit(solution)/shard_map/ppermute | solution.py:308
  109.9 62.2 %collective-permute-start.24 = (bf16[256,2048]{1,0:T(8,128)(2,1)}, bf16[256,2048]{1,0:T(8,128)(2,1)}, u32[]{:S(2)}, u32[]{:S(2)}) collective-permute-start(bf16[256,2048]{1,0:T(8,128)(2,1)} %bitcast.10.refs_7_), channel_id=1, source_target_pairs={{3,2},{7,6},{11,10},{15,14},{19,18},{23,22},{27,26},{31,30}} | collective-permute-start | bytes 3145736 | tf_op jit(solution)/shard_map/ppermute | solution.py:308
  124.8 51.9 %collective-permute-start.16 = (bf16[256,2048]{1,0:T(8,128)(2,1)}, bf16[256,2048]{1,0:T(8,128)(2,1)}, u32[]{:S(2)}, u32[]{:S(2)}) collective-permute-start(bf16[256,2048]{1,0:T(8,128)(2,1)} %collective-permute-done.15.refs_8_), channel_id=1, source_target_pairs={{1,2},{5,6},{9,10},{13,14},{17,18},{21,22},{25,26},{29,30}} | collective-permute-start | bytes 3145736 | tf_op jit(solution)/shard_map/ppermute | solution.py:308
  128.7 36.1 %collective-permute-start.22 = (bf16[512,384]{1,0:T(8,128)(2,1)S(1)}, bf16[512,384]{1,0:T(8,128)(2,1)}, u32[]{:S(2)}, u32[]{:S(2)}) collective-permute-start(bf16[512,384]{1,0:T(8,128)(2,1)S(1)} %copy-done.16), channel_id=1, source_target_pairs={{1,0},{2,1},{5,4},{6,5},{9,8},{10,9},{13,12},{14,13},{17,16},{18,1... | collective-permute-start | bytes 1179656 | tf_op jit(solution)/shard_map/ppermute | solution.py:308
  139.2 30.2 %collective-permute-start.27 = (bf16[512,384]{1,0:T(8,128)(2,1)S(1)}, bf16[512,384]{1,0:T(8,128)(2,1)}, u32[]{:S(2)}, u32[]{:S(2)}) collective-permute-start(bf16[512,384]{1,0:T(8,128)(2,1)S(1)} %pad_maximum_fusion.4.refs_0_), channel_id=1, source_target_pairs={{0,1},{1,2},{2,3},{4,5},{5,6},{6,7},{8,9},{9,10},{10,11},{12,13},{... | collective-permute-start | bytes 1179656 | tf_op jit(solution)/shard_map/ppermute | solution.py:308
  141.1 29.7 %collective-permute-start.30 = (bf16[512,384]{1,0:T(8,128)(2,1)S(1)}, bf16[512,384]{1,0:T(8,128)(2,1)}, u32[]{:S(2)}, u32[]{:S(2)}) collective-permute-start(bf16[512,384]{1,0:T(8,128)(2,1)S(1)} %pad_maximum_fusion.4.refs_0_), channel_id=1, source_target_pairs={{1,0},{2,1},{3,2},{5,4},{6,5},{7,6},{9,8},{10,9},{11,10},{13,12},{... | collective-permute-start | bytes 1179656 | tf_op jit(solution)/shard_map/ppermute | solution.py:308
  172.1 26.0 %collective-permute-start.25 = (bf16[256,2048]{1,0:T(8,128)(2,1)}, bf16[256,2048]{1,0:T(8,128)(2,1)}, u32[]{:S(2)}, u32[]{:S(2)}) collective-permute-start(bf16[256,2048]{1,0:T(8,128)(2,1)} %collective-permute-done.24.refs_8_), channel_id=1, source_target_pairs={{2,1},{6,5},{10,9},{14,13},{18,17},{22,21},{26,25},{30,29}} | collective-permute-start | bytes 3145736 | tf_op jit(solution)/shard_map/ppermute | solution.py:308
  174.4 39.6 %collective-permute-start.34 = (bf16[256,2048]{1,0:T(8,128)(2,1)}, bf16[256,2048]{1,0:T(8,128)(2,1)}, u32[]{:S(2)}, u32[]{:S(2)}) collective-permute-start(bf16[256,2048]{1,0:T(8,128)(2,1)} %bitcast.10.refs_7_), channel_id=1, source_target_pairs={{2,1},{6,5},{10,9},{14,13},{18,17},{22,21},{26,25},{30,29}} | collective-permute-start | bytes 3145736 | tf_op jit(solution)/shard_map/ppermute | solution.py:308
  176.7 39.1 %collective-permute-start.66 = (bf16[256,2048]{1,0:T(8,128)(2,1)S(1)}, bf16[256,2048]{1,0:T(8,128)(2,1)}, u32[]{:S(2)}, u32[]{:S(2)}) collective-permute-start(bf16[256,2048]{1,0:T(8,128)(2,1)S(1)} %get-tuple-element.57), channel_id=1, source_target_pairs={{3,2},{7,6},{11,10},{15,14},{19,18},{23,22},{27,26},{31,30}} | collective-permute-start | bytes 3145736 | tf_op jit(solution)/shard_map/ppermute | solution.py:330
  178.0 41.8 %collective-permute-start.17 = (bf16[256,2048]{1,0:T(8,128)(2,1)}, bf16[256,2048]{1,0:T(8,128)(2,1)}, u32[]{:S(2)}, u32[]{:S(2)}) collective-permute-start(bf16[256,2048]{1,0:T(8,128)(2,1)} %collective-permute-done.16.refs_9_), channel_id=1, source_target_pairs={{2,3},{6,7},{10,11},{14,15},{18,19},{22,23},{26,27},{30,31}} | collective-permute-start | bytes 3145736 | tf_op jit(solution)/shard_map/ppermute | solution.py:308
  198.2 46.1 %collective-permute-start.26 = (bf16[256,2048]{1,0:T(8,128)(2,1)}, bf16[256,2048]{1,0:T(8,128)(2,1)S(1)}, u32[]{:S(2)}, u32[]{:S(2)}) collective-permute-start(bf16[256,2048]{1,0:T(8,128)(2,1)} %collective-permute-done.25.refs_9_), channel_id=1, source_target_pairs={{1,0},{5,4},{9,8},{13,12},{17,16},{21,20},{25,24},{29,28}} | collective-permute-start | bytes 3145736 | tf_op jit(solution)/shard_map/ppermute | solution.py:308
  201.4 62.0 %collective-permute-start.33 = (bf16[256,2048]{1,0:T(8,128)(2,1)}, bf16[256,2048]{1,0:T(8,128)(2,1)S(1)}, u32[]{:S(2)}, u32[]{:S(2)}) collective-permute-start(bf16[256,2048]{1,0:T(8,128)(2,1)} %bitcast.10.refs_7_), channel_id=1, source_target_pairs={{2,3},{6,7},{10,11},{14,15},{18,19},{22,23},{26,27},{30,31}} | collective-permute-start | bytes 3145736 | tf_op jit(solution)/shard_map/ppermute | solution.py:308
  213.9 26.4 %collective-permute-start.28 = (bf16[512,384]{1,0:T(8,128)(2,1)}, bf16[512,384]{1,0:T(8,128)(2,1)S(1)}, u32[]{:S(2)}, u32[]{:S(2)}) collective-permute-start(bf16[512,384]{1,0:T(8,128)(2,1)} %collective-permute-done.27.refs_1_), channel_id=1, source_target_pairs={{1,2},{2,3},{5,6},{6,7},{9,10},{10,11},{13,14},{14,15},{17,18},{18... | collective-permute-start | bytes 1179656 | tf_op jit(solution)/shard_map/ppermute | solution.py:308
  215.9 25.8 %collective-permute-start.31 = (bf16[512,384]{1,0:T(8,128)(2,1)}, bf16[512,384]{1,0:T(8,128)(2,1)S(1)}, u32[]{:S(2)}, u32[]{:S(2)}) collective-permute-start(bf16[512,384]{1,0:T(8,128)(2,1)} %collective-permute-done.30.refs_4_), channel_id=1, source_target_pairs={{1,0},{2,1},{5,4},{6,5},{9,8},{10,9},{13,12},{14,13},{17,16},{18,1... | collective-permute-start | bytes 1179656 | tf_op jit(solution)/shard_map/ppermute | solution.py:308
  219.8 46.9 %collective-permute-start.35 = (bf16[256,2048]{1,0:T(8,128)(2,1)}, bf16[256,2048]{1,0:T(8,128)(2,1)S(1)}, u32[]{:S(2)}, u32[]{:S(2)}) collective-permute-start(bf16[256,2048]{1,0:T(8,128)(2,1)} %collective-permute-done.34.refs_9_), channel_id=1, source_target_pairs={{1,0},{5,4},{9,8},{13,12},{17,16},{21,20},{25,24},{29,28}} | collective-permute-start | bytes 3145736 | tf_op jit(solution)/shard_map/ppermute | solution.py:308
  244.3 43.6 %collective-permute-start.48 = (bf16[512,384]{1,0:T(8,128)(2,1)}, bf16[512,384]{1,0:T(8,128)(2,1)}, u32[]{:S(2)}, u32[]{:S(2)}) collective-permute-start(bf16[512,384]{1,0:T(8,128)(2,1)} %get-tuple-element.112), channel_id=1, source_target_pairs={{2,1},{3,2},{6,5},{7,6},{10,9},{11,10},{14,13},{15,14},{18,17},{19... | collective-permute-start | bytes 1179656 | tf_op jit(solution)/shard_map/ppermute | solution.py:330
  264.2 33.8 %collective-permute-start.41 = (bf16[512,384]{1,0:T(8,128)(2,1)}, bf16[512,384]{1,0:T(8,128)(2,1)S(1)}, u32[]{:S(2)}, u32[]{:S(2)}) collective-permute-start(bf16[512,384]{1,0:T(8,128)(2,1)} %get-tuple-element.118), channel_id=1, source_target_pairs={{3,2},{7,6},{11,10},{15,14},{19,18},{23,22},{27,26},{31,30}} | collective-permute-start | bytes 1179656 | tf_op jit(solution)/shard_map/ppermute | solution.py:330
  265.5 54.1 %collective-permute-start.68 = (bf16[256,2048]{1,0:T(8,128)(2,1)S(1)}, bf16[256,2048]{1,0:T(8,128)(2,1)}, u32[]{:S(2)}, u32[]{:S(2)}) collective-permute-start(bf16[256,2048]{1,0:T(8,128)(2,1)S(1)} %get-tuple-element.56), channel_id=1, source_target_pairs={{3,2},{7,6},{11,10},{15,14},{19,18},{23,22},{27,26},{31,30}} | collective-permute-start | bytes 3145736 | tf_op jit(solution)/shard_map/ppermute | solution.py:330
  295.8 30.3 %collective-permute-start.53 = (bf16[512,384]{1,0:T(8,128)(2,1)S(1)}, bf16[512,384]{1,0:T(8,128)(2,1)S(1)}, u32[]{:S(2)}, u32[]{:S(2)}) collective-permute-start(bf16[512,384]{1,0:T(8,128)(2,1)S(1)} %get-tuple-element.110), channel_id=1, source_target_pairs={{3,2},{7,6},{11,10},{15,14},{19,18},{23,22},{27,26},{31,30}} | collective-permute-start | bytes 1179656 | tf_op jit(solution)/shard_map/ppermute | solution.py:330
  298.0 32.2 %collective-permute-start.59 = (bf16[512,384]{1,0:T(8,128)(2,1)S(1)}, bf16[512,384]{1,0:T(8,128)(2,1)S(1)}, u32[]{:S(2)}, u32[]{:S(2)}) collective-permute-start(bf16[512,384]{1,0:T(8,128)(2,1)S(1)} %get-tuple-element.106), channel_id=1, source_target_pairs={{3,2},{7,6},{11,10},{15,14},{19,18},{23,22},{27,26},{31,30}} | collective-permute-start | bytes 1179656 | tf_op jit(solution)/shard_map/ppermute | solution.py:330
  299.3 59.7 %collective-permute-start.71 = (bf16[256,2048]{1,0:T(8,128)(2,1)S(1)}, bf16[256,2048]{1,0:T(8,128)(2,1)S(1)}, u32[]{:S(2)}, u32[]{:S(2)}) collective-permute-start(bf16[256,2048]{1,0:T(8,128)(2,1)S(1)} %get-tuple-element.55), channel_id=1, source_target_pairs={{0,1},{4,5},{8,9},{12,13},{16,17},{20,21},{24,25},{28,29}} | collective-permute-start | bytes 3145736 | tf_op jit(solution)/shard_map/ppermute | solution.py:330
  324.7 27.2 %collective-permute-start.63 = (bf16[512,384]{1,0:T(8,128)(2,1)S(1)}, bf16[512,384]{1,0:T(8,128)(2,1)S(1)}, u32[]{:S(2)}, u32[]{:S(2)}) collective-permute-start(bf16[512,384]{1,0:T(8,128)(2,1)S(1)} %fusion.7), channel_id=1, source_target_pairs={{0,1},{1,2},{4,5},{5,6},{8,9},{9,10},{12,13},{13,14},{16,17},{17,1... | collective-permute-start | bytes 1179656 | tf_op jit(solution)/shard_map/ppermute | solution.py:330
  326.1 77.5 %collective-permute-start.65 = (bf16[256,2048]{1,0:T(8,128)(2,1)S(1)}, bf16[256,2048]{1,0:T(8,128)(2,1)S(1)}, u32[]{:S(2)}, u32[]{:S(2)}) collective-permute-start(bf16[256,2048]{1,0:T(8,128)(2,1)S(1)} %get-tuple-element.57), channel_id=1, source_target_pairs={{0,1},{4,5},{8,9},{12,13},{16,17},{20,21},{24,25},{28,29}} | collective-permute-start | bytes 3145736 | tf_op jit(solution)/shard_map/ppermute | solution.py:330
  329.2 32.4 %collective-permute-start.74 = (bf16[256,2048]{1,0:T(8,128)(2,1)}, bf16[256,2048]{1,0:T(8,128)(2,1)S(1)}, u32[]{:S(2)}, u32[]{:S(2)}) collective-permute-start(bf16[256,2048]{1,0:T(8,128)(2,1)} %get-tuple-element.54), channel_id=1, source_target_pairs={{0,1},{4,5},{8,9},{12,13},{16,17},{20,21},{24,25},{28,29}} | collective-permute-start | bytes 3145736 | tf_op jit(solution)/shard_map/ppermute | solution.py:330
  330.2 73.6 %collective-permute-start.69 = (bf16[256,2048]{1,0:T(8,128)(2,1)S(1)}, bf16[256,2048]{1,0:T(8,128)(2,1)S(1)}, u32[]{:S(2)}, u32[]{:S(2)}) collective-permute-start(bf16[256,2048]{1,0:T(8,128)(2,1)S(1)} %fusion.3), channel_id=1, source_target_pairs={{2,1},{6,5},{10,9},{14,13},{18,17},{22,21},{26,25},{30,29}} | collective-permute-start | bytes 3145736 | tf_op jit(solution)/shard_map/ppermute | solution.py:330
  361.6 78.3 %collective-permute-start.72 = (bf16[256,2048]{1,0:T(8,128)(2,1)S(1)}, bf16[256,2048]{1,0:T(8,128)(2,1)S(1)}, u32[]{:S(2)}, u32[]{:S(2)}) collective-permute-start(bf16[256,2048]{1,0:T(8,128)(2,1)S(1)} %fusion.5), channel_id=1, source_target_pairs={{1,2},{5,6},{9,10},{13,14},{17,18},{21,22},{25,26},{29,30}} | collective-permute-start | bytes 3145736 | tf_op jit(solution)/shard_map/ppermute | solution.py:330
  376.1 52.0 %collective-permute-start.52 = (bf16[512,384]{1,0:T(8,128)(2,1)S(1)}, bf16[512,384]{1,0:T(8,128)(2,1)S(1)}, u32[]{:S(2)}, u32[]{:S(2)}) collective-permute-start(bf16[512,384]{1,0:T(8,128)(2,1)S(1)} %copy-done.57), channel_id=1, source_target_pairs={{0,1},{1,2},{2,3},{4,5},{5,6},{6,7},{8,9},{9,10},{10,11},{12,13},{... | collective-permute-start | bytes 1179656 | tf_op jit(solution)/shard_map/ppermute | solution.py:330
  378.1 51.9 %collective-permute-start.49 = (bf16[512,384]{1,0:T(8,128)(2,1)S(1)}, bf16[512,384]{1,0:T(8,128)(2,1)S(1)}, u32[]{:S(2)}, u32[]{:S(2)}) collective-permute-start(bf16[512,384]{1,0:T(8,128)(2,1)S(1)} %fusion.18), channel_id=1, source_target_pairs={{1,0},{2,1},{3,2},{5,4},{6,5},{7,6},{9,8},{10,9},{11,10},{13,12},{... | collective-permute-start | bytes 1179656 | tf_op jit(solution)/shard_map/ppermute | solution.py:330
  403.7 30.3 %collective-permute-start.37 = (f32[2048]{0:T(1024)S(1)}, f32[2048]{0:T(1024)S(1)}, u32[]{:S(2)}, u32[]{:S(2)}) collective-permute-start(f32[2048]{0:T(1024)S(1)} %add.237), channel_id=1, source_target_pairs={{0,2},{1,3},{2,0},{3,1},{4,6},{5,7},{6,4},{7,5},{8,10},{9,11},{10,... | collective-permute-start | bytes 24584 | tf_op jit(solution)/shard_map/ppermute | solution.py:338
  403.8 32.9 %collective-permute-start.46 = (bf16[512,384]{1,0:T(8,128)(2,1)S(1)}, bf16[512,384]{1,0:T(8,128)(2,1)S(1)}, u32[]{:S(2)}, u32[]{:S(2)}) collective-permute-start(bf16[512,384]{1,0:T(8,128)(2,1)S(1)} %get-tuple-element.115), channel_id=1, source_target_pairs={{0,1},{1,2},{2,3},{4,5},{5,6},{6,7},{8,9},{9,10},{10,11},{12,13},{... | collective-permute-start | bytes 1179656 | tf_op jit(solution)/shard_map/ppermute | solution.py:330
  444.0 41.8 %collective-permute-start.67 = (bf16[256,2048]{1,0:T(8,128)(2,1)}, bf16[256,2048]{1,0:T(8,128)(2,1)}, u32[]{:S(2)}, u32[]{:S(2)}) collective-permute-start(bf16[256,2048]{1,0:T(8,128)(2,1)} %add_convert_fusion.1), channel_id=1, source_target_pairs={{2,1},{6,5},{10,9},{14,13},{18,17},{22,21},{26,25},{30,29}} | collective-permute-start | bytes 3145736 | tf_op jit(solution)/shard_map/ppermute | solution.py:330
  447.6 38.2 %collective-permute-start.76 = (bf16[256,2048]{1,0:T(8,128)(2,1)}, bf16[256,2048]{1,0:T(8,128)(2,1)}, u32[]{:S(2)}, u32[]{:S(2)}) collective-permute-start(bf16[256,2048]{1,0:T(8,128)(2,1)} %get-tuple-element.54), channel_id=1, source_target_pairs={{3,2},{7,6},{11,10},{15,14},{19,18},{23,22},{27,26},{31,30}} | collective-permute-start | bytes 3145736 | tf_op jit(solution)/shard_map/ppermute | solution.py:330
  449.7 36.1 %collective-permute-start.75 = (bf16[256,2048]{1,0:T(8,128)(2,1)}, bf16[256,2048]{1,0:T(8,128)(2,1)}, u32[]{:S(2)}, u32[]{:S(2)}) collective-permute-start(bf16[256,2048]{1,0:T(8,128)(2,1)} %add_convert_fusion), channel_id=1, source_target_pairs={{1,2},{5,6},{9,10},{13,14},{17,18},{21,22},{25,26},{29,30}} | collective-permute-start | bytes 3145736 | tf_op jit(solution)/shard_map/ppermute | solution.py:330
  451.7 34.1 %collective-permute-start.70 = (bf16[256,2048]{1,0:T(8,128)(2,1)}, bf16[256,2048]{1,0:T(8,128)(2,1)}, u32[]{:S(2)}, u32[]{:S(2)}) collective-permute-start(bf16[256,2048]{1,0:T(8,128)(2,1)} %fusion.4), channel_id=1, source_target_pairs={{1,0},{5,4},{9,8},{13,12},{17,16},{21,20},{25,24},{29,28}} | collective-permute-start | bytes 3145736 | tf_op jit(solution)/shard_map/ppermute | solution.py:330
  458.2 27.7 %collective-permute-start.73 = (bf16[256,2048]{1,0:T(8,128)(2,1)}, bf16[256,2048]{1,0:T(8,128)(2,1)}, u32[]{:S(2)}, u32[]{:S(2)}) collective-permute-start(bf16[256,2048]{1,0:T(8,128)(2,1)} %fusion.6), channel_id=1, source_target_pairs={{2,3},{6,7},{10,11},{14,15},{18,19},{22,23},{26,27},{30,31}} | collective-permute-start | bytes 3145736 | tf_op jit(solution)/shard_map/ppermute | solution.py:330
  (107 other events, 1579.9 us)
Sparse Core Ops, SparseCore 0:
  11.9 38.5 reduce-scatter.6
  53.7 36.0 reduce-scatter.4
  91.6 25.6 all-gather.2
  198.3 22.6 all-gather.4

commit v2 on v0

v2 whole, which is shorter than its diff:
```python
import functools

import jax
import jax.numpy as jnp
from jax import lax
from jax.experimental import pallas as pl
from jax.experimental.pallas import tpu as pltpu
from jax.sharding import PartitionSpec as P

HEADS = 16
KV_HEADS = 4
HEAD_DIM = 64
GROUP = HEADS // KV_HEADS
QP = 2 * GROUP * HEAD_DIM
CP = QP + 4 * HEAD_DIM

BETA_ONE = 0.9
BETA_TWO = 0.95
ADAM_EPS = 1e-08
INNER_RATE = 0.001
WEIGHT_DECAY = 0.1
STEP_COUNT = 100.0
OUTER_RATE = 0.7
OUTER_MOMENTUM = 0.9
MIXING = 0.5
NORM_EPS = 1e-05
ROPE_BASE = 500000.0
VMEM_LIMIT = 50 * 1024 * 1024

PAIRS = KV_HEADS // 2
F32 = jnp.float32
BF16 = jnp.bfloat16
NN = (((1,), (0,)), ((), ()))
NT = (((1,), (1,)), ((), ()))


def mm(a, b, dims=NN):
    return lax.dot_general(a, b, dims, preferred_element_type=F32)


def rope_tables(length):
    half = HEAD_DIM // 2
    freqs = ROPE_BASE ** (-jnp.arange(half, dtype=F32) / half)
    angles = jnp.arange(length, dtype=F32)[:, None] * freqs[None, :]
    cosine = jnp.cos(angles)
    sine = jnp.sin(angles)
    zero = jnp.zeros_like(sine)
    c = jnp.concatenate([cosine] * 4, axis=1)
    above = jnp.concatenate([zero, sine] * 2, axis=1)
    below = jnp.concatenate([-sine, zero] * 2, axis=1)
    return jnp.stack([c, above, below])


def turn(x, tab, sign):
    side = pltpu.roll(x, 32, 1) * tab[1] + pltpu.roll(x, 96, 1) * tab[2]
    return x * tab[0] + sign * side


def halves(x, at):
    lane = lax.broadcasted_iota(jnp.int32, x.shape, 1)
    alone = jnp.where((lane < HEAD_DIM) == (at == 0), x, 0.0)
    other = pltpu.roll(alone, HEAD_DIM, 1)
    pair = (alone, other) if at == 0 else (other, alone)
    return tuple(t.astype(BF16) for t in pair)


def added(total, part):
    return part if total is None else total + part


def forward_kernel(normed, w_q, w_k, w_v, cot, tab, q_ref, k_ref, v_ref, top_ref, low_ref, go_ref):
    length = normed.shape[0]
    step = length // 2
    x = normed[...]
    k_tile = turn(mm(x, w_k[...]), tab, 1.0).astype(BF16)
    v_tile = mm(x, w_v[...]).astype(BF16)
    k_ref[...] = k_tile
    v_ref[...] = v_tile
    row = lax.broadcasted_iota(jnp.int32, (step, step), 0)
    col = lax.broadcasted_iota(jnp.int32, (step, step), 1)
    causal = row >= col
    for group in range(2):
        keys = halves(k_tile.astype(F32), group)
        values = halves(v_tile.astype(F32), group)
        for pair in range(GROUP // 2):
            tile = group * (GROUP // 2) + pair
            cut = slice(tile * 128, tile * 128 + 128)
            q = turn(mm(x, w_q[:, cut]), tab, 1.0).astype(BF16).astype(F32) * HEAD_DIM**-0.5
            q = q.astype(BF16)
            q_ref[:, cut] = q
            att = [None] * 2
            for half in range(2):
                head = tile * 2 + half
                for blk in range(2):
                    r0 = blk * step
                    nk = r0 + step
                    s = mm(q[r0:nk], keys[half][:nk], NT)
                    last = jnp.where(causal, s[:, r0:], -1e30)
                    s = last if blk == 0 else jnp.concatenate([s[:, :r0], last], axis=1)
                    top = jnp.max(s, axis=1, keepdims=True)
                    e = jnp.exp(s - top)
                    p = (e * (1.0 / jnp.sum(e, axis=1, keepdims=True))).astype(BF16)
                    if blk == 0:
                        top_ref[head] = p
                    else:
                        low_ref[head] = p
                    att[blk] = added(att[blk], mm(p, values[half][:nk]))
            att = jnp.concatenate(att, axis=0).astype(BF16).astype(F32).T.astype(BF16)
            go_ref[cut, :] = mm(att, cot[...]).astype(BF16)


def backward_kernel(normed_t, w_q, w_k, w_v, cot, wo, tab, q_ref, k_ref, v_ref, top_ref, low_ref, gain_in, g_ref, gain_ref):
    length = cot.shape[0]
    step = length // 2
    dm = []
    dks = []
    dvs = []
    for group in range(2):
        keys = halves(k_ref[...].astype(F32), group)
        values = halves(v_ref[...].astype(F32), group)
        dk_t = [[None] * 2 for _ in range(2)]
        dv_t = [[None] * 2 for _ in range(2)]
        for pair in range(GROUP // 2):
            tile = group * (GROUP // 2) + pair
            cut = slice(tile * 128, tile * 128 + 128)
            da_f = mm(cot[...], wo[cut, :], NT)
            da = da_f.astype(BF16)
            da_t = da.astype(F32).T.astype(BF16)
            q_t = q_ref[:, cut].astype(F32).T.astype(BF16)
            dq = [None] * 2
            for half in range(2):
                head = tile * 2 + half
                key = keys[half]
                value = values[half]
                for blk in range(2):
                    r0 = blk * step
                    nk = r0 + step
                    pb = top_ref[head] if blk == 0 else low_ref[head]
                    p = pb.astype(F32)
                    dp = mm(da[r0:nk], value[:nk], NT)
                    ds = (p * (dp - jnp.sum(p * dp, axis=1, keepdims=True))).astype(BF16)
                    dq[blk] = added(dq[blk], mm(ds, key[:nk]))
                    dv = mm(da_t[:, r0:nk], pb)
                    dk = mm(q_t[:, r0:nk], ds)
                    for kb in range(blk + 1):
                        part = slice(kb * step, kb * step + step)
                        dv_t[half][kb] = added(dv_t[half][kb], dv[:, part])
                        dk_t[half][kb] = added(dk_t[half][kb], dk[:, part])
            dq = jnp.concatenate(dq, axis=0) * HEAD_DIM**-0.5
            dm.append(turn(dq, tab, -1.0).astype(BF16))
        dks.append([dk_t[0][kb][:HEAD_DIM] + dk_t[1][kb][HEAD_DIM:] for kb in range(2)])
        dvs.append([dv_t[0][kb][:HEAD_DIM] + dv_t[1][kb][HEAD_DIM:] for kb in range(2)])

    def joined(parts):
        return jnp.concatenate(
            [jnp.concatenate([parts[0][kb], parts[1][kb]], axis=0).T for kb in range(2)], axis=0
        )

    dm.append(turn(joined(dks), tab, -1.0).astype(BF16))
    dm.append(joined(dvs).astype(BF16))
    dm = jnp.concatenate(dm, axis=1)
    ones = jnp.ones((8, CP), BF16)
    block = 512
    for at in range(g_ref.shape[0] // block):
        cut = slice(at * block, at * block + block)
        g = mm(normed_t[cut, :], dm)
        g_ref[cut, :] = g.astype(BF16)
        w = jnp.concatenate([w_q[cut, :], w_k[cut, :], w_v[cut, :]], axis=1)
        prod = g * w.astype(F32)
        high = prod.astype(BF16)
        low = (prod - high.astype(F32)).astype(BF16)
        gain_ref[:, cut] = gain_in[:, cut] + mm(ones, high, NT) + mm(ones, low, NT)


def w_specs(width, pair=None):
    first_k = HEADS * HEAD_DIM // 128
    first_v = first_k + KV_HEADS * HEAD_DIM // 128

    def at(i):
        return i if pair is None else pair

    return [
        pl.BlockSpec((width, QP), lambda i: (0, at(i))),
        pl.BlockSpec((width, 128), lambda i: (0, first_k + at(i))),
        pl.BlockSpec((width, 128), lambda i: (0, first_v + at(i))),
    ]


def full_spec(x):
    return pl.BlockSpec(x.shape, lambda i: (0,) * len(x.shape))


def forward(normed, w, cot, tab):
    length, width = normed.shape
    step = length // 2
    outs = (
        jax.ShapeDtypeStruct((length, PAIRS * QP), BF16),
        jax.ShapeDtypeStruct((length, PAIRS * 128), BF16),
        jax.ShapeDtypeStruct((length, PAIRS * 128), BF16),
        jax.ShapeDtypeStruct((HEADS, step, step), BF16),
        jax.ShapeDtypeStruct((HEADS, step, length), BF16),
        jax.ShapeDtypeStruct((HEADS * HEAD_DIM, width), BF16),
    )
    return pl.pallas_call(
        forward_kernel,
        out_shape=outs,
        grid=(PAIRS,),
        in_specs=[full_spec(normed)] + w_specs(width) + [full_spec(cot), full_spec(tab)],
        out_specs=saved_specs(length) + (pl.BlockSpec((QP, width), lambda i: (i, 0)),),
        compiler_params=pltpu.CompilerParams(vmem_limit_bytes=VMEM_LIMIT),
        cost_estimate=pl.CostEstimate(flops=32_000_000_000, bytes_accessed=30_000_000, transcendentals=0),
    )(normed, w, w, w, cot, tab)


def saved_specs(length, pair=None):
    step = length // 2

    def at(i):
        return i if pair is None else pair

    return (
        pl.BlockSpec((length, QP), lambda i: (0, at(i))),
        pl.BlockSpec((length, 128), lambda i: (0, at(i))),
        pl.BlockSpec((length, 128), lambda i: (0, at(i))),
        pl.BlockSpec((2 * GROUP, step, step), lambda i: (at(i), 0, 0)),
        pl.BlockSpec((2 * GROUP, step, length), lambda i: (at(i), 0, 0)),
    )


def backward(pair, normed_t, w, cot, wo, tab, saved, gain_in):
    width = w.shape[0]
    outs = (
        jax.ShapeDtypeStruct((width, CP), BF16),
        jax.ShapeDtypeStruct((8, width), F32),
    )
    return pl.pallas_call(
        backward_kernel,
        out_shape=outs,
        grid=(1,),
        in_specs=[full_spec(normed_t)]
        + w_specs(width, pair)
        + [full_spec(cot), pl.BlockSpec((QP, width), lambda i: (pair, 0)), full_spec(tab)]
        + list(saved_specs(cot.shape[0], pair))
        + [full_spec(gain_in)],
        out_specs=tuple(full_spec(x) for x in outs),
        compiler_params=pltpu.CompilerParams(vmem_limit_bytes=VMEM_LIMIT),
        cost_estimate=pl.CostEstimate(flops=20_000_000_000, bytes_accessed=18_000_000, transcendentals=0),
    )(normed_t, w, w, w, cot, wo, tab, *saved, gain_in)


def adam(wide, grad, first, second, decay):
    first_next = BETA_ONE * first + (1.0 - BETA_ONE) * grad
    second_next = BETA_TWO * second + (1.0 - BETA_TWO) * grad * grad
    update = (
        first_next
        / (1.0 - BETA_ONE**STEP_COUNT)
        / (jnp.sqrt(second_next / (1.0 - BETA_TWO**STEP_COUNT)) + ADAM_EPS)
    )
    return (wide - INNER_RATE * (update + decay * wide), first_next, second_next)


def mixed_step(w, grad, first, second, outer):
    stepped, first_next, second_next = adam(w.astype(F32), grad, first, second, WEIGHT_DECAY)
    new = (MIXING * stepped + (1.0 - MIXING) * outer.astype(F32)).astype(BF16)
    return new, first_next, second_next


def adam_kernel(held, *refs):
    grad, w, first, second, outer = refs[:5]
    new, first_next, second_next = refs[5 + held :]
    new[...], first_next[...], second_next[...] = mixed_step(
        w[...], grad[...].astype(F32), first[...], second[...], outer[...]
    )


def qkv_adam(pair, grad, w, first, second, outer, held):
    rows, width = w.shape
    q_blocks = QP // 128
    first_k = HEADS * HEAD_DIM // 128
    first_v = first_k + KV_HEADS * HEAD_DIM // 128

    def column(j):
        return (0, jnp.where(j < q_blocks, pair * q_blocks + j, jnp.where(j == q_blocks, first_k, first_v) + pair))

    part = pl.BlockSpec((rows, 128), lambda j: (0, j))
    full = pl.BlockSpec((rows, 128), column)
    return pl.pallas_call(
        functools.partial(adam_kernel, len(held)),
        out_shape=(
            jax.ShapeDtypeStruct((rows, width), BF16),
            jax.ShapeDtypeStruct((rows, width), F32),
            jax.ShapeDtypeStruct((rows, width), F32),
        ),
        grid=(CP // 128,),
        in_specs=[part] + [full] * 4 + [pl.BlockSpec(memory_space=pl.ANY)] * len(held),
        out_specs=(full, full, full),
        input_output_aliases={5 + i: i for i in range(len(held))},
        compiler_params=pltpu.CompilerParams(vmem_limit_bytes=VMEM_LIMIT),
        cost_estimate=pl.CostEstimate(flops=20_000_000, bytes_accessed=10_000_000, transcendentals=0),
    )(grad, w, first, second, outer, *held)


def out_adam(grad, w, first, second, outer):
    rows, width = w.shape
    block = 64
    full = pl.BlockSpec((block, width), lambda i: (i, 0))
    return pl.pallas_call(
        functools.partial(adam_kernel, 0),
        out_shape=(
            jax.ShapeDtypeStruct((rows, width), BF16),
            jax.ShapeDtypeStruct((rows, width), F32),
            jax.ShapeDtypeStruct((rows, width), F32),
        ),
        grid=(rows // block,),
        in_specs=[full] * 5,
        out_specs=(full, full, full),
        compiler_params=pltpu.CompilerParams(vmem_limit_bytes=VMEM_LIMIT),
        cost_estimate=pl.CostEstimate(flops=20_000_000, bytes_accessed=14_000_000, transcendentals=0),
    )(grad, w, first, second, outer)


def nesterov(global_value, momentum, average):
    delta = global_value - average
    momentum_next = OUTER_MOMENTUM * momentum + delta
    return (global_value - OUTER_RATE * (delta + OUTER_MOMENTUM * momentum_next), momentum_next)


def after(x, *others):
    return lax.optimization_barrier((x, *others))[0]


def all_sum(x, axis, n):
    k = 1
    while k < n:
        x = x + lax.ppermute(x, axis, [(i, i ^ k) for i in range(n)])
        k *= 2
    return x


def shards(
    tokens,
    cotangent,
    norm_gain,
    qkv_weight,
    out_weight,
    gain_first,
    gain_second,
    qkv_first,
    qkv_second,
    out_first,
    out_second,
    gain_global,
    gain_momentum,
    qkv_global,
    qkv_momentum,
    out_global,
    out_momentum,
):
    n = lax.axis_size("fsdp")
    islands = lax.axis_size("island")
    gain = norm_gain[0]
    w_qkv = qkv_weight[0]
    w_out = out_weight[0]
    length, width = tokens.shape

    all_qkv = lax.all_gather(w_qkv, "fsdp", axis=0, tiled=True)

    wide = tokens.astype(F32)
    factor = lax.rsqrt(jnp.mean(wide * wide, axis=-1, keepdims=True) + NORM_EPS)
    normed = (wide * factor * gain).astype(BF16)
    normed_t = normed.T
    tab = rope_tables(length)
    all_out = lax.all_gather(after(w_out, all_qkv, normed, normed_t, tab), "fsdp", axis=0, tiled=True)

    *saved, g_out = forward(normed, all_qkv, cotangent, tab)
    out_grad = lax.psum_scatter(g_out, "fsdp", scatter_dimension=0, tiled=True)

    gain_sum = jnp.zeros((8, width), F32)
    qkv_grad = []
    for pair in range(PAIRS):
        grad, gain_sum = backward(
            pair, normed_t, all_qkv, cotangent, all_out, tab, saved, gain_sum
        )
        qkv_grad.append(lax.psum_scatter(grad, "fsdp", scatter_dimension=0, tiled=True))

    gain_grad = all_sum(gain_sum[0], "fsdp", n) / gain
    gain_step, gain_first_next, gain_second_next = adam(gain, gain_grad, gain_first[0], gain_second[0], 0.0)

    scale = 1.0 / islands
    qkv_total = lax.psum_scatter(w_qkv, "island", scatter_dimension=1, tiled=True).astype(F32)
    out_total = lax.psum_scatter(w_out, "island", scatter_dimension=1, tiled=True).astype(F32)
    gain_total = all_sum(gain, "island", islands)
    gain_pair = nesterov(gain_global, gain_momentum, gain_total * scale)
    qkv_pair = nesterov(qkv_global, qkv_momentum, qkv_total * scale)
    out_pair = nesterov(out_global, out_momentum, out_total * scale)
    qkv_whole = lax.all_gather(qkv_pair[0].astype(BF16), "island", axis=1, tiled=True)
    out_whole = lax.all_gather(out_pair[0].astype(BF16), "island", axis=1, tiled=True)

    out_state = out_adam(out_grad, w_out, out_first[0], out_second[0], out_whole)
    qkv_state = ()
    for pair in range(PAIRS):
        qkv_state = qkv_adam(
            pair, qkv_grad[pair], w_qkv, qkv_first[0], qkv_second[0], qkv_whole, qkv_state
        )
    gain_next = MIXING * gain_step + (1.0 - MIXING) * gain_pair[0]
    return (
        gain_next[None],
        qkv_state[0][None],
        out_state[0][None],
        gain_first_next[None],
        gain_second_next[None],
        qkv_state[1][None],
        qkv_state[2][None],
        out_state[1][None],
        out_state[2][None],
        gain_pair[0],
        gain_pair[1],
        qkv_pair[0],
        qkv_pair[1],
        out_pair[0],
        out_pair[1],
    )


def solution(mesh):
    placed = (
        P(("island", "fsdp"), None),
        P(("island", "fsdp"), None),
        P("island", None),
        P("island", "fsdp", None),
        P("island", "fsdp", None),
        P("island", None),
        P("island", None),
        P("island", "fsdp", None),
        P("island", "fsdp", None),
        P("island", "fsdp", None),
        P("island", "fsdp", None),
        P(),
        P(),
        P("fsdp", "island"),
        P("fsdp", "island"),
        P("fsdp", "island"),
        P("fsdp", "island"),
    )
    return jax.shard_map(
        shards,
        mesh=mesh,
        in_specs=placed,
        out_specs=(
            P("island", None),
            P("island", "fsdp", None),
            P("island", "fsdp", None),
            P("island", None),
            P("island", None),
            P("island", "fsdp", None),
            P("island", "fsdp", None),
            P("island", "fsdp", None),
            P("island", "fsdp", None),
            P(),
            P(),
            P("fsdp", "island"),
            P("fsdp", "island"),
            P("fsdp", "island"),
            P("fsdp", "island"),
        ),
        check_vma=False,
    )
```

time: 481 us -> 487 us (1.012); the launches traced: 480 us -> 480 us
  Pallas kernels: 0 us -> 86.7 us
  matrix products: 69 us -> 0 us
  other arithmetic: 50.3 us -> 11.1 us
  waiting for transfers between devices: 299 us -> 337 us
  blocking collectives: 21.5 us -> 0 us
    pallas_call x0 -> x6, Pallas kernels: none -> 86.7 us  [the longest x2 36.7 us: backward(): pl.pallas_call(backward_kernel, out_shape=outs, grid=(1,), in_specs=[full...]
    dot_general x11 -> x0, matrix products: 69 us -> none  [the longest x3 24.3 us: attend_part(): jnp.einsum('kgqs,skd->qkgd', weights, values, preferred_element_type=jnp....]
    reduce_scatter x3 -> x4, waiting for transfers between devices: 150 us -> 190 us  [the longest x2 109 us: shards(): lax.psum_scatter(grad, 'fsdp', scatter_dimension=0, tiled=True)]
    unnamed x9 -> x10, waiting for transfers between devices: 39.9 us -> 1.33 us
    all_gather x4, waiting for transfers between devices: 109 us -> 143 us  [the longest x1 104 us: shards(): all_qkv = lax.all_gather(w_qkv, 'fsdp', axis=0, tiled=True)]
    psum x2 -> x0, blocking collectives: 21.5 us -> none  [the longest x1 11.2 us: outer_sync(): gain_total = lax.psum(gain, 'island')]
    broadcast_in_dim x2 -> x0, other arithmetic: 15.7 us -> none  [the longest x1 8.51 us: shards(): qkv_state[2][None]]
    mul x3 -> x2, other arithmetic: 11.9 us -> 0.02 us  [the longest x1 0.01 us: adam(): first_next = BETA_ONE * first + (1.0 - BETA_ONE) * grad]
  transfers between devices with their start and end apart: 8 -> 14, of which waited for: 6 -> 8; matrix products, arithmetic and copies ran while one was open for 27% -> 6% of each run, Pallas kernels for 0% -> 17%
where the time goes in v2:
time: 487 us; the launch traced here: 480 us
  waiting for transfers between devices  337 us (69%)
  Pallas kernels  86.7 us (18%)
  local copies, waits for them, and re-layouts  24 us (5%)
  between operations  16.2 us (3%)
  other arithmetic  11.1 us (2%)
    reduce_scatter x2, waiting for transfers between devices, shards(): lax.psum_scatter(grad, 'fsdp', scatter_dimension=0, tiled=True)  109 us
    all_gather x1, waiting for transfers between devices, shards(): all_qkv = lax.all_gather(w_qkv, 'fsdp', axis=0, tiled=True)  104 us
    reduce_scatter x1, waiting for transfers between devices, shards(): out_grad = lax.psum_scatter(g_out, 'fsdp', scatter_dimension=0, tiled=True)  80.4 us
    pallas_call x2, Pallas kernels, backward(): pl.pallas_call(backward_kernel, out_shape=outs, grid=(1,), in_specs=[full...  36.7 us
    all_gather x1, waiting for transfers between devices, shards(): lax.all_gather(after(w_out, all_qkv, normed, normed_t, tab), 'fsdp', axis...  34.6 us
    pallas_call x1, Pallas kernels, forward(): pl.pallas_call(forward_kernel, out_shape=outs, grid=(PAIRS,), in_specs=[f...  32.3 us
    unnamed x35, local copies, waits for them, and re-layouts  18.1 us
    pallas_call x2, Pallas kernels, qkv_adam(): pl.pallas_call(functools.partial(adam_kernel, len(held)), out_shape=(jax....  11.8 us
  transfers between devices with their start and end apart: 14, of which 8 were waited for; matrix products, arithmetic and copies ran while one was open for 6% of the time, Pallas kernels for 17%

profile of v2, /device:TPU:22, one launch (start us, length us, event | category | flops | bytes accessed | tf_op | source)
XLA Modules:
  0.0 479.8 jit_solution(13365608043984077980)
XLA Ops:
  8.1 0.7 all-gather.12.cloned.1.call-update
  8.8 2.6 copy.52
  11.5 0.5 reduce-scatter.14.cloned.1.call-update
  12.1 2.9 copy.42
  15.0 1.0 fusion.4
  15.9 0.3 maximum_bitcast_fusion
  16.2 0.5 maximum_bitcast_fusion.1
  16.8 0.5 fusion
  17.3 1.9 fusion.10.normed_t
  19.2 1.9 fusion.2
  21.0 104.0 %all-gather.12.cloned.1.call-done = bf16[1,2048,1536]{2,1,0:T(8,128)(2,1)} async-done(((bf16[1,512,1536]{2,1,0:T(8,128)(2,1)}), bf16[1,2048,1536]{2,1,0:T(8,128)(2,1)}) %all-gather.12.cloned.1.call-update) | async-done | bytes 6291472 | tf_op jit(solution)/shard_map/all_gather | solution.py:366
  125.1 1.0 copy.46
  126.1 2.0 copy.45
  128.1 1.8 copy.53
  129.9 2.3 fusion.8
  132.2 1.8 copy.47
  134.0 2.4 copy.43.normed
  136.4 2.1 fusion.7
  138.5 0.2 reduce-scatter.12.cloned.1.call-start
  138.7 32.3 %shard_map.280 = (bf16[512,1024]{1,0:T(8,128)(2,1)S(1)}, bf16[512,256]{1,0:T(8,128)(2,1)S(1)}, bf16[512,256]{1,0:T(8,128)(2,1)S(1)}, bf16[16,256,256]{2,1,0:T(8,...) custom-call(bf16[512,2048]{1,0:T(8,128)(2,1)} %copy.43.normed, bf16[2048,1536]{1,0:T(8,128)(2,1)} %bitcast.59, ...), custom_call_target="tpu_custom_call" | custom-call | flops 32000000000 | bytes 30000000 | tf_op jit(solution)/shard_map/pallas_call | solution.py:204
  171.1 0.3 reduce-scatter.10.cloned.1.call-start
  171.3 34.6 %all-gather.6.cloned.1.call-done.wo = bf16[1024,2048]{1,0:T(8,128)(2,1)} async-done(((bf16[256,2048]{1,0:T(8,128)(2,1)}), bf16[1024,2048]{1,0:T(8,128)(2,1)}) %all-gather.6.cloned.1.call-update) | async-done | bytes 4194320 | tf_op jit(solution)/shard_map/all_gather | solution.py:373
  205.9 18.2 %shard_map.281 = (bf16[2048,768]{1,0:T(8,128)(2,1)}, f32[8,2048]{1,0:T(8,128)S(1)}) custom-call(bf16[2048,512]{1,0:T(8,128)(2,1)} %fusion.10.normed_t, bf16[2048,1536]{1,0:T(8,128)(2,1)} %bitcast.62, bf16[2048,1536]{1,0:T(8,128)(2,1)} %bitcast.63, bf16[2048,1536]{1,0:T(8,128)(2,1)} %bitcast.64, bf16[512,2048]{1,0:T(8,128)(2,1)} %cot.5, ...), custom_call_target="tpu_custom_call" | custom-call | flops 20000000000 | bytes 18000000 | tf_op jit(solution)/shard_map/pallas_call | solution.py:236
  224.2 0.3 reduce-scatter.8.cloned.1.call-start
  224.5 18.5 %shard_map.282 = (bf16[2048,768]{1,0:T(8,128)(2,1)}, f32[8,2048]{1,0:T(8,128)S(1)}) custom-call(bf16[2048,512]{1,0:T(8,128)(2,1)} %fusion.10.normed_t, bf16[2048,1536]{1,0:T(8,128)(2,1)} %bitcast.65, bf16[2048,1536]{1,0:T(8,128)(2,1)} %bitcast.66, bf16[2048,1536]{1,0:T(8,128)(2,1)} %bitcast.67, bf16[512,2048]{1,0:T(8,128)(2,1)} %cot.5, ...), custom_call_target="tpu_custom_call" | custom-call | flops 20000000000 | bytes 18000000 | tf_op jit(solution)/shard_map/pallas_call | solution.py:236
  243.0 0.1 collective-permute-start.2
  243.1 1.2 collective-permute-done.2
  244.3 0.6 collective-permute-start.3
  244.8 0.4 collective-permute-start
  245.3 2.6 collective-permute-done.3
  247.9 0.6 collective-permute-start.4
  248.5 1.9 collective-permute-start.1
  250.4 0.9 copy.50
  251.3 0.9 copy.51
  252.2 1.8 copy.49.refs_4_
  254.1 0.6 add_multiply_fusion
  254.7 3.9 all-gather.10.cloned.1.call-done.refs_4_
  258.6 80.4 %reduce-scatter.12.cloned.1.call-done.refs_0_ = bf16[256,2048]{1,0:T(8,128)(2,1)} async-done(((bf16[1024,2048]{1,0:T(8,128)(2,1)}), bf16[256,2048]{1,0:T(8,128)(2,1)}) %reduce-scatter.12.cloned.1.call-update) | async-done | bytes 1048592 | tf_op jit(solution)/shard_map/reduce_scatter | solution.py:376
  339.0 1.2 copy-done.1
  340.2 1.2 copy-done.2
  341.4 1.2 copy-done.3
  342.7 5.9 %shard_map.285 = (bf16[256,2048]{1,0:T(8,128)(2,1)}, f32[256,2048]{1,0:T(8,128)}, f32[256,2048]{1,0:T(8,128)}) custom-call(bf16[256,2048]{1,0:T(8,128)(2,1)S(1)} %copy-done.3, bf16[256,2048]{1,0:T(8,128)(2,1)S(1)} %bitcast.35, f32[256,2048]{1,0:T(8,128)} %bitcast.43, f32[256,2048]{1,0:T(8,128)} %bitcast.44, bf16[256,2048]{1,0:T(8,128)(2,1)S(1)} %copy-done.2), custom_call_target="tpu_custom_call" | custom-call | flops 20000000 | bytes 14000000 | tf_op jit(solution)/shard_map/pallas_call | solution.py:307
  348.6 53.5 %reduce-scatter.10.cloned.1.call-done.refs_0_ = bf16[512,768]{1,0:T(8,128)(2,1)} async-done(((bf16[2048,768]{1,0:T(8,128)(2,1)}), bf16[512,768]{1,0:T(8,128)(2,1)}) %reduce-scatter.10.cloned.1.call-update) | async-done | bytes 786448 | tf_op jit(solution)/shard_map/reduce_scatter | solution.py:384
  402.1 1.1 copy-done.5
  403.3 5.9 %shard_map.283 = (bf16[512,1536]{1,0:T(8,128)(2,1)}, f32[512,1536]{1,0:T(8,128)}, f32[512,1536]{1,0:T(8,128)}) custom-call(bf16[512,768]{1,0:T(8,128)(2,1)S(1)} %copy-done.5, bf16[512,1536]{1,0:T(8,128)(2,1)S(1)} %bitcast.31, f32[512,1536]{1,0:T(8,128)} %bitcast.36, f32[512,1536]{1,0:T(8,128)} %bitcast.38, bf16[512,1536]{1,0:T(8,128)(2,1)S(1)} %copy.49.refs_4_), custom_call_target="tpu_custom_call" | custom-call | flops 20000000 | bytes 10000000 | tf_op jit(solution)/shard_map/pallas_call | solution.py:287
  409.2 55.7 %reduce-scatter.8.cloned.1.call-done.refs_0_ = bf16[512,768]{1,0:T(8,128)(2,1)} async-done(((bf16[2048,768]{1,0:T(8,128)(2,1)}), bf16[512,768]{1,0:T(8,128)(2,1)}) %reduce-scatter.8.cloned.1.call-update) | async-done | bytes 786448 | tf_op jit(solution)/shard_map/reduce_scatter | solution.py:384
  464.8 1.1 copy-done.4
  466.0 5.9 %shard_map.284 = (bf16[512,1536]{1,0:T(8,128)(2,1)}, f32[512,1536]{1,0:T(8,128)}, f32[512,1536]{1,0:T(8,128)}) custom-call(bf16[512,768]{1,0:T(8,128)(2,1)S(1)} %copy-done.4, bf16[512,1536]{1,0:T(8,128)(2,1)S(1)} %bitcast.32, f32[512,1536]{1,0:T(8,128)} %bitcast.37, ...), custom_call_target="tpu_custom_call", output_to_operand_aliasing={{0}: (5, {}), {1}: (6, {}), {2}: (7, {})} | custom-call | flops 20000000 | bytes 10000000 | tf_op jit(solution)/shard_map/pallas_call | solution.py:287
  (53 shorter events, 0.6 us)
Async XLA Ops:
  8.0 117.0 %all-gather.12.cloned.1.call-start = ((), (), s32[]{:S(2)}) async-start(), calls=%async_computation.12 | async-start | bytes 7864320 | tf_op jit(solution)/shard_map/all_gather | solution.py:366
  8.7 119.4 %reduce-scatter.16.cloned.1.call-start = ((), (), s32[]{:S(2)}) async-start(), calls=%async_computation.13 | async-start | bytes 1769472
  11.4 125.0 %reduce-scatter.14.cloned.1.call-start = ((), (), s32[]{:S(2)}) async-start(), calls=%async_computation.10 | async-start | bytes 1179648 | tf_op jit(solution)/shard_map/reduce_scatter | solution.py:391
  12.0 193.9 %all-gather.6.cloned.1.call-start = ((), (), s32[]{:S(2)}) async-start(), calls=%async_computation.5 | async-start | bytes 5242880 | tf_op jit(solution)/shard_map/all_gather | solution.py:373
  14.9 2.4 copy-start.9
  19.2 105.9 %copy-start.8 = (f32[512,192]{0,1:T(8,128)S(1)}, f32[512,192]{0,1:T(8,128)}, u32[]{:S(2)}) copy-start(f32[512,192]{0,1:T(8,128)} %param.30) | copy-start | bytes 1179652
  125.0 9.0 %copy-start.6 = (bf16[512,2048]{0,1:T(8,128)(2,1)S(1)}, bf16[512,2048]{0,1:T(8,128)(2,1)}, u32[]{:S(2)}) copy-start(bf16[512,2048]{0,1:T(8,128)(2,1)} %fusion.2) | copy-start | bytes 6291460
  125.1 127.2 %all-gather.8.cloned.1.call-start = ((), (), s32[]{:S(2)}) async-start(), calls=%async_computation.7 | async-start | bytes 1769472 | tf_op jit(solution)/shard_map/all_gather | solution.py:396
  134.0 124.7 %all-gather.10.cloned.1.call-start = ((), (), s32[]{:S(2)}) async-start(), calls=%async_computation.11 | async-start | bytes 1179648 | tf_op jit(solution)/shard_map/all_gather | solution.py:397
  138.5 200.5 %reduce-scatter.12.cloned.1.call-start = ((), (), s32[]{:S(2)}) async-start(), calls=%async_computation.9 | async-start | bytes 5242880 | tf_op jit(solution)/shard_map/reduce_scatter | solution.py:376
  171.1 231.1 %reduce-scatter.10.cloned.1.call-start = ((), (), s32[]{:S(2)}) async-start(), calls=%async_computation.8 | async-start | bytes 3932160 | tf_op jit(solution)/shard_map/reduce_scatter | solution.py:384
  224.2 240.7 %reduce-scatter.8.cloned.1.call-start = ((), (), s32[]{:S(2)}) async-start(), calls=%async_computation.6 | async-start | bytes 3932160 | tf_op jit(solution)/shard_map/reduce_scatter | solution.py:384
  243.0 2.3 copy-start.12
  243.0 7.4 %copy-start.13 = (f32[1,2048]{1,0:T(1,128)S(1)}, f32[1,2048]{1,0:T(1,128)}, u32[]{:S(2)}) copy-start(f32[1,2048]{1,0:T(1,128)} %param.23) | copy-start | bytes 24580
  243.0 7.4 %copy-start.7 = (f32[512,192]{1,0:T(8,128)S(1)}, f32[512,192]{1,0:T(8,128)}, u32[]{:S(2)}) copy-start(f32[512,192]{1,0:T(8,128)} %get-tuple-element.89) | copy-start | bytes 1179652
  243.0 11.1 %copy-start.10 = (f32[2048]{0:T(1024)S(1)}, f32[2048]{0:T(1024)}, u32[]{:S(2)}) copy-start(f32[2048]{0:T(1024)} %param.28) | copy-start | bytes 24580
  243.0 11.1 %copy-start.11 = (f32[2048]{0:T(1024)S(1)}, f32[2048]{0:T(1024)}, u32[]{:S(2)}) copy-start(f32[2048]{0:T(1024)} %param.29) | copy-start | bytes 24580
  243.0 1.2 collective-permute-start.2
  244.3 3.7 collective-permute-start.3
  244.8 3.7 collective-permute-start
  247.9 6.1 %collective-permute-start.4 = (f32[2048]{0:T(1024)S(1)}, f32[2048]{0:T(1024)S(1)}, u32[]{:S(2)}, u32[]{:S(2)}) collective-permute-start(f32[2048]{0:T(1024)S(1)} %add.83), channel_id=1, source_target_pairs={{0,16},{4,20},{8,24},{12,28},{16,0},{20,4},{24,8},{28,12},{1,17},{... | collective-permute-start | bytes 24584 | tf_op jit(solution)/shard_map/ppermute | solution.py:335
  248.5 5.6 %collective-permute-start.1 = (f32[2048]{0:T(1024)S(1)}, f32[2048]{0:T(1024)S(1)}, u32[]{:S(2)}, u32[]{:S(2)}) collective-permute-start(f32[2048]{0:T(1024)S(1)} %add.75), channel_id=1, source_target_pairs={{0,2},{1,3},{2,0},{3,1},{4,6},{5,7},{6,4},{7,5},{8,10},{9,11},{10,... | collective-permute-start | bytes 24584 | tf_op jit(solution)/shard_map/ppermute | solution.py:335
  339.0 1.2 copy-start.1
  340.2 1.2 copy-start.2
  341.4 1.2 copy-start.3
  342.7 59.5 %copy-start = (bf16[1,512,1536]{2,1,0:T(8,128)(2,1)S(1)}, bf16[1,512,1536]{2,1,0:T(8,128)(2,1)}, u32[]{:S(2)}) copy-start(bf16[1,512,1536]{2,1,0:T(8,128)(2,1)} %param.20) | copy-start | bytes 4718596
  402.1 1.1 copy-start.5
  464.8 1.1 copy-start.4
Sparse Core Ops, SparseCore 0:
  10.4 114.5 all-gather.11
  126.6 79.2 all-gather.5
  208.4 24.7 all-gather.7
  234.9 23.6 all-gather.9
  260.8 78.1 reduce-scatter.11
  341.8 60.2 reduce-scatter.9
  404.5 60.2 reduce-scatter.7
Sparse Core Ops, SparseCore 1:
  13.1 38.4 reduce-scatter.15
  54.6 35.9 reduce-scatter.13

commit v3 on v2

--- a/solution.py
+++ b/solution.py
@@ -68,12 +68,28 @@
     return part if total is None else total + part
 
 
-def forward_kernel(normed, w_q, w_k, w_v, cot, tab, q_ref, k_ref, v_ref, top_ref, low_ref, go_ref):
+def forward_kernel(n_cand, starts, normed, cot, tab, *refs):
+    cands = refs[:n_cand]
+    q_ref, k_ref, v_ref, top_ref, low_ref, go_ref, w_ref, sems = refs[n_cand:]
+
+    def copy_of(at):
+        rows = cands[at].shape[0]
+        to = pl.ds(pl.multiple_of(starts[at], rows), rows)
+        return pltpu.make_async_copy(cands[at], w_ref.at[to], sems.at[at])
+
+    for at in range(n_cand):
+        @pl.when(starts[at] >= 0)
+        def _(at=at):
+            copy_of(at).start()
+    for at in range(n_cand):
+        @pl.when(starts[at] >= 0)
+        def _(at=at):
+            copy_of(at).wait()
     length = normed.shape[0]
     step = length // 2
     x = normed[...]
-    k_tile = turn(mm(x, w_k[...]), tab, 1.0).astype(BF16)
-    v_tile = mm(x, w_v[...]).astype(BF16)
+    k_tile = turn(mm(x, w_ref[:, QP : QP + 128]), tab, 1.0).astype(BF16)
+    v_tile = mm(x, w_ref[:, QP + 128 :]).astype(BF16)
     k_ref[...] = k_tile
     v_ref[...] = v_tile
     row = lax.broadcasted_iota(jnp.int32, (step, step), 0)
@@ -85,7 +101,7 @@
         for pair in range(GROUP // 2):
             tile = group * (GROUP // 2) + pair
             cut = slice(tile * 128, tile * 128 + 128)
-            q = turn(mm(x, w_q[:, cut]), tab, 1.0).astype(BF16).astype(F32) * HEAD_DIM**-0.5
+            q = turn(mm(x, w_ref[:, cut]), tab, 1.0).astype(BF16).astype(F32) * HEAD_DIM**-0.5
             q = q.astype(BF16)
             q_ref[:, cut] = q
             att = [None] * 2
@@ -109,7 +125,7 @@
             go_ref[cut, :] = mm(att, cot[...]).astype(BF16)
 
 
-def backward_kernel(normed_t, w_q, w_k, w_v, cot, wo, tab, q_ref, k_ref, v_ref, top_ref, low_ref, gain_in, g_ref, gain_ref):
+def backward_kernel(normed_t, w_ref, cot, wo, tab, q_ref, k_ref, v_ref, top_ref, low_ref, gain_in, g_ref, gain_ref):
     length = cot.shape[0]
     step = length // 2
     dm = []
@@ -165,87 +181,86 @@
         cut = slice(at * block, at * block + block)
         g = mm(normed_t[cut, :], dm)
         g_ref[cut, :] = g.astype(BF16)
-        w = jnp.concatenate([w_q[cut, :], w_k[cut, :], w_v[cut, :]], axis=1)
-        prod = g * w.astype(F32)
+        prod = g * w_ref[cut, :].astype(F32)
         high = prod.astype(BF16)
         low = (prod - high.astype(F32)).astype(BF16)
         gain_ref[:, cut] = gain_in[:, cut] + mm(ones, high, NT) + mm(ones, low, NT)
 
 
-def w_specs(width, pair=None):
-    first_k = HEADS * HEAD_DIM // 128
-    first_v = first_k + KV_HEADS * HEAD_DIM // 128
-
-    def at(i):
-        return i if pair is None else pair
-
-    return [
-        pl.BlockSpec((width, QP), lambda i: (0, at(i))),
-        pl.BlockSpec((width, 128), lambda i: (0, first_k + at(i))),
-        pl.BlockSpec((width, 128), lambda i: (0, first_v + at(i))),
-    ]
-
-
-def full_spec(x):
-    return pl.BlockSpec(x.shape, lambda i: (0,) * len(x.shape))
-
-
-def forward(normed, w, cot, tab):
+def vmem_call(kernel, outs, n_hbm=0, hbm_at=0, smem=0, scratch=(), other=None):
+    whole = pl.BlockSpec(memory_space=pltpu.VMEM)
+
+    def call(*args):
+        specs = [whole] * len(args)
+        for i in range(smem):
+            specs[i] = pl.BlockSpec(memory_space=pltpu.SMEM)
+        for i in range(hbm_at, hbm_at + n_hbm):
+            specs[i] = pl.BlockSpec(memory_space=pl.ANY)
+        for i, spec in (other or {}).items():
+            specs[i] = spec
+        return pl.pallas_call(
+            kernel,
+            out_shape=outs,
+            grid=(1,),
+            in_specs=specs,
+            out_specs=tuple(whole for _ in outs),
+            scratch_shapes=list(scratch),
+            compiler_params=pltpu.CompilerParams(vmem_limit_bytes=VMEM_LIMIT),
+            cost_estimate=pl.CostEstimate(flops=1, bytes_accessed=1, transcendentals=0),
+        )(*args)
+
+    return call
+
+
+def forward(starts, normed, cot, tab, cands):
     length, width = normed.shape
     step = length // 2
+    heads = 2 * GROUP
     outs = (
-        jax.ShapeDtypeStruct((length, PAIRS * QP), BF16),
-        jax.ShapeDtypeStruct((length, PAIRS * 128), BF16),
-        jax.ShapeDtypeStruct((length, PAIRS * 128), BF16),
-        jax.ShapeDtypeStruct((HEADS, step, step), BF16),
-        jax.ShapeDtypeStruct((HEADS, step, length), BF16),
-        jax.ShapeDtypeStruct((HEADS * HEAD_DIM, width), BF16),
-    )
-    return pl.pallas_call(
-        forward_kernel,
-        out_shape=outs,
-        grid=(PAIRS,),
-        in_specs=[full_spec(normed)] + w_specs(width) + [full_spec(cot), full_spec(tab)],
-        out_specs=saved_specs(length) + (pl.BlockSpec((QP, width), lambda i: (i, 0)),),
-        compiler_params=pltpu.CompilerParams(vmem_limit_bytes=VMEM_LIMIT),
-        cost_estimate=pl.CostEstimate(flops=32_000_000_000, bytes_accessed=30_000_000, transcendentals=0),
-    )(normed, w, w, w, cot, tab)
-
-
-def saved_specs(length, pair=None):
-    step = length // 2
-
-    def at(i):
-        return i if pair is None else pair
-
-    return (
-        pl.BlockSpec((length, QP), lambda i: (0, at(i))),
-        pl.BlockSpec((length, 128), lambda i: (0, at(i))),
-        pl.BlockSpec((length, 128), lambda i: (0, at(i))),
-        pl.BlockSpec((2 * GROUP, step, step), lambda i: (at(i), 0, 0)),
-        pl.BlockSpec((2 * GROUP, step, length), lambda i: (at(i), 0, 0)),
-    )
+        jax.ShapeDtypeStruct((length, QP), BF16),
+        jax.ShapeDtypeStruct((length, 128), BF16),
+        jax.ShapeDtypeStruct((length, 128), BF16),
+        jax.ShapeDtypeStruct((heads, step, step), BF16),
+        jax.ShapeDtypeStruct((heads, step, length), BF16),
+        jax.ShapeDtypeStruct((QP, width), BF16),
+        jax.ShapeDtypeStruct((width, CP), BF16),
+    )
+    call = vmem_call(
+        functools.partial(forward_kernel, len(cands)),
+        outs,
+        n_hbm=len(cands),
+        hbm_at=4,
+        smem=1,
+        scratch=[pltpu.SemaphoreType.DMA((len(cands),))],
+    )
+    return call(starts, normed, cot, tab, *cands)
 
 
 def backward(pair, normed_t, w, cot, wo, tab, saved, gain_in):
     width = w.shape[0]
+    rows = pl.BlockSpec((QP, width), lambda i: (pair, 0))
     outs = (
         jax.ShapeDtypeStruct((width, CP), BF16),
         jax.ShapeDtypeStruct((8, width), F32),
     )
-    return pl.pallas_call(
-        backward_kernel,
-        out_shape=outs,
-        grid=(1,),
-        in_specs=[full_spec(normed_t)]
-        + w_specs(width, pair)
-        + [full_spec(cot), pl.BlockSpec((QP, width), lambda i: (pair, 0)), full_spec(tab)]
-        + list(saved_specs(cot.shape[0], pair))
-        + [full_spec(gain_in)],
-        out_specs=tuple(full_spec(x) for x in outs),
-        compiler_params=pltpu.CompilerParams(vmem_limit_bytes=VMEM_LIMIT),
-        cost_estimate=pl.CostEstimate(flops=20_000_000_000, bytes_accessed=18_000_000, transcendentals=0),
-    )(normed_t, w, w, w, cot, wo, tab, *saved, gain_in)
+    return vmem_call(backward_kernel, outs, other={3: rows})(normed_t, w, cot, wo, tab, *saved, gain_in)
+
+
+def norm_kernel(x_ref, gain_ref, out_ref, out_t_ref):
+    block = 128
+    for at in range(x_ref.shape[0] // block):
+        cut = slice(at * block, at * block + block)
+        x = x_ref[cut, :].astype(F32)
+        factor = lax.rsqrt(jnp.mean(x * x, axis=1, keepdims=True) + NORM_EPS)
+        y = (x * factor * gain_ref[...]).astype(BF16)
+        out_ref[cut, :] = y
+        out_t_ref[:, cut] = y.astype(F32).T.astype(BF16)
+
+
+def norm(tokens, gain):
+    length, width = tokens.shape
+    outs = (jax.ShapeDtypeStruct((length, width), BF16), jax.ShapeDtypeStruct((width, length), BF16))
+    return vmem_call(norm_kernel, outs)(tokens, gain)
 
 
 def adam(wide, grad, first, second, decay):
@@ -265,58 +280,66 @@
     return new, first_next, second_next
 
 
-def adam_kernel(held, *refs):
-    grad, w, first, second, outer = refs[:5]
-    new, first_next, second_next = refs[5 + held :]
+def adam_kernel(n_parts, held, idx_ref, *refs):
+    grad = refs[0][0].astype(F32)
+    for part in refs[1:n_parts]:
+        grad = grad + part[0].astype(F32)
+    w, first, second, outer = refs[n_parts : n_parts + 4]
+    new, first_next, second_next = refs[n_parts + 4 + held :]
     new[...], first_next[...], second_next[...] = mixed_step(
-        w[...], grad[...].astype(F32), first[...], second[...], outer[...]
-    )
-
-
-def qkv_adam(pair, grad, w, first, second, outer, held):
+        w[...], grad, first[...], second[...], outer[...]
+    )
+
+
+def adam_call(grid, block, part_at, full_at, idx, parts, w, first, second, outer, held):
     rows, width = w.shape
-    q_blocks = QP // 128
-    first_k = HEADS * HEAD_DIM // 128
-    first_v = first_k + KV_HEADS * HEAD_DIM // 128
-
-    def column(j):
-        return (0, jnp.where(j < q_blocks, pair * q_blocks + j, jnp.where(j == q_blocks, first_k, first_v) + pair))
-
-    part = pl.BlockSpec((rows, 128), lambda j: (0, j))
-    full = pl.BlockSpec((rows, 128), column)
+
+    def part_spec(at):
+        return pl.BlockSpec((1,) + block, lambda j, idx: (idx[at],) + part_at(j))
+
+    full = pl.BlockSpec(block, lambda j, idx: full_at(j))
+    n_parts = len(parts)
     return pl.pallas_call(
-        functools.partial(adam_kernel, len(held)),
+        functools.partial(adam_kernel, n_parts, len(held)),
         out_shape=(
             jax.ShapeDtypeStruct((rows, width), BF16),
             jax.ShapeDtypeStruct((rows, width), F32),
             jax.ShapeDtypeStruct((rows, width), F32),
         ),
-        grid=(CP // 128,),
-        in_specs=[part] + [full] * 4 + [pl.BlockSpec(memory_space=pl.ANY)] * len(held),
-        out_specs=(full, full, full),
-        input_output_aliases={5 + i: i for i in range(len(held))},
+        grid_spec=pltpu.PrefetchScalarGridSpec(
+            num_scalar_prefetch=1,
+            grid=(grid,),
+            in_specs=[part_spec(i) for i in range(n_parts)]
+            + [full] * 4
+            + [pl.BlockSpec(memory_space=pl.ANY)] * len(held),
+            out_specs=(full, full, full),
+        ),
+        input_output_aliases={1 + n_parts + 4 + i: i for i in range(len(held))},
         compiler_params=pltpu.CompilerParams(vmem_limit_bytes=VMEM_LIMIT),
-        cost_estimate=pl.CostEstimate(flops=20_000_000, bytes_accessed=10_000_000, transcendentals=0),
-    )(grad, w, first, second, outer, *held)
+        cost_estimate=pl.CostEstimate(flops=20_000_000, bytes_accessed=14_000_000, transcendentals=0),
+    )(idx, *parts, w, first, second, outer, *held)
+
+
+def qkv_adam(pair, grad, w, first, second, outer, held):
+    q_blocks = QP // 128
+    first_k = HEADS * HEAD_DIM // 128
+    first_v = first_k + KV_HEADS * HEAD_DIM // 128
+
+    def column(j):
+        return (0, jnp.where(j < q_blocks, pair * q_blocks + j, jnp.where(j == q_blocks, first_k, first_v) + pair))
+
+    idx, parts = grad
+    return adam_call(
+        CP // 128, (w.shape[0], 128), lambda j: (0, j), column, idx, parts, w, first, second, outer, held
+    )
 
 
 def out_adam(grad, w, first, second, outer):
     rows, width = w.shape
-    block = 64
-    full = pl.BlockSpec((block, width), lambda i: (i, 0))
-    return pl.pallas_call(
-        functools.partial(adam_kernel, 0),
-        out_shape=(
-            jax.ShapeDtypeStruct((rows, width), BF16),
-            jax.ShapeDtypeStruct((rows, width), F32),
-            jax.ShapeDtypeStruct((rows, width), F32),
-        ),
-        grid=(rows // block,),
-        in_specs=[full] * 5,
-        out_specs=(full, full, full),
-        compiler_params=pltpu.CompilerParams(vmem_limit_bytes=VMEM_LIMIT),
-        cost_estimate=pl.CostEstimate(flops=20_000_000, bytes_accessed=14_000_000, transcendentals=0),
-    )(grad, w, first, second, outer)
+    idx, parts = grad
+    return adam_call(
+        rows // 64, (64, width), lambda j: (j, 0), lambda j: (j, 0), idx, parts, w, first, second, outer, ()
+    )
 
 
 def nesterov(global_value, momentum, average):
@@ -327,6 +350,59 @@
 
 def after(x, *others):
     return lax.optimization_barrier((x, *others))[0]
+
+
+def line_gather(x, me, before=None):
+    middle = jnp.logical_or(me == 1, me == 2)
+    near = jnp.where(me < 2, 2, 1)
+    far = jnp.where(me < 2, 3, 0)
+    pair = lax.ppermute(x, "fsdp", [(0, 1), (1, 0), (2, 3), (3, 2)])
+    mid_near = lax.ppermute(x, "fsdp", [(1, 2), (2, 1)])
+    waits = (pair, mid_near) if before is None else (pair, mid_near, before)
+    pair, mid_near = lax.optimization_barrier(waits)[:2]
+    mid_far = lax.ppermute(pair, "fsdp", [(1, 2), (2, 1)])
+    end_near = lax.ppermute(mid_near, "fsdp", [(1, 0), (2, 3)])
+    end_far = lax.ppermute(mid_far, "fsdp", [(1, 0), (2, 3)])
+    blocks = (x, pair, mid_near, mid_far, end_near, end_far)
+    places = (
+        me,
+        me ^ 1,
+        jnp.where(middle, near, -1),
+        jnp.where(middle, far, -1),
+        jnp.where(middle, -1, near),
+        jnp.where(middle, -1, far),
+    )
+    return blocks, places
+
+
+def gather(x, n, me, before=None):
+    if n == 4:
+        blocks, places = line_gather(x, me, before)
+    else:
+        blocks, places = (lax.all_gather(x, "fsdp", axis=0, tiled=True),), (me * 0,)
+    starts = jnp.stack([p * x.shape[0] for p in places]).astype(jnp.int32)
+    return blocks, starts
+
+
+def scatter(x, n, me):
+    rows = x.shape[0] // n
+    blocks = x.reshape(n, rows, x.shape[1])
+    if n != 4:
+        return jnp.zeros((1,), jnp.int32), (lax.psum_scatter(x, "fsdp", scatter_dimension=0, tiled=True)[None],)
+
+    def two(at):
+        return lax.dynamic_slice_in_dim(blocks, at, 2, 0)
+
+    def plus(a, b):
+        return (a.astype(F32) + b.astype(F32)).astype(BF16)
+
+    inward = lax.ppermute(two(jnp.where(me == 0, 2, 0)), "fsdp", [(3, 2), (0, 1)])
+    across = lax.ppermute(plus(two(jnp.where(me == 1, 2, 0)), inward), "fsdp", [(2, 1), (1, 2)])
+    passed = lax.dynamic_index_in_dim(across, jnp.where(me == 1, 0, 1), 0, keepdims=True)
+    other = lax.dynamic_index_in_dim(blocks, me ^ 1, 0, keepdims=True)
+    outward = lax.ppermute(plus(other, passed), "fsdp", [(0, 1), (1, 0), (2, 3), (3, 2)])
+    idx = jnp.stack([me, jnp.where(me == 1, 1, 0), me * 0]).astype(jnp.int32)
+    return idx, (blocks, across, outward)
 
 
 def all_sum(x, axis, n):
@@ -363,28 +439,27 @@
     w_out = out_weight[0]
     length, width = tokens.shape
 
-    all_qkv = lax.all_gather(w_qkv, "fsdp", axis=0, tiled=True)
-
-    wide = tokens.astype(F32)
-    factor = lax.rsqrt(jnp.mean(wide * wide, axis=-1, keepdims=True) + NORM_EPS)
-    normed = (wide * factor * gain).astype(BF16)
-    normed_t = normed.T
+    me = lax.axis_index("fsdp")
+    qw = HEADS * HEAD_DIM
+    kw = KV_HEADS * HEAD_DIM
+
+    got = []
+    for pair in range(PAIRS):
+        own = jnp.concatenate(
+            [
+                w_qkv[:, pair * QP : (pair + 1) * QP],
+                w_qkv[:, qw + pair * 128 : qw + (pair + 1) * 128],
+                w_qkv[:, qw + kw + pair * 128 : qw + kw + (pair + 1) * 128],
+            ],
+            axis=1,
+        )
+        if got:
+            own = after(own, *got[0][0][3:5])
+        got.append(gather(own, n, me, got[0][0][-1] if got else None))
+    all_out = lax.all_gather(after(w_out, *got[0][0][3:5]), "fsdp", axis=0, tiled=True)
+
+    normed, normed_t = norm(tokens, gain[None])
     tab = rope_tables(length)
-    all_out = lax.all_gather(after(w_out, all_qkv, normed, normed_t, tab), "fsdp", axis=0, tiled=True)
-
-    *saved, g_out = forward(normed, all_qkv, cotangent, tab)
-    out_grad = lax.psum_scatter(g_out, "fsdp", scatter_dimension=0, tiled=True)
-
-    gain_sum = jnp.zeros((8, width), F32)
-    qkv_grad = []
-    for pair in range(PAIRS):
-        grad, gain_sum = backward(
-            pair, normed_t, all_qkv, cotangent, all_out, tab, saved, gain_sum
-        )
-        qkv_grad.append(lax.psum_scatter(grad, "fsdp", scatter_dimension=0, tiled=True))
-
-    gain_grad = all_sum(gain_sum[0], "fsdp", n) / gain
-    gain_step, gain_first_next, gain_second_next = adam(gain, gain_grad, gain_first[0], gain_second[0], 0.0)
 
     scale = 1.0 / islands
     qkv_total = lax.psum_scatter(w_qkv, "island", scatter_dimension=1, tiled=True).astype(F32)
@@ -393,8 +468,29 @@
     gain_pair = nesterov(gain_global, gain_momentum, gain_total * scale)
     qkv_pair = nesterov(qkv_global, qkv_momentum, qkv_total * scale)
     out_pair = nesterov(out_global, out_momentum, out_total * scale)
-    qkv_whole = lax.all_gather(qkv_pair[0].astype(BF16), "island", axis=1, tiled=True)
-    out_whole = lax.all_gather(out_pair[0].astype(BF16), "island", axis=1, tiled=True)
+    saved = []
+    g_out = []
+    for pair in range(PAIRS):
+        blocks, starts = got[pair]
+        if pair:
+            starts = after(starts, qkv_pair[0], qkv_pair[1], out_pair[0], out_pair[1])
+        *kept, grad, w_pair = forward(starts, normed, cotangent, tab, blocks)
+        saved.append((kept, w_pair))
+        g_out.append(grad)
+    out_grad = scatter(jnp.concatenate(g_out, axis=0), n, me)
+
+    gain_sum = after(jnp.zeros((8, width), F32), *g_out)
+    qkv_grad = []
+    for pair in range(PAIRS):
+        kept, w_pair = saved[pair]
+        grad, gain_sum = backward(pair, normed_t, w_pair, cotangent, all_out, tab, kept, gain_sum)
+        qkv_grad.append(scatter(grad, n, me))
+
+    gain_grad = all_sum(gain_sum[0], "fsdp", n) / gain
+    gain_step, gain_first_next, gain_second_next = adam(gain, gain_grad, gain_first[0], gain_second[0], 0.0)
+
+    qkv_whole = lax.all_gather(after(qkv_pair[0].astype(BF16), g_out[1]), "island", axis=1, tiled=True)
+    out_whole = lax.all_gather(after(out_pair[0].astype(BF16), g_out[1]), "island", axis=1, tiled=True)
 
     out_state = out_adam(out_grad, w_out, out_first[0], out_second[0], out_whole)
     qkv_state = ()

time: 487 us -> 448 us (0.920)
  waiting for transfers between devices: 337 us -> 215 us
  starting transfers between devices: 4.53 us -> 42.5 us
  other arithmetic: 11.1 us -> 27.9 us
  local copies, waits for them, and re-layouts: 24 us -> 40.4 us
  Pallas kernels: 86.7 us -> 99.4 us
    ppermute x0 -> x19, waiting for transfers between devices: none -> 210 us  [the longest x3 44.2 us: scatter(): lax.ppermute(plus(two(jnp.where(me == 1, 2, 0)), inward), 'fsdp', [(2, 1)...]
    reduce_scatter x3 -> x0, waiting for transfers between devices: 190 us -> none  [the longest x2 109 us: shards(): lax.psum_scatter(grad, 'fsdp', scatter_dimension=0, tiled=True)]
    all_gather x4 -> x3, waiting for transfers between devices: 143 us -> 0.03 us  [the longest x1 0.03 us: shards(): lax.all_gather(after(w_out, *got[0][0][3:5]), 'fsdp', axis=0, tiled=True)]
    ppermute x0 -> x19, starting transfers between devices: none -> 38.6 us  [the longest x3 8.15 us: scatter(): lax.ppermute(plus(two(jnp.where(me == 1, 2, 0)), inward), 'fsdp', [(2, 1)...]
    convert_element_type x1 -> x6, other arithmetic: 1.86 us -> 17.3 us  [plus(): return (a.astype(F32) + b.astype(F32)).astype(BF16)]
    pallas_call x6 -> x8, Pallas kernels: 86.7 us -> 99.4 us  [the longest x5 77.8 us: call(): pl.pallas_call(kernel, out_shape=outs, grid=(1,), in_specs=specs, out_spe...]
    unnamed x35 -> x84, local copies, waits for them, and re-layouts: 18.1 us -> 27.1 us
    dynamic_slice x0 -> x3, local copies, waits for them, and re-layouts: none -> 7.04 us  [two(): return lax.dynamic_slice_in_dim(blocks, at, 2, 0)]
  transfers between devices with their start and end apart: 14 -> 29, of which waited for: 8 -> 13; matrix products, arithmetic and copies ran while one was open for 6% -> 12% of each run, Pallas kernels for 17% -> 21%
where the time goes in v3:
time: 448 us; the launch traced here: 441 us
  waiting for transfers between devices  215 us (48%)
  Pallas kernels  99.4 us (22%)
  starting transfers between devices  42.5 us (9%)
  local copies, waits for them, and re-layouts  40.4 us (9%)
  other arithmetic  27.9 us (6%)
  between operations  16 us (4%)
    pallas_call x5, Pallas kernels, call(): pl.pallas_call(kernel, out_shape=outs, grid=(1,), in_specs=specs, out_spe...  77.8 us
    ppermute x3, waiting for transfers between devices, scatter(): lax.ppermute(plus(two(jnp.where(me == 1, 2, 0)), inward), 'fsdp', [(2, 1)...  44.2 us
    ppermute x2, waiting for transfers between devices, line_gather(): pair = lax.ppermute(x, 'fsdp', [(0, 1), (1, 0), (2, 3), (3, 2)])  43.8 us
    ppermute x2, waiting for transfers between devices, line_gather(): end_far = lax.ppermute(mid_far, 'fsdp', [(1, 0), (2, 3)])  42.2 us
    ppermute x3, waiting for transfers between devices, scatter(): lax.ppermute(two(jnp.where(me == 0, 2, 0)), 'fsdp', [(3, 2), (0, 1)])  40.4 us
    unnamed x84, local copies, waits for them, and re-layouts  27.1 us
    ppermute x2, waiting for transfers between devices, line_gather(): mid_near = lax.ppermute(x, 'fsdp', [(1, 2), (2, 1)])  25.5 us
    pallas_call x3, Pallas kernels, adam_call(): pl.pallas_call(functools.partial(adam_kernel, n_parts, len(held)), out_sh...  21.6 us
  transfers between devices with their start and end apart: 29, of which 13 were waited for; matrix products, arithmetic and copies ran while one was open for 12% of the time, Pallas kernels for 21%

profile of v3, /device:TPU:22, one launch (start us, length us, event | category | flops | bytes accessed | tf_op | source)
XLA Modules:
  0.0 440.9 jit_solution(12917835091662672207)
XLA Ops:
  8.8 2.7 copy.48
  12.6 2.4 collective-permute-start.1
  15.1 18.7 %collective-permute-done.1.refs_2_ = bf16[512,768]{1,0:T(8,128)(2,1)S(1)} collective-permute-done((bf16[512,768]{1,0:T(8,128)(2,1)S(1)}, bf16[512,768]{1,0:T(8,128)(2,1)S(1)}, u32[]{:S(2)}, u32[]{:S(2)}) %collective-permute-start.1) | collective-permute-done | bytes 786464 | tf_op jit(solution)/shard_map/ppermute | solution.py:360
  34.1 3.5 collective-permute-start.2
  38.4 2.2 collective-permute-start.3
  40.6 13.5 %collective-permute-done.2.refs_3_ = bf16[512,768]{1,0:T(8,128)(2,1)S(1)} collective-permute-done((bf16[512,768]{1,0:T(8,128)(2,1)S(1)}, bf16[512,768]{1,0:T(8,128)(2,1)S(1)}, u32[]{:S(2)}, u32[]{:S(2)}) %collective-permute-start.2) | collective-permute-done | bytes 786464 | tf_op jit(solution)/shard_map/ppermute | solution.py:363
  56.5 4.7 %collective-permute-start.6 = (bf16[512,768]{1,0:T(8,128)(2,1)}, bf16[512,768]{1,0:T(8,128)(2,1)S(1)}, u32[]{:S(2)}, u32[]{:S(2)}) collective-permute-start(bf16[512,768]{1,0:T(8,128)(2,1)} %copy-done.32), channel_id=1, source_target_pairs={{1,0},{2,3},{5,4},{6,7},{9,8},{10,11},{13,12},{14,15},{17,16},{18,... | collective-permute-start | bytes 2359304 | tf_op jit(solution)/shard_map/ppermute | solution.py:365
  61.2 2.4 collective-permute-start.5
  63.7 42.2 %collective-permute-done.6.refs_5_ = bf16[512,768]{1,0:T(8,128)(2,1)S(1)} collective-permute-done((bf16[512,768]{1,0:T(8,128)(2,1)}, bf16[512,768]{1,0:T(8,128)(2,1)S(1)}, u32[]{:S(2)}, u32[]{:S(2)}) %collective-permute-start.6) | collective-permute-done | bytes 786464 | tf_op jit(solution)/shard_map/ppermute | solution.py:365
  105.9 6.8 %collective-permute-done.5.refs_2_ = bf16[512,768]{1,0:T(8,128)(2,1)} collective-permute-done((bf16[512,768]{1,0:T(8,128)(2,1)S(1)}, bf16[512,768]{1,0:T(8,128)(2,1)}, u32[]{:S(2)}, u32[]{:S(2)}) %collective-permute-start.5) | collective-permute-done | bytes 786464 | tf_op jit(solution)/shard_map/ppermute | solution.py:360
  112.7 43.6 %collective-permute-done.4.refs_1_ = bf16[512,768]{1,0:T(8,128)(2,1)} collective-permute-done((bf16[512,768]{1,0:T(8,128)(2,1)S(1)}, bf16[512,768]{1,0:T(8,128)(2,1)}, u32[]{:S(2)}, u32[]{:S(2)}) %collective-permute-start.4) | collective-permute-done | bytes 786464 | tf_op jit(solution)/shard_map/ppermute | solution.py:359
  156.3 2.5 collective-permute-start.7
  158.8 4.1 shard_map.280
  165.2 2.0 copy.41
  168.9 4.4 %collective-permute-start.8 = (bf16[512,768]{1,0:T(8,128)(2,1)}, bf16[512,768]{1,0:T(8,128)(2,1)}, u32[]{:S(2)}, u32[]{:S(2)}) collective-permute-start(bf16[512,768]{1,0:T(8,128)(2,1)} %collective-permute-done.5.refs_2_), channel_id=1, source_target_pairs={{1,0},{2,3},{5,4},{6,7},{9,8},{10,11},{13,12},{14,15},{17,16},{18,... | collective-permute-start | bytes 2359304 | tf_op jit(solution)/shard_map/ppermute | solution.py:364
  173.3 2.2 collective-permute-start.9
  175.9 2.0 fusion.4
  180.1 19.2 %shard_map.282 = (bf16[512,512]{1,0:T(8,128)(2,1)S(1)}, bf16[512,128]{1,0:T(8,128)(2,1)S(1)}, bf16[512,128]{1,0:T(8,128)(2,1)S(1)}, bf16[8,256,256]{2,1,0:T(8,12...) custom-call(s32[6]{0:T(128)S(1)} %stack.61.starts, ...), custom_call_target="tpu_custom_call" | custom-call | flops 1 | bytes 1 | tf_op jit(solution)/shard_map/pallas_call | solution.py:201
  200.2 1.8 copy.49
  202.0 2.5 fusion.5
  204.5 18.9 %shard_map.281 = (bf16[512,512]{1,0:T(8,128)(2,1)S(1)}, bf16[512,128]{1,0:T(8,128)(2,1)S(1)}, bf16[512,128]{1,0:T(8,128)(2,1)S(1)}, bf16[8,256,256]{2,1,0:T(8,12...) custom-call(s32[6]{0:T(128)S(1)} %stack.61.starts, ...), custom_call_target="tpu_custom_call" | custom-call | flops 1 | bytes 1 | tf_op jit(solution)/shard_map/pallas_call | solution.py:201
  223.4 2.4 pad_maximum_fusion
  225.8 2.0 copy-done.28
  232.9 17.8 %shard_map.283 = (bf16[2048,768]{1,0:T(8,128)(2,1)}, f32[8,2048]{1,0:T(8,128)S(1)}) custom-call(bf16[2048,512]{1,0:T(8,128)(2,1)} %get-tuple-element.54.normed_t, bf16[2048,768]{1,0:T(8,128)(2,1)} %get-tuple-element.69.w_ref, bf16[512,2048]{1,0:T(8,128)(2,1)} %cot.7, bf16[1024,2048]{1,0:T(8,128)(2,1)} %all-gather.4.cloned.1.call-done.wo, ...), custom_call_target="tpu_custom_call" | custom-call | flops 1 | bytes 1 | tf_op jit(solution)/shard_map/pallas_call | solution.py:201
  251.4 2.7 constant_dynamic-slice_fusion.1
  260.4 17.8 %shard_map.284 = (bf16[2048,768]{1,0:T(8,128)(2,1)}, f32[8,2048]{1,0:T(8,128)S(1)}) custom-call(bf16[2048,512]{1,0:T(8,128)(2,1)} %get-tuple-element.54.normed_t, bf16[2048,768]{1,0:T(8,128)(2,1)} %get-tuple-element.62.w_ref, bf16[512,2048]{1,0:T(8,128)(2,1)} %cot.7, bf16[1024,2048]{1,0:T(8,128)(2,1)} %all-gather.4.cloned.1.call-done.wo, ...), custom_call_target="tpu_custom_call" | custom-call | flops 1 | bytes 1 | tf_op jit(solution)/shard_map/pallas_call | solution.py:201
  278.9 2.7 constant_dynamic-slice_fusion.2
  282.9 4.6 %add_convert_fusion = bf16[2,256,2048]{2,1,0:T(8,128)(2,1)} fusion(bf16[2,256,2048]{2,1,0:T(8,128)(2,1)} %collective-permute-done.21, bf16[4,256,2048]{2,1,0:T(8,128)(2,1)} %bitcast.50, s32[]{:T(128)S(6)} %select_n.72), kind=kLoop, calls=%fused_computation.1 | loop fusion | flops 4194304 | bytes 6291460 | tf_op jit(solution)/shard_map/convert_element_type | solution.py:397
  287.6 2.7 collective-permute-start.22
  290.3 23.6 %collective-permute-done.18 = bf16[2,512,768]{2,1,0:T(8,128)(2,1)} collective-permute-done((bf16[2,512,768]{2,1,0:T(8,128)(2,1)}, bf16[2,512,768]{2,1,0:T(8,128)(2,1)}, u32[]{:S(2)}, u32[]{:S(2)}) %collective-permute-start.18) | collective-permute-done | bytes 1572896 | tf_op jit(solution)/shard_map/ppermute | solution.py:399
  313.9 2.9 add_convert_fusion.1
  316.8 2.8 collective-permute-start.19
  319.6 16.8 %collective-permute-done.15 = bf16[2,512,768]{2,1,0:T(8,128)(2,1)S(1)} collective-permute-done((bf16[2,512,768]{2,1,0:T(8,128)(2,1)}, bf16[2,512,768]{2,1,0:T(8,128)(2,1)S(1)}, u32[]{:S(2)}, u32[]{:S(2)}) %collective-permute-start.15) | collective-permute-done | bytes 1572896 | tf_op jit(solution)/shard_map/ppermute | solution.py:399
  338.0 2.7 collective-permute-start.16
  343.3 2.9 add_convert_fusion.3
  346.2 2.0 collective-permute-start.23
  348.2 24.1 %collective-permute-done.19.refs_1_ = bf16[2,512,768]{2,1,0:T(8,128)(2,1)} collective-permute-done((bf16[2,512,768]{2,1,0:T(8,128)(2,1)}, bf16[2,512,768]{2,1,0:T(8,128)(2,1)}, u32[]{:S(2)}, u32[]{:S(2)}) %collective-permute-start.19) | collective-permute-done | bytes 1572896 | tf_op jit(solution)/shard_map/ppermute | solution.py:400
  372.3 2.4 add_convert_fusion.4
  374.7 20.1 %collective-permute-done.16.refs_1_ = bf16[2,512,768]{2,1,0:T(8,128)(2,1)S(1)} collective-permute-done((bf16[2,512,768]{2,1,0:T(8,128)(2,1)}, bf16[2,512,768]{2,1,0:T(8,128)(2,1)S(1)}, u32[]{:S(2)}, u32[]{:S(2)}) %collective-permute-start.16) | collective-permute-done | bytes 1572896 | tf_op jit(solution)/shard_map/ppermute | solution.py:400
  394.8 2.8 add_convert_fusion.5
  398.1 2.2 collective-permute-start.11
  400.4 2.0 copy.46
  402.4 2.1 copy.47
  404.5 2.6 copy.45.refs_6_
  407.1 3.0 collective-permute-done.11
  411.9 7.2 %shard_map.287 = (bf16[256,2048]{1,0:T(8,128)(2,1)}, f32[256,2048]{1,0:T(8,128)}, f32[256,2048]{1,0:T(8,128)}) custom-call(s32[3]{0:T(128)S(1)} %pad_add_fusion.idx_ref, bf16[4,256,2048]{2,1,0:T(8,128)(2,1)} %bitcast.52, bf16[2,256,2048]{2,1,0:T(8,128)(2,1)} %collective-permute-done.22.refs_1_, bf16[1,256,2048]{2,1,0:T(8,128)(2,1)} %collective-permute-done.23.refs_2_, ...), custom_call_target="tpu_custom_call" | custom-call | flops 20000000 | bytes 14000000 | tf_op jit(solution)/shard_map/pallas_call | solution.py:302
  419.1 7.3 %shard_map.285 = (bf16[512,1536]{1,0:T(8,128)(2,1)}, f32[512,1536]{1,0:T(8,128)}, f32[512,1536]{1,0:T(8,128)}) custom-call(s32[3]{0:T(128)S(1)} %pad_add_fusion.idx_ref, bf16[4,512,768]{2,1,0:T(8,128)(2,1)} %bitcast.59, bf16[2,512,768]{2,1,0:T(8,128)(2,1)} %collective-permute-done.19.refs_1_, bf16[1,512,768]{2,1,0:T(8,128)(2,1)} %collective-permute-done.20.refs_2_, ...), custom_call_target="tpu_custom_call" | custom-call | flops 20000000 | bytes 14000000 | tf_op jit(solution)/shard_map/pallas_call | solution.py:302
  426.5 7.1 %shard_map.286 = (bf16[512,1536]{1,0:T(8,128)(2,1)}, f32[512,1536]{1,0:T(8,128)}, f32[512,1536]{1,0:T(8,128)}) custom-call(s32[3]{0:T(128)S(1)} %pad_add_fusion.idx_ref, bf16[4,512,768]{2,1,0:T(8,128)(2,1)} %bitcast.55, bf16[2,512,768]{2,1,0:T(8,128)(2,1)S(1)} %copy-done.4, ...), custom_call_target="tpu_custom_call", output_to_operand_aliasing={{0}: (8, {}), {1}: (9, {}), {2}: (10, {})} | custom-call | flops 20000000 | bytes 14000000 | tf_op jit(solution)/shard_map/pallas_call | solution.py:302
  (141 shorter events, 33.4 us)
Async XLA Ops:
  8.0 167.9 %reduce-scatter.5.cloned.1.call-start = ((), (), s32[]{:S(2)}) async-start(), calls=%async_computation.2 | async-start | bytes 1179648 | tf_op jit(solution)/shard_map/reduce_scatter | solution.py:466
  8.7 191.4 %reduce-scatter.7.cloned.1.call-start = ((), (), s32[]{:S(2)}) async-start(), calls=%async_computation.6 | async-start | bytes 1769472
  11.5 219.4 %all-gather.4.cloned.1.call-start = ((), (), s32[]{:S(2)}) async-start(), calls=%async_computation.3 | async-start | bytes 5242880 | tf_op jit(solution)/shard_map/all_gather | solution.py:459
  12.6 146.2 %copy-start.24 = (f32[1,2048]{1,0:T(1,128)S(1)}, f32[1,2048]{1,0:T(1,128)}, u32[]{:S(2)}) copy-start(f32[1,2048]{1,0:T(1,128)} %gain_ref.1) | copy-start | bytes 24580
  12.6 21.2 %collective-permute-start.1 = (bf16[512,768]{1,0:T(8,128)(2,1)S(1)}, bf16[512,768]{1,0:T(8,128)(2,1)S(1)}, u32[]{:S(2)}, u32[]{:S(2)}) collective-permute-start(bf16[512,768]{1,0:T(8,128)(2,1)S(1)} %pad_maximum_fusion.3.refs_0_), channel_id=1, source_target_pairs={{1,2},{2,1},{5,6},{6,5},{9,10},{10,9},{13,14},{14,13},{17,18},{18,... | collective-permute-start | bytes 2359304 | tf_op jit(solution)/shard_map/ppermute | solution.py:360
  15.0 19.1 %collective-permute-start = (bf16[512,768]{1,0:T(8,128)(2,1)S(1)}, bf16[512,768]{1,0:T(8,128)(2,1)S(1)}, u32[]{:S(2)}, u32[]{:S(2)}) collective-permute-start(bf16[512,768]{1,0:T(8,128)(2,1)S(1)} %pad_maximum_fusion.3.refs_0_), channel_id=1, source_target_pairs={{0,1},{1,0},{2,3},{3,2},{4,5},{5,4},{6,7},{7,6},{8,9},{9,8},{10,11... | collective-permute-start | bytes 2359304 | tf_op jit(solution)/shard_map/ppermute | solution.py:359
  33.8 21.6 %copy-start.10 = (bf16[512,768]{1,0:T(8,128)(2,1)}, bf16[512,768]{1,0:T(8,128)(2,1)S(1)}, u32[]{:S(2)}) copy-start(bf16[512,768]{1,0:T(8,128)(2,1)S(1)} %collective-permute-done.1.refs_2_) | copy-start | bytes 2359300
  34.1 20.0 %collective-permute-start.2 = (bf16[512,768]{1,0:T(8,128)(2,1)S(1)}, bf16[512,768]{1,0:T(8,128)(2,1)S(1)}, u32[]{:S(2)}, u32[]{:S(2)}) collective-permute-start(bf16[512,768]{1,0:T(8,128)(2,1)S(1)} %collective-permute-done.refs_1_), channel_id=1, source_target_pairs={{1,2},{2,1},{5,6},{6,5},{9,10},{10,9},{13,14},{14,13},{17,18},{18,... | collective-permute-start | bytes 2359304 | tf_op jit(solution)/shard_map/ppermute | solution.py:363
  38.4 16.9 %collective-permute-start.3 = (bf16[512,768]{1,0:T(8,128)(2,1)S(1)}, bf16[512,768]{1,0:T(8,128)(2,1)}, u32[]{:S(2)}, u32[]{:S(2)}) collective-permute-start(bf16[512,768]{1,0:T(8,128)(2,1)S(1)} %collective-permute-done.1.refs_2_), channel_id=1, source_target_pairs={{1,0},{2,3},{5,4},{6,7},{9,8},{10,11},{13,12},{14,15},{17,16},{18,... | collective-permute-start | bytes 2359304 | tf_op jit(solution)/shard_map/ppermute | solution.py:364
  55.3 349.2 %all-gather.6.cloned.1.call-start = ((), (), s32[]{:S(2)}) async-start(), calls=%async_computation.4 | async-start | bytes 1769472 | tf_op jit(solution)/shard_map/all_gather | solution.py:492
  56.5 111.9 %copy-start.5 = (bf16[512,768]{1,0:T(8,128)(2,1)}, bf16[512,768]{1,0:T(8,128)(2,1)S(1)}, u32[]{:S(2)}) copy-start(bf16[512,768]{1,0:T(8,128)(2,1)S(1)} %pad_maximum_fusion.2.refs_0_) | copy-start | bytes 2359300
  56.5 107.7 %copy-start.34 = (f32[512,192]{0,1:T(8,128)S(1)}, f32[512,192]{0,1:T(8,128)}, u32[]{:S(2)}) copy-start(f32[512,192]{0,1:T(8,128)} %param.30) | copy-start | bytes 1179652
  56.5 49.4 %collective-permute-start.6 = (bf16[512,768]{1,0:T(8,128)(2,1)}, bf16[512,768]{1,0:T(8,128)(2,1)S(1)}, u32[]{:S(2)}, u32[]{:S(2)}) collective-permute-start(bf16[512,768]{1,0:T(8,128)(2,1)} %copy-done.32), channel_id=1, source_target_pairs={{1,0},{2,3},{5,4},{6,7},{9,8},{10,11},{13,12},{14,15},{17,16},{18,... | collective-permute-start | bytes 2359304 | tf_op jit(solution)/shard_map/ppermute | solution.py:365
  61.2 51.5 %collective-permute-start.5 = (bf16[512,768]{1,0:T(8,128)(2,1)S(1)}, bf16[512,768]{1,0:T(8,128)(2,1)}, u32[]{:S(2)}, u32[]{:S(2)}) collective-permute-start(bf16[512,768]{1,0:T(8,128)(2,1)S(1)} %pad_maximum_fusion.2.refs_0_), channel_id=1, source_target_pairs={{1,2},{2,1},{5,6},{6,5},{9,10},{10,9},{13,14},{14,13},{17,18},{18,... | collective-permute-start | bytes 2359304 | tf_op jit(solution)/shard_map/ppermute | solution.py:360
  63.6 92.7 %collective-permute-start.4 = (bf16[512,768]{1,0:T(8,128)(2,1)S(1)}, bf16[512,768]{1,0:T(8,128)(2,1)}, u32[]{:S(2)}, u32[]{:S(2)}) collective-permute-start(bf16[512,768]{1,0:T(8,128)(2,1)S(1)} %pad_maximum_fusion.2.refs_0_), channel_id=1, source_target_pairs={{0,1},{1,0},{2,3},{3,2},{4,5},{5,4},{6,7},{7,6},{8,9},{9,8},{10,11... | collective-permute-start | bytes 2359304 | tf_op jit(solution)/shard_map/ppermute | solution.py:359
  105.9 50.4 %copy-start.33 = (bf16[512,768]{1,0:T(8,128)(2,1)}, bf16[512,768]{1,0:T(8,128)(2,1)S(1)}, u32[]{:S(2)}) copy-start(bf16[512,768]{1,0:T(8,128)(2,1)S(1)} %collective-permute-done.6.refs_5_) | copy-start | bytes 2359300
  156.3 17.0 %collective-permute-start.7 = (bf16[512,768]{1,0:T(8,128)(2,1)}, bf16[512,768]{1,0:T(8,128)(2,1)}, u32[]{:S(2)}, u32[]{:S(2)}) collective-permute-start(bf16[512,768]{1,0:T(8,128)(2,1)} %collective-permute-done.4.refs_1_), channel_id=1, source_target_pairs={{1,2},{2,1},{5,6},{6,5},{9,10},{10,9},{13,14},{14,13},{17,18},{18,... | collective-permute-start | bytes 2359304 | tf_op jit(solution)/shard_map/ppermute | solution.py:363
  168.9 35.6 %collective-permute-start.8 = (bf16[512,768]{1,0:T(8,128)(2,1)}, bf16[512,768]{1,0:T(8,128)(2,1)}, u32[]{:S(2)}, u32[]{:S(2)}) collective-permute-start(bf16[512,768]{1,0:T(8,128)(2,1)} %collective-permute-done.5.refs_2_), channel_id=1, source_target_pairs={{1,0},{2,3},{5,4},{6,7},{9,8},{10,11},{13,12},{14,15},{17,16},{18,... | collective-permute-start | bytes 2359304 | tf_op jit(solution)/shard_map/ppermute | solution.py:364
  173.3 31.2 %collective-permute-start.9 = (bf16[512,768]{1,0:T(8,128)(2,1)}, bf16[512,768]{1,0:T(8,128)(2,1)}, u32[]{:S(2)}, u32[]{:S(2)}) collective-permute-start(bf16[512,768]{1,0:T(8,128)(2,1)} %collective-permute-done.7.refs_3_), channel_id=1, source_target_pairs={{1,0},{2,3},{5,4},{6,7},{9,8},{10,11},{13,12},{14,15},{17,16},{18,... | collective-permute-start | bytes 2359304 | tf_op jit(solution)/shard_map/ppermute | solution.py:365
  200.2 23.2 %copy-start.18 = (bf16[512,128]{1,0:T(8,128)(2,1)}, bf16[512,128]{1,0:T(8,128)(2,1)S(1)}, u32[]{:S(2)}) copy-start(bf16[512,128]{1,0:T(8,128)(2,1)S(1)} %get-tuple-element.72.v_ref) | copy-start | bytes 393220
  200.2 4.3 copy-start.6
  204.5 18.9 %copy-start.31 = (bf16[512,2048]{1,0:T(8,128)(2,1)S(1)}, bf16[512,2048]{1,0:T(8,128)(2,1)}, u32[]{:S(2)}) copy-start(bf16[512,2048]{1,0:T(8,128)(2,1)} %get-tuple-element.75) | copy-start | bytes 6291460
  229.4 53.5 %collective-permute-start.21 = (bf16[2,256,2048]{2,1,0:T(8,128)(2,1)}, bf16[2,256,2048]{2,1,0:T(8,128)(2,1)}, u32[]{:S(2)}, u32[]{:S(2)}) collective-permute-start(bf16[2,256,2048]{2,1,0:T(8,128)(2,1)} %constant_dynamic-slice_fusion), channel_id=1, source_target_pairs={{3,2},{0,1},{7,6},{4,5},{11,10},{8,9},{15,14},{12,13},{19,18},{16,... | collective-permute-start | bytes 6291464 | tf_op jit(solution)/shard_map/ppermute | solution.py:399
  251.4 6.3 %copy-start.8 = (bf16[8,256,256]{2,1,0:T(8,128)(2,1)S(1)}, bf16[8,256,256]{2,1,0:T(8,128)(2,1)}, u32[]{:S(2)}) copy-start(bf16[8,256,256]{2,1,0:T(8,128)(2,1)} %get-tuple-element.67.top_ref) | copy-start | bytes 3145732
  251.4 6.3 %copy-start.21 = (bf16[512,128]{1,0:T(8,128)(2,1)S(1)}, bf16[512,128]{1,0:T(8,128)(2,1)}, u32[]{:S(2)}) copy-start(bf16[512,128]{1,0:T(8,128)(2,1)} %copy-done.20) | copy-start | bytes 393220
  254.1 59.8 %collective-permute-start.18 = (bf16[2,512,768]{2,1,0:T(8,128)(2,1)}, bf16[2,512,768]{2,1,0:T(8,128)(2,1)}, u32[]{:S(2)}, u32[]{:S(2)}) collective-permute-start(bf16[2,512,768]{2,1,0:T(8,128)(2,1)} %constant_dynamic-slice_fusion.1), channel_id=1, source_target_pairs={{3,2},{0,1},{7,6},{4,5},{11,10},{8,9},{15,14},{12,13},{19,18},{16,... | collective-permute-start | bytes 4718600 | tf_op jit(solution)/shard_map/ppermute | solution.py:399
  257.2 153.5 %all-gather.8.cloned.1.call-start = ((), (), s32[]{:S(2)}) async-start(), calls=%async_computation.5 | async-start | bytes 1179648 | tf_op jit(solution)/shard_map/all_gather | solution.py:493
  281.6 54.8 %collective-permute-start.15 = (bf16[2,512,768]{2,1,0:T(8,128)(2,1)}, bf16[2,512,768]{2,1,0:T(8,128)(2,1)S(1)}, u32[]{:S(2)}, u32[]{:S(2)}) collective-permute-start(bf16[2,512,768]{2,1,0:T(8,128)(2,1)} %constant_dynamic-slice_fusion.2), channel_id=1, source_target_pairs={{3,2},{0,1},{7,6},{4,5},{11,10},{8,9},{15,14},{12,13},{19,18},{16,... | collective-permute-start | bytes 4718600 | tf_op jit(solution)/shard_map/ppermute | solution.py:399
  282.9 31.0 %copy-start.30 = (bf16[2048,768]{1,0:T(8,128)(2,1)S(1)}, bf16[2048,768]{1,0:T(8,128)(2,1)}, u32[]{:S(2)}) copy-start(bf16[2048,768]{1,0:T(8,128)(2,1)} %get-tuple-element.82) | copy-start | bytes 9437188
  287.6 48.8 %copy-start.29 = (bf16[2048,768]{1,0:T(8,128)(2,1)S(1)}, bf16[2048,768]{1,0:T(8,128)(2,1)}, u32[]{:S(2)}) copy-start(bf16[2048,768]{1,0:T(8,128)(2,1)} %get-tuple-element.80) | copy-start | bytes 9437188
  287.6 55.7 %collective-permute-start.22 = (bf16[2,256,2048]{2,1,0:T(8,128)(2,1)}, bf16[2,256,2048]{2,1,0:T(8,128)(2,1)}, u32[]{:S(2)}, u32[]{:S(2)}) collective-permute-start(bf16[2,256,2048]{2,1,0:T(8,128)(2,1)} %add_convert_fusion), channel_id=1, source_target_pairs={{2,1},{1,2},{6,5},{5,6},{10,9},{9,10},{14,13},{13,14},{18,17},{17,... | collective-permute-start | bytes 6291464 | tf_op jit(solution)/shard_map/ppermute | solution.py:400
  316.8 23.9 %copy-start.37 = (f32[1,2048]{1,0:T(1,128)S(1)}, f32[1,2048]{1,0:T(1,128)}, u32[]{:S(2)}) copy-start(f32[1,2048]{1,0:T(1,128)} %param.22) | copy-start | bytes 24580
  316.8 55.5 %collective-permute-start.19 = (bf16[2,512,768]{2,1,0:T(8,128)(2,1)}, bf16[2,512,768]{2,1,0:T(8,128)(2,1)}, u32[]{:S(2)}, u32[]{:S(2)}) collective-permute-start(bf16[2,512,768]{2,1,0:T(8,128)(2,1)} %add_convert_fusion.1), channel_id=1, source_target_pairs={{2,1},{1,2},{6,5},{5,6},{10,9},{9,10},{14,13},{13,14},{18,17},{17,... | collective-permute-start | bytes 4718600 | tf_op jit(solution)/shard_map/ppermute | solution.py:400
  338.0 56.8 %collective-permute-start.16 = (bf16[2,512,768]{2,1,0:T(8,128)(2,1)}, bf16[2,512,768]{2,1,0:T(8,128)(2,1)S(1)}, u32[]{:S(2)}, u32[]{:S(2)}) collective-permute-start(bf16[2,512,768]{2,1,0:T(8,128)(2,1)} %add_convert_fusion.2), channel_id=1, source_target_pairs={{2,1},{1,2},{6,5},{5,6},{10,9},{9,10},{14,13},{13,14},{18,17},{17,... | collective-permute-start | bytes 4718600 | tf_op jit(solution)/shard_map/ppermute | solution.py:400
  340.7 1.2 collective-permute-start.12
  341.9 55.7 %collective-permute-start.13 = (f32[2048]{0:T(1024)S(1)}, f32[2048]{0:T(1024)S(1)}, u32[]{:S(2)}, u32[]{:S(2)}) collective-permute-start(f32[2048]{0:T(1024)S(1)} %add.103), channel_id=1, source_target_pairs={{0,8},{4,12},{8,0},{12,4},{16,24},{20,28},{24,16},{28,20},{1,9},{5... | collective-permute-start | bytes 24584 | tf_op jit(solution)/shard_map/ppermute | solution.py:411
  343.3 54.9 %collective-permute-start.10 = (f32[2048]{0:T(1024)S(1)}, f32[2048]{0:T(1024)S(1)}, u32[]{:S(2)}, u32[]{:S(2)}) collective-permute-start(f32[2048]{0:T(1024)S(1)} %bitcast.74), channel_id=1, source_target_pairs={{0,1},{1,0},{2,3},{3,2},{4,5},{5,4},{6,7},{7,6},{8,9},{9,8},{10,11... | collective-permute-start | bytes 24584 | tf_op jit(solution)/shard_map/ppermute | solution.py:411
  346.2 51.4 %copy-start.38 = (f32[1,2048]{1,0:T(1,128)S(1)}, f32[1,2048]{1,0:T(1,128)}, u32[]{:S(2)}) copy-start(f32[1,2048]{1,0:T(1,128)} %param.23) | copy-start | bytes 24580
  346.2 64.5 %collective-permute-start.23 = (bf16[1,256,2048]{2,1,0:T(8,128)(2,1)}, bf16[1,256,2048]{2,1,0:T(8,128)(2,1)}, u32[]{:S(2)}, u32[]{:S(2)}) collective-permute-start(bf16[1,256,2048]{2,1,0:T(8,128)(2,1)} %add_convert_fusion.3), channel_id=1, source_target_pairs={{0,1},{1,0},{2,3},{3,2},{4,5},{5,4},{6,7},{7,6},{8,9},{9,8},{10,11... | collective-permute-start | bytes 3145736 | tf_op jit(solution)/shard_map/ppermute | solution.py:403
  374.7 44.4 %collective-permute-start.20 = (bf16[1,512,768]{2,1,0:T(8,128)(2,1)}, bf16[1,512,768]{2,1,0:T(8,128)(2,1)}, u32[]{:S(2)}, u32[]{:S(2)}) collective-permute-start(bf16[1,512,768]{2,1,0:T(8,128)(2,1)} %add_convert_fusion.4), channel_id=1, source_target_pairs={{0,1},{1,0},{2,3},{3,2},{4,5},{5,4},{6,7},{7,6},{8,9},{9,8},{10,11... | collective-permute-start | bytes 2359304 | tf_op jit(solution)/shard_map/ppermute | solution.py:403
  394.8 5.6 %copy-start.3 = (bf16[2,512,768]{2,1,0:T(8,128)(2,1)}, bf16[2,512,768]{2,1,0:T(8,128)(2,1)S(1)}, u32[]{:S(2)}) copy-start(bf16[2,512,768]{2,1,0:T(8,128)(2,1)S(1)} %collective-permute-done.16.refs_1_) | copy-start | bytes 4718596
  397.6 28.9 %collective-permute-start.17 = (bf16[1,512,768]{2,1,0:T(8,128)(2,1)}, bf16[1,512,768]{2,1,0:T(8,128)(2,1)}, u32[]{:S(2)}, u32[]{:S(2)}) collective-permute-start(bf16[1,512,768]{2,1,0:T(8,128)(2,1)} %add_convert_fusion.5), channel_id=1, source_target_pairs={{0,1},{1,0},{2,3},{3,2},{4,5},{5,4},{6,7},{7,6},{8,9},{9,8},{10,11... | collective-permute-start | bytes 2359304 | tf_op jit(solution)/shard_map/ppermute | solution.py:403
  397.6 9.4 %collective-permute-start.14 = (f32[2048]{0:T(1024)S(1)}, f32[2048]{0:T(1024)S(1)}, u32[]{:S(2)}, u32[]{:S(2)}) collective-permute-start(f32[2048]{0:T(1024)S(1)} %add.104), channel_id=1, source_target_pairs={{0,16},{4,20},{8,24},{12,28},{16,0},{20,4},{24,8},{28,12},{1,17},{... | collective-permute-start | bytes 24584 | tf_op jit(solution)/shard_map/ppermute | solution.py:411
  398.1 11.9 %collective-permute-start.11 = (f32[2048]{0:T(1024)S(1)}, f32[2048]{0:T(1024)S(1)}, u32[]{:S(2)}, u32[]{:S(2)}) collective-permute-start(f32[2048]{0:T(1024)S(1)} %add.96), channel_id=1, source_target_pairs={{0,2},{1,3},{2,0},{3,1},{4,6},{5,7},{6,4},{7,5},{8,10},{9,11},{10,... | collective-permute-start | bytes 24584 | tf_op jit(solution)/shard_map/ppermute | solution.py:411
  402.4 7.6 %copy-start.35 = (f32[2048]{0:T(1024)S(1)}, f32[2048]{0:T(1024)}, u32[]{:S(2)}) copy-start(f32[2048]{0:T(1024)} %param.28) | copy-start | bytes 24580
  402.4 7.6 %copy-start.36 = (f32[2048]{0:T(1024)S(1)}, f32[2048]{0:T(1024)}, u32[]{:S(2)}) copy-start(f32[2048]{0:T(1024)} %param.29) | copy-start | bytes 24580
  402.4 8.3 %copy-start.1 = (bf16[1,256,2048]{2,1,0:T(8,128)(2,1)S(1)}, bf16[1,256,2048]{2,1,0:T(8,128)(2,1)}, u32[]{:S(2)}) copy-start(bf16[1,256,2048]{2,1,0:T(8,128)(2,1)} %param.21) | copy-start | bytes 3145732
  419.1 7.3 %copy-start.4 = (bf16[2,512,768]{2,1,0:T(8,128)(2,1)S(1)}, bf16[2,512,768]{2,1,0:T(8,128)(2,1)}, u32[]{:S(2)}) copy-start(bf16[2,512,768]{2,1,0:T(8,128)(2,1)} %copy-done.3) | copy-start | bytes 4718596
  (20 other events, 28.6 us)
Sparse Core Ops, SparseCore 0:
  12.0 36.1 reduce-scatter.4
  52.0 38.4 reduce-scatter.6
  257.3 29.2 all-gather.5
  340.8 22.6 all-gather.7
Sparse Core Ops, SparseCore 1:
  55.4 104.9 all-gather.3

commit v4 on v3

--- a/solution.py
+++ b/solution.py
@@ -68,23 +68,27 @@
     return part if total is None else total + part
 
 
+def assemble(starts, cands, whole, sems):
+    def copy_of(at):
+        rows = cands[at].shape[0]
+        to = pl.ds(pl.multiple_of(starts[at], rows), rows)
+        return pltpu.make_async_copy(cands[at], whole.at[to], sems.at[at])
+
+    for at in range(len(cands)):
+        @pl.when(starts[at] >= 0)
+        def _(at=at):
+            copy_of(at).start()
+    for at in range(len(cands)):
+        @pl.when(starts[at] >= 0)
+        def _(at=at):
+            copy_of(at).wait()
+
+
 def forward_kernel(n_cand, starts, normed, cot, tab, *refs):
     cands = refs[:n_cand]
     q_ref, k_ref, v_ref, top_ref, low_ref, go_ref, w_ref, sems = refs[n_cand:]
 
-    def copy_of(at):
-        rows = cands[at].shape[0]
-        to = pl.ds(pl.multiple_of(starts[at], rows), rows)
-        return pltpu.make_async_copy(cands[at], w_ref.at[to], sems.at[at])
-
-    for at in range(n_cand):
-        @pl.when(starts[at] >= 0)
-        def _(at=at):
-            copy_of(at).start()
-    for at in range(n_cand):
-        @pl.when(starts[at] >= 0)
-        def _(at=at):
-            copy_of(at).wait()
+    assemble(starts, cands, w_ref, sems)
     length = normed.shape[0]
     step = length // 2
     x = normed[...]
@@ -125,7 +129,10 @@
             go_ref[cut, :] = mm(att, cot[...]).astype(BF16)
 
 
-def backward_kernel(normed_t, w_ref, cot, wo, tab, q_ref, k_ref, v_ref, top_ref, low_ref, gain_in, g_ref, gain_ref):
+def backward_kernel(n_cand, starts, normed_t, w_ref, cot, tab, q_ref, k_ref, v_ref, top_ref, low_ref, gain_in, *refs):
+    cands = refs[:n_cand]
+    g_ref, gain_ref, wo, sems = refs[n_cand:]
+    assemble(starts, cands, wo, sems)
     length = cot.shape[0]
     step = length // 2
     dm = []
@@ -187,7 +194,7 @@
         gain_ref[:, cut] = gain_in[:, cut] + mm(ones, high, NT) + mm(ones, low, NT)
 
 
-def vmem_call(kernel, outs, n_hbm=0, hbm_at=0, smem=0, scratch=(), other=None):
+def vmem_call(kernel, outs, n_hbm=0, hbm_at=0, smem=0, scratch=()):
     whole = pl.BlockSpec(memory_space=pltpu.VMEM)
 
     def call(*args):
@@ -196,8 +203,6 @@
             specs[i] = pl.BlockSpec(memory_space=pltpu.SMEM)
         for i in range(hbm_at, hbm_at + n_hbm):
             specs[i] = pl.BlockSpec(memory_space=pl.ANY)
-        for i, spec in (other or {}).items():
-            specs[i] = spec
         return pl.pallas_call(
             kernel,
             out_shape=outs,
@@ -236,14 +241,21 @@
     return call(starts, normed, cot, tab, *cands)
 
 
-def backward(pair, normed_t, w, cot, wo, tab, saved, gain_in):
+def backward(starts, normed_t, w, cot, tab, saved, gain_in, cands):
     width = w.shape[0]
-    rows = pl.BlockSpec((QP, width), lambda i: (pair, 0))
     outs = (
         jax.ShapeDtypeStruct((width, CP), BF16),
         jax.ShapeDtypeStruct((8, width), F32),
     )
-    return vmem_call(backward_kernel, outs, other={3: rows})(normed_t, w, cot, wo, tab, *saved, gain_in)
+    call = vmem_call(
+        functools.partial(backward_kernel, len(cands)),
+        outs,
+        n_hbm=len(cands),
+        hbm_at=6 + len(saved),
+        smem=1,
+        scratch=[pltpu.VMEM((QP, width), BF16), pltpu.SemaphoreType.DMA((len(cands),))],
+    )
+    return call(starts, normed_t, w, cot, tab, *saved, gain_in, *cands)
 
 
 def norm_kernel(x_ref, gain_ref, out_ref, out_t_ref):
@@ -352,57 +364,68 @@
     return lax.optimization_barrier((x, *others))[0]
 
 
-def line_gather(x, me, before=None):
-    middle = jnp.logical_or(me == 1, me == 2)
-    near = jnp.where(me < 2, 2, 1)
-    far = jnp.where(me < 2, 3, 0)
-    pair = lax.ppermute(x, "fsdp", [(0, 1), (1, 0), (2, 3), (3, 2)])
-    mid_near = lax.ppermute(x, "fsdp", [(1, 2), (2, 1)])
-    waits = (pair, mid_near) if before is None else (pair, mid_near, before)
-    pair, mid_near = lax.optimization_barrier(waits)[:2]
-    mid_far = lax.ppermute(pair, "fsdp", [(1, 2), (2, 1)])
-    end_near = lax.ppermute(mid_near, "fsdp", [(1, 0), (2, 3)])
-    end_far = lax.ppermute(mid_far, "fsdp", [(1, 0), (2, 3)])
-    blocks = (x, pair, mid_near, mid_far, end_near, end_far)
-    places = (
-        me,
-        me ^ 1,
-        jnp.where(middle, near, -1),
-        jnp.where(middle, far, -1),
-        jnp.where(middle, -1, near),
-        jnp.where(middle, -1, far),
-    )
-    return blocks, places
-
-
-def gather(x, n, me, before=None):
-    if n == 4:
-        blocks, places = line_gather(x, me, before)
-    else:
-        blocks, places = (lax.all_gather(x, "fsdp", axis=0, tiled=True),), (me * 0,)
-    starts = jnp.stack([p * x.shape[0] for p in places]).astype(jnp.int32)
-    return blocks, starts
-
-
-def scatter(x, n, me):
-    rows = x.shape[0] // n
-    blocks = x.reshape(n, rows, x.shape[1])
-    if n != 4:
-        return jnp.zeros((1,), jnp.int32), (lax.psum_scatter(x, "fsdp", scatter_dimension=0, tiled=True)[None],)
+PAIR_SWAP = [(0, 1), (1, 0), (2, 3), (3, 2)]
+MID_SWAP = [(1, 2), (2, 1)]
+INWARD = [(0, 1), (3, 2)]
+OUTWARD = [(1, 0), (2, 3)]
+
+
+def send(x, pairs):
+    return lax.ppermute(x, "fsdp", pairs)
+
+
+def table(me, *values):
+    return jnp.array(values, jnp.int32)[me]
+
+
+def plus(a, b):
+    return (a.astype(F32) + b.astype(F32)).astype(BF16)
+
+
+def block(x, at):
+    return lax.dynamic_slice_in_dim(x, at, 1, 0)
+
+
+def starts_of(rows, places):
+    return jnp.stack([jnp.where(p < 0, -1, p * rows) for p in places]).astype(jnp.int32)
+
+
+def line_starts(me, rows):
+    return starts_of(
+        rows,
+        (
+            me,
+            me ^ 1,
+            table(me, -1, 2, 1, -1),
+            table(me, -1, 3, 0, -1),
+            table(me, 2, -1, -1, 1),
+            table(me, 3, -1, -1, 0),
+        ),
+    )
+
+
+def scatter_merged(x, me):
+    blocks = x.reshape(4, x.shape[0] // 4, x.shape[1])
 
     def two(at):
         return lax.dynamic_slice_in_dim(blocks, at, 2, 0)
 
-    def plus(a, b):
-        return (a.astype(F32) + b.astype(F32)).astype(BF16)
-
-    inward = lax.ppermute(two(jnp.where(me == 0, 2, 0)), "fsdp", [(3, 2), (0, 1)])
-    across = lax.ppermute(plus(two(jnp.where(me == 1, 2, 0)), inward), "fsdp", [(2, 1), (1, 2)])
-    passed = lax.dynamic_index_in_dim(across, jnp.where(me == 1, 0, 1), 0, keepdims=True)
-    other = lax.dynamic_index_in_dim(blocks, me ^ 1, 0, keepdims=True)
-    outward = lax.ppermute(plus(other, passed), "fsdp", [(0, 1), (1, 0), (2, 3), (3, 2)])
-    idx = jnp.stack([me, jnp.where(me == 1, 1, 0), me * 0]).astype(jnp.int32)
+    inward = send(two(table(me, 2, 0, 0, 0)), INWARD)
+    across = send(plus(two(table(me, 0, 2, 0, 0)), inward), MID_SWAP)
+    outward = send(plus(block(blocks, me ^ 1), block(across, table(me, 0, 0, 1, 0))), PAIR_SWAP)
+    idx = jnp.stack([me, table(me, 0, 1, 0, 0), me * 0]).astype(jnp.int32)
     return idx, (blocks, across, outward)
+
+
+def scatter_single(x, me, before):
+    blocks = x.reshape(4, x.shape[0] // 4, x.shape[1])
+    far_in = send(block(blocks, 3 - me), INWARD)
+    near_in = send(block(blocks, table(me, 2, 0, 0, 1)), INWARD)
+    far = send(plus(block(blocks, table(me, 0, 3, 0, 0)), far_in), MID_SWAP)
+    near = send(plus(block(blocks, 3 - me), near_in), MID_SWAP)
+    outward = send(after(plus(block(blocks, me ^ 1), far), *before), PAIR_SWAP)
+    idx = jnp.stack([me, me * 0, me * 0]).astype(jnp.int32)
+    return idx, (blocks, near, outward)
 
 
 def all_sum(x, axis, n):
@@ -443,9 +466,8 @@
     qw = HEADS * HEAD_DIM
     kw = KV_HEADS * HEAD_DIM
 
-    got = []
-    for pair in range(PAIRS):
-        own = jnp.concatenate(
+    packed = [
+        jnp.concatenate(
             [
                 w_qkv[:, pair * QP : (pair + 1) * QP],
                 w_qkv[:, qw + pair * 128 : qw + (pair + 1) * 128],
@@ -453,13 +475,35 @@
             ],
             axis=1,
         )
-        if got:
-            own = after(own, *got[0][0][3:5])
-        got.append(gather(own, n, me, got[0][0][-1] if got else None))
-    all_out = lax.all_gather(after(w_out, *got[0][0][3:5]), "fsdp", axis=0, tiled=True)
-
-    normed, normed_t = norm(tokens, gain[None])
-    tab = rope_tables(length)
+        for pair in range(PAIRS)
+    ]
+    w_rows = w_qkv.shape[0]
+    o_rows = w_out.shape[0]
+    line = n == 4
+
+    if line:
+        x0, x1 = packed
+        pair0 = send(x0, PAIR_SWAP)
+        near0 = send(x0, MID_SWAP)
+        normed, normed_t = norm(tokens, gain[None])
+        tab = rope_tables(length)
+        pair0, near0, normed, normed_t, tab = lax.optimization_barrier((pair0, near0, normed, normed_t, tab))
+        far0 = send(pair0, MID_SWAP)
+        end_near0 = send(near0, OUTWARD)
+        o_in = send(after(w_out, pair0, near0), INWARD)
+        far0, end_near0 = lax.optimization_barrier((far0, end_near0))
+        end_far0 = send(far0, OUTWARD)
+        o_near = send(after(w_out, far0), MID_SWAP)
+        o_far = send(after(o_in, far0), MID_SWAP)
+        o_one = send(jnp.where(me == 1, w_out, o_near), OUTWARD)
+        q_cands = [(x0, pair0, near0, far0, end_near0, end_far0)]
+        q_starts = line_starts(me, w_rows)
+    else:
+        normed, normed_t = norm(tokens, gain[None])
+        tab = rope_tables(length)
+        q_cands = [(lax.all_gather(x, "fsdp", axis=0, tiled=True),) for x in packed]
+        q_starts = starts_of(0, (me,))
+        all_out = lax.all_gather(w_out, "fsdp", axis=0, tiled=True)
 
     scale = 1.0 / islands
     qkv_total = lax.psum_scatter(w_qkv, "island", scatter_dimension=1, tiled=True).astype(F32)
@@ -468,36 +512,93 @@
     gain_pair = nesterov(gain_global, gain_momentum, gain_total * scale)
     qkv_pair = nesterov(qkv_global, qkv_momentum, qkv_total * scale)
     out_pair = nesterov(out_global, out_momentum, out_total * scale)
-    saved = []
-    g_out = []
-    for pair in range(PAIRS):
-        blocks, starts = got[pair]
-        if pair:
-            starts = after(starts, qkv_pair[0], qkv_pair[1], out_pair[0], out_pair[1])
-        *kept, grad, w_pair = forward(starts, normed, cotangent, tab, blocks)
-        saved.append((kept, w_pair))
-        g_out.append(grad)
-    out_grad = scatter(jnp.concatenate(g_out, axis=0), n, me)
-
-    gain_sum = after(jnp.zeros((8, width), F32), *g_out)
-    qkv_grad = []
-    for pair in range(PAIRS):
-        kept, w_pair = saved[pair]
-        grad, gain_sum = backward(pair, normed_t, w_pair, cotangent, all_out, tab, kept, gain_sum)
-        qkv_grad.append(scatter(grad, n, me))
+    qkv_whole = lax.all_gather(qkv_pair[0].astype(BF16), "island", axis=1, tiled=True)
+    out_whole = lax.all_gather(out_pair[0].astype(BF16), "island", axis=1, tiled=True)
+
+    *kept0, go0, w0 = forward(q_starts, normed, cotangent, tab, q_cands[0])
+    gain_sum = jnp.zeros((8, width), F32)
+    if line:
+        go0 = go0.reshape(2, o_rows, width)
+        o_two = send(after(o_far, go0), OUTWARD)
+        go_in0 = send(go0, [(3, 2)])
+        synced = (qkv_pair[0], qkv_pair[1], out_pair[0], out_pair[1])
+        x1 = after(x1, o_two)
+        pair1 = send(x1, PAIR_SWAP)
+        near1 = send(x1, MID_SWAP)
+        o_cands = (w_out, o_in, o_near, o_far, o_one, o_two)
+        places = (
+            table(me, 0, 1, -1, -1),
+            table(me, -1, 0, -1, -1),
+            table(me, -1, -1, 1, -1),
+            table(me, -1, -1, 0, -1),
+            table(me, 1, -1, -1, 1),
+            table(me, -1, -1, -1, 0),
+        )
+        o_starts = starts_of(o_rows, places)
+        g0, gain_sum = backward(o_starts, normed_t, w0, cotangent, tab, kept0, gain_sum, o_cands)
+        pair1, near1 = lax.optimization_barrier((pair1, near1, g0))[:2]
+        far1 = send(pair1, MID_SWAP)
+        end_near1 = send(near1, OUTWARD)
+        grad0 = scatter_merged(g0, me)
+        go_over0 = send(plus(go0, go_in0), [(2, 1)])
+        far1, end_near1 = lax.optimization_barrier((far1, end_near1))
+        end_far1 = send(far1, OUTWARD)
+        o_three = send(after(jnp.where(me == 2, w_out, o_near), end_far1), OUTWARD)
+        *kept1, go1, w1 = forward(
+            after(q_starts, *synced), normed, cotangent, tab, (x1, pair1, near1, far1, end_near1, end_far1)
+        )
+        go1 = go1.reshape(2, o_rows, width)
+        go_in1_far = send(go1[1:], [(0, 1)])
+        go_in1_near = send(go1[:1], [(0, 1)])
+        o_cands = (w_out, o_in, o_near, o_far, o_three, o_two)
+        places = (
+            table(me, -1, -1, 0, 1),
+            table(me, -1, -1, 1, -1),
+            table(me, -1, 0, -1, -1),
+            table(me, -1, 1, -1, -1),
+            table(me, 0, -1, -1, 0),
+            table(me, 1, -1, -1, -1),
+        )
+        g1, gain_sum = backward(
+            starts_of(o_rows, places), normed_t, w1, cotangent, tab, kept1, after(gain_sum, go1), o_cands
+        )
+    else:
+        *kept1, go1, w1 = forward(q_starts, normed, cotangent, tab, q_cands[1])
+        go = jnp.concatenate([go0, go1], axis=0)
+        none = jnp.zeros((1,), jnp.int32)
+        out_grad = (none, (lax.psum_scatter(go, "fsdp", scatter_dimension=0, tiled=True)[None],))
+        grads = []
+        for pair, kept, w in ((0, kept0, w0), (1, kept1, w1)):
+            g, gain_sum = backward(
+                q_starts, normed_t, w, cotangent, tab, kept, gain_sum, (all_out[pair * QP : (pair + 1) * QP],)
+            )
+            grads.append((none, (lax.psum_scatter(g, "fsdp", scatter_dimension=0, tiled=True)[None],)))
+
+    def adam_pair(pair, grad, held):
+        return qkv_adam(pair, grad, w_qkv, qkv_first[0], qkv_second[0], qkv_whole, held)
+
+    if line:
+        qkv_state = adam_pair(0, grad0, ())
+        go_over1_far = send(plus(go1[1:], go_in1_far), [(1, 2)])
+        go_over1_near = send(plus(go1[:1], go_in1_near), [(1, 2)])
+        low = me < 2
+        mine = jnp.where(low, go0, go1)
+        over1 = jnp.concatenate([go_over1_near, go_over1_far], axis=0)
+        over = jnp.where(low, go_over0, over1)
+        odd = me & 1
+        go_out = send(plus(block(mine, 1 - odd), block(over, 1 - odd)), PAIR_SWAP)
+        out_grad = (jnp.stack([odd, odd, odd * 0]).astype(jnp.int32), (mine, over, go_out))
+        out_state = out_adam(out_grad, w_out, out_first[0], out_second[0], out_whole)
+        grad1 = scatter_single(g1, me, (qkv_state[0],))
+    else:
+        out_state = out_adam(out_grad, w_out, out_first[0], out_second[0], out_whole)
+        qkv_state = adam_pair(0, grads[0], ())
+        grad1 = grads[1]
+    qkv_state = adam_pair(1, grad1, qkv_state)
 
     gain_grad = all_sum(gain_sum[0], "fsdp", n) / gain
     gain_step, gain_first_next, gain_second_next = adam(gain, gain_grad, gain_first[0], gain_second[0], 0.0)
 
-    qkv_whole = lax.all_gather(after(qkv_pair[0].astype(BF16), g_out[1]), "island", axis=1, tiled=True)
-    out_whole = lax.all_gather(after(out_pair[0].astype(BF16), g_out[1]), "island", axis=1, tiled=True)
-
-    out_state = out_adam(out_grad, w_out, out_first[0], out_second[0], out_whole)
-    qkv_state = ()
-    for pair in range(PAIRS):
-        qkv_state = qkv_adam(
-            pair, qkv_grad[pair], w_qkv, qkv_first[0], qkv_second[0], qkv_whole, qkv_state
-        )
     gain_next = MIXING * gain_step + (1.0 - MIXING) * gain_pair[0]
     return (
         gain_next[None],

time: 448 us -> 445 us (level)
  waiting for transfers between devices: 215 us -> 131 us
  starting transfers between devices: 42.5 us -> 79.3 us
  between operations: 16 us -> 42.8 us
  local copies, waits for them, and re-layouts: 40.4 us -> 49.7 us
  other arithmetic: 27.9 us -> 33.5 us
    ppermute x19 -> x31, waiting for transfers between devices: 210 us -> 118 us  [send(): return lax.ppermute(x, 'fsdp', pairs)]
    ppermute x19 -> x31, starting transfers between devices: 38.6 us -> 76.8 us  [send(): return lax.ppermute(x, 'fsdp', pairs)]
    dynamic_slice x0 -> x21, local copies, waits for them, and re-layouts: none -> 14.3 us  [the longest x20 13.1 us: table(): return jnp.array(values, jnp.int32)[me]]
    ppermute x5, waiting for transfers between devices: 4.11 us -> 12.9 us  [all_sum(): x = x + lax.ppermute(x, axis, [(i, i ^ k) for i in range(n)])]
    unnamed x84 -> x102, local copies, waits for them, and re-layouts: 27.1 us -> 19.9 us
    select_n x0 -> x3, other arithmetic: none -> 6.77 us  [the longest x1 3.14 us: shards(): o_three = send(after(jnp.where(me == 2, w_out, o_near), end_far1), OUTWARD)]
    convert_element_type x0 -> x2, local copies, waits for them, and re-layouts: none -> 5.12 us  [the longest x1 3.37 us: plus(): return (a.astype(F32) + b.astype(F32)).astype(BF16)]
    convert_element_type x6 -> x8, other arithmetic: 17.3 us -> 19.5 us  [plus(): return (a.astype(F32) + b.astype(F32)).astype(BF16)]
  transfers between devices with their start and end apart: 29 -> 40, of which waited for: 13 -> 18; matrix products, arithmetic and copies ran while one was open for 12% -> 16% of each run, Pallas kernels for 21% -> 22%
where the time goes in v4:
time: 445 us; the launch traced here: 437 us
  waiting for transfers between devices  131 us (29%)
  Pallas kernels  102 us (23%)
  starting transfers between devices  79.3 us (18%)
  local copies, waits for them, and re-layouts  49.7 us (11%)
  between operations  42.8 us (10%)
  other arithmetic  33.5 us (8%)
    ppermute x31, waiting for transfers between devices, send(): return lax.ppermute(x, 'fsdp', pairs)  118 us
    pallas_call x5, Pallas kernels, call(): pl.pallas_call(kernel, out_shape=outs, grid=(1,), in_specs=specs, out_spe...  79.7 us
    ppermute x31, starting transfers between devices, send(): return lax.ppermute(x, 'fsdp', pairs)  76.8 us
    pallas_call x3, Pallas kernels, adam_call(): pl.pallas_call(functools.partial(adam_kernel, n_parts, len(held)), out_sh...  21.9 us
    unnamed x102, local copies, waits for them, and re-layouts  19.9 us
    convert_element_type x8, other arithmetic, plus(): return (a.astype(F32) + b.astype(F32)).astype(BF16)  19.5 us
    dynamic_slice x20, local copies, waits for them, and re-layouts, table(): return jnp.array(values, jnp.int32)[me]  13.1 us
    ppermute x5, waiting for transfers between devices, all_sum(): x = x + lax.ppermute(x, axis, [(i, i ^ k) for i in range(n)])  12.9 us
  transfers between devices with their start and end apart: 40, of which 18 were waited for; matrix products, arithmetic and copies ran while one was open for 16% of the time, Pallas kernels for 22%

profile of v4, /device:TPU:22, one launch (start us, length us, event | category | flops | bytes accessed | tf_op | source)
XLA Modules:
  0.0 437.5 jit_solution(11321604584737018904)
XLA Ops:
  9.0 2.1 fusion.7
  14.8 4.1 shard_map.478
  20.8 9.8 %collective-permute-done.refs_1_ = bf16[512,768]{1,0:T(8,128)(2,1)S(1)} collective-permute-done((bf16[512,768]{1,0:T(8,128)(2,1)S(1)}, bf16[512,768]{1,0:T(8,128)(2,1)S(1)}, u32[]{:S(2)}, u32[]{:S(2)}) %collective-permute-start) | collective-permute-done | bytes 786464 | tf_op jit(solution)/shard_map/ppermute | solution.py:374
  30.5 3.2 collective-permute-done.1.refs_2_
  35.0 2.2 collective-permute-start.3
  37.2 4.9 %collective-permute-start.4 = (bf16[512,768]{1,0:T(8,128)(2,1)S(1)}, bf16[512,768]{1,0:T(8,128)(2,1)S(1)}, u32[]{:S(2)}, u32[]{:S(2)}) collective-permute-start(bf16[512,768]{1,0:T(8,128)(2,1)S(1)} %collective-permute-done.1.refs_2_), channel_id=1, source_target_pairs={{1,0},{2,3},{5,4},{6,7},{9,8},{10,11},{13,12},{14,15},{17,16},{18,... | collective-permute-start | bytes 2359304 | tf_op jit(solution)/shard_map/ppermute | solution.py:374
  42.1 13.0 %collective-permute-done.3.refs_3_ = bf16[512,768]{1,0:T(8,128)(2,1)} collective-permute-done((bf16[512,768]{1,0:T(8,128)(2,1)S(1)}, bf16[512,768]{1,0:T(8,128)(2,1)}, u32[]{:S(2)}, u32[]{:S(2)}) %collective-permute-start.3) | collective-permute-done | bytes 786464 | tf_op jit(solution)/shard_map/ppermute | solution.py:374
  55.1 2.3 collective-permute-done.4.refs_4_
  59.6 2.5 collective-permute-start.5
  62.2 3.3 collective-permute-start.10
  65.5 2.2 collective-permute-start.6
  76.7 4.7 %collective-permute-done.6.refs_5_ = bf16[512,768]{1,0:T(8,128)(2,1)} collective-permute-done((bf16[512,768]{1,0:T(8,128)(2,1)}, bf16[512,768]{1,0:T(8,128)(2,1)}, u32[]{:S(2)}, u32[]{:S(2)}) %collective-permute-start.6) | collective-permute-done | bytes 786464 | tf_op jit(solution)/shard_map/ppermute | solution.py:374
  81.5 19.3 %shard_map.479 = (bf16[512,512]{1,0:T(8,128)(2,1)S(1)}, bf16[512,128]{1,0:T(8,128)(2,1)S(1)}, bf16[512,128]{1,0:T(8,128)(2,1)S(1)}, bf16[8,256,256]{2,1,0:T(8,12...) custom-call(s32[6]{0:T(128)S(1)} %stack.67.starts, ...), custom_call_target="tpu_custom_call" | custom-call | flops 1 | bytes 1 | tf_op jit(solution)/shard_map/pallas_call | solution.py:206
  101.6 5.6 %collective-permute-start.7 = (bf16[256,2048]{1,0:T(8,128)(2,1)}, bf16[256,2048]{1,0:T(8,128)(2,1)}, u32[]{:S(2)}, u32[]{:S(2)}) collective-permute-start(bf16[256,2048]{1,0:T(8,128)(2,1)} %collective-permute-done.5.refs_3_), channel_id=1, source_target_pairs={{1,0},{2,3},{5,4},{6,7},{9,8},{10,11},{13,12},{14,15},{17,16},{18,... | collective-permute-start | bytes 3145736 | tf_op jit(solution)/shard_map/ppermute | solution.py:374
  107.1 3.1 broadcast_select_fusion.1
  110.3 2.3 collective-permute-start.11
  112.7 17.3 %collective-permute-done.7.refs_5_ = bf16[256,2048]{1,0:T(8,128)(2,1)} collective-permute-done((bf16[256,2048]{1,0:T(8,128)(2,1)}, bf16[256,2048]{1,0:T(8,128)(2,1)}, u32[]{:S(2)}, u32[]{:S(2)}) %collective-permute-start.7) | collective-permute-done | bytes 1048608 | tf_op jit(solution)/shard_map/ppermute | solution.py:374
  130.0 2.5 collective-permute-start.8
  132.5 2.8 collective-permute-start.9
  154.8 19.0 %shard_map.480 = (bf16[2048,768]{1,0:T(8,128)(2,1)}, f32[8,2048]{1,0:T(8,128)S(1)}) custom-call(s32[6]{0:T(128)S(1)} %stack.68.starts, bf16[2048,512]{1,0:T(8,128)(2,1)} %get-tuple-element.66.normed_t, bf16[2048,768]{1,0:T(8,128)(2,1)} %get-tuple-element.79.w_ref, bf16[512,2048]{1,0:T(8,128)(2,1)} %cot.7, f32[3,512,128]{2,1,0:T(8,128)S(1)} %pad_maximum_fusion.1.tab, ...), custom_call_target="tpu_custom_call" | custom-call | flops 1 | bytes 1 | tf_op jit(solution)/shard_map/pallas_call | solution.py:206
  173.9 2.9 collective-permute-start.12
  176.8 4.0 collective-permute-start.13
  180.8 2.7 constant_dynamic-slice_fusion
  184.7 3.3 collective-permute-done.12.refs_3_
  188.1 6.6 %collective-permute-done.13.refs_4_ = bf16[512,768]{1,0:T(8,128)(2,1)} collective-permute-done((bf16[512,768]{1,0:T(8,128)(2,1)}, bf16[512,768]{1,0:T(8,128)(2,1)}, u32[]{:S(2)}, u32[]{:S(2)}) %collective-permute-start.13) | collective-permute-done | bytes 786464 | tf_op jit(solution)/shard_map/ppermute | solution.py:374
  194.7 5.3 %collective-permute-start.14 = (bf16[512,768]{1,0:T(8,128)(2,1)}, bf16[512,768]{1,0:T(8,128)(2,1)}, u32[]{:S(2)}, u32[]{:S(2)}) collective-permute-start(bf16[512,768]{1,0:T(8,128)(2,1)} %collective-permute-done.12.refs_3_), channel_id=1, source_target_pairs={{1,0},{2,3},{5,4},{6,7},{9,8},{10,11},{13,12},{14,15},{17,16},{18,... | collective-permute-start | bytes 2359304 | tf_op jit(solution)/shard_map/ppermute | solution.py:374
  210.8 4.0 collective-permute-done.14.refs_5_
  214.8 5.7 %collective-permute-start.15 = (bf16[256,2048]{1,0:T(8,128)(2,1)}, bf16[256,2048]{1,0:T(8,128)(2,1)}, u32[]{:S(2)}, u32[]{:S(2)}) collective-permute-start(bf16[256,2048]{1,0:T(8,128)(2,1)} %get-tuple-element.100), channel_id=1, source_target_pairs={{1,0},{2,3},{5,4},{6,7},{9,8},{10,11},{13,12},{14,15},{17,16},{18,... | collective-permute-start | bytes 3145736 | tf_op jit(solution)/shard_map/ppermute | solution.py:374
  220.5 2.5 collective-permute-done.25
  223.0 3.4 add_convert_fusion.1
  231.4 18.5 %shard_map.481 = (bf16[512,512]{1,0:T(8,128)(2,1)S(1)}, bf16[512,128]{1,0:T(8,128)(2,1)S(1)}, bf16[512,128]{1,0:T(8,128)(2,1)S(1)}, bf16[8,256,256]{2,1,0:T(8,12...) custom-call(s32[6]{0:T(128)S(1)} %stack.67.starts, ...), custom_call_target="tpu_custom_call" | custom-call | flops 1 | bytes 1 | tf_op jit(solution)/shard_map/pallas_call | solution.py:206
  250.6 3.4 slice_bitcast_fusion.1
  273.3 18.8 %shard_map.482 = (bf16[2048,768]{1,0:T(8,128)(2,1)}, f32[8,2048]{1,0:T(8,128)S(1)}) custom-call(s32[6]{0:T(128)S(1)} %stack.28.starts, bf16[2048,512]{1,0:T(8,128)(2,1)} %get-tuple-element.66.normed_t, bf16[2048,768]{1,0:T(8,128)(2,1)} %get-tuple-element.91.w_ref, bf16[512,2048]{1,0:T(8,128)(2,1)} %cot.7, f32[3,512,128]{2,1,0:T(8,128)S(1)} %pad_maximum_fusion.1.tab, ...), custom_call_target="tpu_custom_call" | custom-call | flops 1 | bytes 1 | tf_op jit(solution)/shard_map/pallas_call | solution.py:206
  294.6 4.4 %add_convert_fusion = bf16[2,256,2048]{2,1,0:T(8,128)(2,1)} fusion(bf16[2,256,2048]{2,1,0:T(8,128)(2,1)} %collective-permute-done.29, bf16[2,256,2048]{2,1,0:T(8,128)(2,1)} %bitcast.11), kind=kLoop, calls=%fused_computation | loop fusion | flops 4194304 | bytes 6291456 | tf_op jit(solution)/shard_map/convert_element_type | solution.py:382
  299.1 4.9 %collective-permute-start.30 = (bf16[2,256,2048]{2,1,0:T(8,128)(2,1)}, bf16[2,256,2048]{2,1,0:T(8,128)(2,1)}, u32[]{:S(2)}, u32[]{:S(2)}) collective-permute-start(bf16[2,256,2048]{2,1,0:T(8,128)(2,1)} %add_convert_fusion), channel_id=1, source_target_pairs={{2,1},{6,5},{10,9},{14,13},{18,17},{22,21},{26,25},{30,29}} | collective-permute-start | bytes 6291464 | tf_op jit(solution)/shard_map/ppermute | solution.py:374
  304.0 2.4 add_convert_fusion.5
  306.6 3.8 add_convert_fusion.4
  311.7 3.8 collective-permute-done.21
  316.9 2.6 add_convert_fusion.8
  326.0 2.6 copy.66.refs_6_
  333.0 7.5 %shard_map.483 = (bf16[512,1536]{1,0:T(8,128)(2,1)}, f32[512,1536]{1,0:T(8,128)}, f32[512,1536]{1,0:T(8,128)}) custom-call(s32[3]{0:T(128)S(1)} %pad_add_fusion.1.idx_ref, bf16[4,512,768]{2,1,0:T(8,128)(2,1)} %bitcast.62, bf16[2,512,768]{2,1,0:T(8,128)(2,1)} %collective-permute-done.26.refs_1_, bf16[1,512,768]{2,1,0:T(8,128)(2,1)S(1)} %collective-permute-done.27.refs_2_, ...), custom_call_target="tpu_custom_call" | custom-call | flops 20000000 | bytes 14000000 | tf_op jit(solution)/shard_map/pallas_call | solution.py:314
  340.5 8.4 %collective-permute-done.23 = bf16[1,512,768]{2,1,0:T(8,128)(2,1)S(1)} collective-permute-done((bf16[1,512,768]{2,1,0:T(8,128)(2,1)}, bf16[1,512,768]{2,1,0:T(8,128)(2,1)S(1)}, u32[]{:S(2)}, u32[]{:S(2)}) %collective-permute-start.23) | collective-permute-done | bytes 786464 | tf_op jit(solution)/shard_map/ppermute | solution.py:374
  349.1 5.5 %collective-permute-start.22 = (bf16[1,512,768]{2,1,0:T(8,128)(2,1)}, bf16[1,512,768]{2,1,0:T(8,128)(2,1)S(1)}, u32[]{:S(2)}, u32[]{:S(2)}) collective-permute-start(bf16[1,512,768]{2,1,0:T(8,128)(2,1)} %get-tuple-element.148), channel_id=1, source_target_pairs={{1,2},{2,1},{5,6},{6,5},{9,10},{10,9},{13,14},{14,13},{17,18},{18,... | collective-permute-start | bytes 2359304 | tf_op jit(solution)/shard_map/ppermute | solution.py:374
  356.5 5.2 %collective-permute-done.32 = bf16[1,256,2048]{2,1,0:T(8,128)(2,1)} collective-permute-done((bf16[1,256,2048]{2,1,0:T(8,128)(2,1)}, bf16[1,256,2048]{2,1,0:T(8,128)(2,1)}, u32[]{:S(2)}, u32[]{:S(2)}) %collective-permute-start.32) | collective-permute-done | bytes 1048608 | tf_op jit(solution)/shard_map/ppermute | solution.py:374
  365.3 29.7 %collective-permute-done.24 = bf16[1,512,768]{2,1,0:T(8,128)(2,1)S(1)} collective-permute-done((bf16[1,512,768]{2,1,0:T(8,128)(2,1)S(1)}, bf16[1,512,768]{2,1,0:T(8,128)(2,1)S(1)}, u32[]{:S(2)}, u32[]{:S(2)}) %collective-permute-start.24) | collective-permute-done | bytes 786464 | tf_op jit(solution)/shard_map/ppermute | solution.py:374
  401.7 12.9 %collective-permute-done.17 = f32[2048]{0:T(1024)S(1)} collective-permute-done((f32[2048]{0:T(1024)S(1)}, f32[2048]{0:T(1024)S(1)}, u32[]{:S(2)}, u32[]{:S(2)}) %collective-permute-start.17) | collective-permute-done | bytes 8224 | tf_op jit(solution)/shard_map/ppermute | solution.py:434
  416.4 7.2 %shard_map.485 = (bf16[256,2048]{1,0:T(8,128)(2,1)}, f32[256,2048]{1,0:T(8,128)}, f32[256,2048]{1,0:T(8,128)}) custom-call(s32[3]{0:T(128)S(1)} %pad_add_fusion.idx_ref, bf16[2,256,2048]{2,1,0:T(8,128)(2,1)} %copy-done.16, bf16[2,256,2048]{2,1,0:T(8,128)(2,1)} %copy-done.17, bf16[1,256,2048]{2,1,0:T(8,128)(2,1)S(1)} %collective-permute-done.35.refs_2_, ...), custom_call_target="tpu_custom_call" | custom-call | flops 20000000 | bytes 14000000 | tf_op jit(solution)/shard_map/pallas_call | solution.py:314
  423.6 7.1 %shard_map.484 = (bf16[512,1536]{1,0:T(8,128)(2,1)}, f32[512,1536]{1,0:T(8,128)}, f32[512,1536]{1,0:T(8,128)}) custom-call(s32[3]{0:T(128)S(1)} %stack.70.idx_ref, bf16[4,512,768]{2,1,0:T(8,128)(2,1)} %bitcast.65, bf16[1,512,768]{2,1,0:T(8,128)(2,1)S(1)} %collective-permute-done.22.refs_1_, ...), custom_call_target="tpu_custom_call", output_to_operand_aliasing={{0}: (8, {}), {1}: (9, {}), {2}: (10, {})} | custom-call | flops 20000000 | bytes 14000000 | tf_op jit(solution)/shard_map/pallas_call | solution.py:314
  (208 shorter events, 79.5 us)
Async XLA Ops:
  7.2 200.6 %reduce-scatter.5.cloned.1.call-start = ((), (), s32[]{:S(2)}) async-start(), calls=%async_computation.2 | async-start | bytes 1179648 | tf_op jit(solution)/shard_map/reduce_scatter | solution.py:510
  11.2 19.3 %collective-permute-start = (bf16[512,768]{1,0:T(8,128)(2,1)S(1)}, bf16[512,768]{1,0:T(8,128)(2,1)S(1)}, u32[]{:S(2)}, u32[]{:S(2)}) collective-permute-start(bf16[512,768]{1,0:T(8,128)(2,1)S(1)} %pad_maximum_fusion.refs_0_), channel_id=1, source_target_pairs={{0,1},{1,0},{2,3},{3,2},{4,5},{5,4},{6,7},{7,6},{8,9},{9,8},{10,11... | collective-permute-start | bytes 2359304 | tf_op jit(solution)/shard_map/ppermute | solution.py:374
  12.8 20.9 %collective-permute-start.1 = (bf16[512,768]{1,0:T(8,128)(2,1)S(1)}, bf16[512,768]{1,0:T(8,128)(2,1)S(1)}, u32[]{:S(2)}, u32[]{:S(2)}) collective-permute-start(bf16[512,768]{1,0:T(8,128)(2,1)S(1)} %pad_maximum_fusion.refs_0_), channel_id=1, source_target_pairs={{1,2},{2,1},{5,6},{6,5},{9,10},{10,9},{13,14},{14,13},{17,18},{18,... | collective-permute-start | bytes 2359304 | tf_op jit(solution)/shard_map/ppermute | solution.py:374
  20.2 52.7 %copy-start.47 = (s32[4]{0:T(128)S(1)}, s32[4]{0:T(128)}, u32[]{:S(2)}) copy-start(s32[4]{0:T(128)} %constant.157.clone) | copy-start | bytes 52
  20.2 54.6 %copy-start.46 = (s32[4]{0:T(128)S(1)}, s32[4]{0:T(128)}, u32[]{:S(2)}) copy-start(s32[4]{0:T(128)} %constant.158.clone) | copy-start | bytes 52
  33.7 25.9 %collective-permute-start.2 = (bf16[256,2048]{1,0:T(8,128)(2,1)}, bf16[256,2048]{1,0:T(8,128)(2,1)}, u32[]{:S(2)}, u32[]{:S(2)}) collective-permute-start(bf16[256,2048]{1,0:T(8,128)(2,1)} %bitcast.10.refs_0_.refs_3_), channel_id=1, source_target_pairs={{0,1},{3,2},{4,5},{7,6},{8,9},{11,10},{12,13},{15,14},{16,17},{19,... | collective-permute-start | bytes 3145736 | tf_op jit(solution)/shard_map/ppermute | solution.py:374
  35.0 20.1 %collective-permute-start.3 = (bf16[512,768]{1,0:T(8,128)(2,1)S(1)}, bf16[512,768]{1,0:T(8,128)(2,1)}, u32[]{:S(2)}, u32[]{:S(2)}) collective-permute-start(bf16[512,768]{1,0:T(8,128)(2,1)S(1)} %collective-permute-done.refs_1_), channel_id=1, source_target_pairs={{1,2},{2,1},{5,6},{6,5},{9,10},{10,9},{13,14},{14,13},{17,18},{18,... | collective-permute-start | bytes 2359304 | tf_op jit(solution)/shard_map/ppermute | solution.py:374
  37.2 20.2 %collective-permute-start.4 = (bf16[512,768]{1,0:T(8,128)(2,1)S(1)}, bf16[512,768]{1,0:T(8,128)(2,1)S(1)}, u32[]{:S(2)}, u32[]{:S(2)}) collective-permute-start(bf16[512,768]{1,0:T(8,128)(2,1)S(1)} %collective-permute-done.1.refs_2_), channel_id=1, source_target_pairs={{1,0},{2,3},{5,4},{6,7},{9,8},{10,11},{13,12},{14,15},{17,16},{18,... | collective-permute-start | bytes 2359304 | tf_op jit(solution)/shard_map/ppermute | solution.py:374
  59.6 41.9 %collective-permute-start.5 = (bf16[256,2048]{1,0:T(8,128)(2,1)}, bf16[256,2048]{1,0:T(8,128)(2,1)}, u32[]{:S(2)}, u32[]{:S(2)}) collective-permute-start(bf16[256,2048]{1,0:T(8,128)(2,1)} %collective-permute-done.2.refs_1_), channel_id=1, source_target_pairs={{1,2},{2,1},{5,6},{6,5},{9,10},{10,9},{13,14},{14,13},{17,18},{18,... | collective-permute-start | bytes 3145736 | tf_op jit(solution)/shard_map/ppermute | solution.py:374
  62.2 45.0 %collective-permute-start.10 = (bf16[256,2048]{1,0:T(8,128)(2,1)}, bf16[256,2048]{1,0:T(8,128)(2,1)}, u32[]{:S(2)}, u32[]{:S(2)}) collective-permute-start(bf16[256,2048]{1,0:T(8,128)(2,1)} %bitcast.10.refs_0_.refs_3_), channel_id=1, source_target_pairs={{1,2},{2,1},{5,6},{6,5},{9,10},{10,9},{13,14},{14,13},{17,18},{18,... | collective-permute-start | bytes 3145736 | tf_op jit(solution)/shard_map/ppermute | solution.py:374
  65.5 16.0 %collective-permute-start.6 = (bf16[512,768]{1,0:T(8,128)(2,1)}, bf16[512,768]{1,0:T(8,128)(2,1)}, u32[]{:S(2)}, u32[]{:S(2)}) collective-permute-start(bf16[512,768]{1,0:T(8,128)(2,1)} %collective-permute-done.3.refs_3_), channel_id=1, source_target_pairs={{1,0},{2,3},{5,4},{6,7},{9,8},{10,11},{13,12},{14,15},{17,16},{18,... | collective-permute-start | bytes 2359304 | tf_op jit(solution)/shard_map/ppermute | solution.py:374
  67.7 142.0 %reduce-scatter.7.cloned.1.call-start = ((), (), s32[]{:S(2)}) async-start(), calls=%async_computation.5 | async-start | bytes 1769472
  101.6 28.5 %collective-permute-start.7 = (bf16[256,2048]{1,0:T(8,128)(2,1)}, bf16[256,2048]{1,0:T(8,128)(2,1)}, u32[]{:S(2)}, u32[]{:S(2)}) collective-permute-start(bf16[256,2048]{1,0:T(8,128)(2,1)} %collective-permute-done.5.refs_3_), channel_id=1, source_target_pairs={{1,0},{2,3},{5,4},{6,7},{9,8},{10,11},{13,12},{14,15},{17,16},{18,... | collective-permute-start | bytes 3145736 | tf_op jit(solution)/shard_map/ppermute | solution.py:374
  110.3 42.2 %collective-permute-start.11 = (bf16[256,2048]{1,0:T(8,128)(2,1)}, bf16[256,2048]{1,0:T(8,128)(2,1)}, u32[]{:S(2)}, u32[]{:S(2)}) collective-permute-start(bf16[256,2048]{1,0:T(8,128)(2,1)} %get-tuple-element.160), channel_id=1, source_target_pairs={{1,0},{2,3},{5,4},{6,7},{9,8},{10,11},{13,12},{14,15},{17,16},{18,... | collective-permute-start | bytes 3145736 | tf_op jit(solution)/shard_map/ppermute | solution.py:374
  112.7 34.0 %copy-start.40 = (s32[4]{0:T(128)S(1)}, s32[4]{0:T(128)}, u32[]{:S(2)}) copy-start(s32[4]{0:T(128)} %constant.164.clone) | copy-start | bytes 52
  112.7 35.9 %copy-start.39 = (s32[4]{0:T(128)S(1)}, s32[4]{0:T(128)}, u32[]{:S(2)}) copy-start(s32[4]{0:T(128)} %constant.165.clone) | copy-start | bytes 52
  130.0 43.8 %collective-permute-start.8 = (bf16[512,768]{1,0:T(8,128)(2,1)S(1)}, bf16[512,768]{1,0:T(8,128)(2,1)}, u32[]{:S(2)}, u32[]{:S(2)}) collective-permute-start(bf16[512,768]{1,0:T(8,128)(2,1)S(1)} %pad_maximum_fusion.2.refs_0_), channel_id=1, source_target_pairs={{0,1},{1,0},{2,3},{3,2},{4,5},{5,4},{6,7},{7,6},{8,9},{9,8},{10,11... | collective-permute-start | bytes 2359304 | tf_op jit(solution)/shard_map/ppermute | solution.py:374
  132.5 41.4 %collective-permute-start.9 = (bf16[512,768]{1,0:T(8,128)(2,1)S(1)}, bf16[512,768]{1,0:T(8,128)(2,1)}, u32[]{:S(2)}, u32[]{:S(2)}) collective-permute-start(bf16[512,768]{1,0:T(8,128)(2,1)S(1)} %pad_maximum_fusion.2.refs_0_), channel_id=1, source_target_pairs={{1,2},{2,1},{5,6},{6,5},{9,10},{10,9},{13,14},{14,13},{17,18},{18,... | collective-permute-start | bytes 2359304 | tf_op jit(solution)/shard_map/ppermute | solution.py:374
  137.0 189.0 %all-gather.3.cloned.1.call-start = ((), (), s32[]{:S(2)}) async-start(), calls=%async_computation.3 | async-start | bytes 1769472 | tf_op jit(solution)/shard_map/all_gather | solution.py:515
  173.8 33.3 %copy-start.12 = (f32[8,2048]{1,0:T(8,128)}, f32[8,2048]{1,0:T(8,128)S(1)}, u32[]{:S(2)}) copy-start(f32[8,2048]{1,0:T(8,128)S(1)} %get-tuple-element.99.gain_in) | copy-start | bytes 196612
  173.9 14.2 %collective-permute-start.12 = (bf16[512,768]{1,0:T(8,128)(2,1)}, bf16[512,768]{1,0:T(8,128)(2,1)}, u32[]{:S(2)}, u32[]{:S(2)}) collective-permute-start(bf16[512,768]{1,0:T(8,128)(2,1)} %collective-permute-done.8.refs_1_), channel_id=1, source_target_pairs={{1,2},{2,1},{5,6},{6,5},{9,10},{10,9},{13,14},{14,13},{17,18},{18,... | collective-permute-start | bytes 2359304 | tf_op jit(solution)/shard_map/ppermute | solution.py:374
  176.8 17.9 %collective-permute-start.13 = (bf16[512,768]{1,0:T(8,128)(2,1)}, bf16[512,768]{1,0:T(8,128)(2,1)}, u32[]{:S(2)}, u32[]{:S(2)}) collective-permute-start(bf16[512,768]{1,0:T(8,128)(2,1)} %collective-permute-done.9.refs_2_), channel_id=1, source_target_pairs={{1,0},{2,3},{5,4},{6,7},{9,8},{10,11},{13,12},{14,15},{17,16},{18,... | collective-permute-start | bytes 2359304 | tf_op jit(solution)/shard_map/ppermute | solution.py:374
  183.5 39.5 %collective-permute-start.25 = (bf16[2,512,768]{2,1,0:T(8,128)(2,1)}, bf16[2,512,768]{2,1,0:T(8,128)(2,1)}, u32[]{:S(2)}, u32[]{:S(2)}) collective-permute-start(bf16[2,512,768]{2,1,0:T(8,128)(2,1)} %constant_dynamic-slice_fusion), channel_id=1, source_target_pairs={{0,1},{3,2},{4,5},{7,6},{8,9},{11,10},{12,13},{15,14},{16,17},{19,... | collective-permute-start | bytes 4718600 | tf_op jit(solution)/shard_map/ppermute | solution.py:374
  194.7 20.1 %collective-permute-start.14 = (bf16[512,768]{1,0:T(8,128)(2,1)}, bf16[512,768]{1,0:T(8,128)(2,1)}, u32[]{:S(2)}, u32[]{:S(2)}) collective-permute-start(bf16[512,768]{1,0:T(8,128)(2,1)} %collective-permute-done.12.refs_3_), channel_id=1, source_target_pairs={{1,0},{2,3},{5,4},{6,7},{9,8},{10,11},{13,12},{14,15},{17,16},{18,... | collective-permute-start | bytes 2359304 | tf_op jit(solution)/shard_map/ppermute | solution.py:374
  199.9 93.4 %collective-permute-start.29 = (bf16[2,256,2048]{2,1,0:T(8,128)(2,1)}, bf16[2,256,2048]{2,1,0:T(8,128)(2,1)}, u32[]{:S(2)}, u32[]{:S(2)}) collective-permute-start(bf16[2,256,2048]{2,1,0:T(8,128)(2,1)} %bitcast.11), channel_id=1, source_target_pairs={{3,2},{7,6},{11,10},{15,14},{19,18},{23,22},{27,26},{31,30}} | collective-permute-start | bytes 6291464 | tf_op jit(solution)/shard_map/ppermute | solution.py:374
  214.8 55.6 %collective-permute-start.15 = (bf16[256,2048]{1,0:T(8,128)(2,1)}, bf16[256,2048]{1,0:T(8,128)(2,1)}, u32[]{:S(2)}, u32[]{:S(2)}) collective-permute-start(bf16[256,2048]{1,0:T(8,128)(2,1)} %get-tuple-element.100), channel_id=1, source_target_pairs={{1,0},{2,3},{5,4},{6,7},{9,8},{10,11},{13,12},{14,15},{17,16},{18,... | collective-permute-start | bytes 3145736 | tf_op jit(solution)/shard_map/ppermute | solution.py:374
  226.4 72.7 %collective-permute-start.26 = (bf16[2,512,768]{2,1,0:T(8,128)(2,1)}, bf16[2,512,768]{2,1,0:T(8,128)(2,1)}, u32[]{:S(2)}, u32[]{:S(2)}) collective-permute-start(bf16[2,512,768]{2,1,0:T(8,128)(2,1)} %add_convert_fusion.1), channel_id=1, source_target_pairs={{1,2},{2,1},{5,6},{6,5},{9,10},{10,9},{13,14},{14,13},{17,18},{18,... | collective-permute-start | bytes 4718600 | tf_op jit(solution)/shard_map/ppermute | solution.py:374
  231.3 183.9 %all-gather.5.cloned.1.call-start = ((), (), s32[]{:S(2)}) async-start(), calls=%async_computation.4 | async-start | bytes 1179648 | tf_op jit(solution)/shard_map/all_gather | solution.py:516
  253.9 52.5 %collective-permute-start.31 = (bf16[1,256,2048]{2,1,0:T(8,128)(2,1)}, bf16[1,256,2048]{2,1,0:T(8,128)(2,1)}, u32[]{:S(2)}, u32[]{:S(2)}) collective-permute-start(bf16[1,256,2048]{2,1,0:T(8,128)(2,1)} %get-tuple-element.157), channel_id=1, source_target_pairs={{0,1},{4,5},{8,9},{12,13},{16,17},{20,21},{24,25},{28,29}} | collective-permute-start | bytes 3145736 | tf_op jit(solution)/shard_map/ppermute | solution.py:374
  255.6 51.0 %collective-permute-start.33 = (bf16[1,256,2048]{2,1,0:T(8,128)(2,1)}, bf16[1,256,2048]{2,1,0:T(8,128)(2,1)}, u32[]{:S(2)}, u32[]{:S(2)}) collective-permute-start(bf16[1,256,2048]{2,1,0:T(8,128)(2,1)} %get-tuple-element.158), channel_id=1, source_target_pairs={{0,1},{4,5},{8,9},{12,13},{16,17},{20,21},{24,25},{28,29}} | collective-permute-start | bytes 3145736 | tf_op jit(solution)/shard_map/ppermute | solution.py:374
  270.5 49.0 %collective-permute-start.18 = (f32[2048]{0:T(1024)S(1)}, f32[2048]{0:T(1024)S(1)}, u32[]{:S(2)}, u32[]{:S(2)}) collective-permute-start(f32[2048]{0:T(1024)S(1)} %bitcast.55), channel_id=1, source_target_pairs={{0,4},{4,0},{8,12},{12,8},{16,20},{20,16},{24,28},{28,24},{1,5},{5... | collective-permute-start | bytes 24584 | tf_op jit(solution)/shard_map/ppermute | solution.py:434
  293.3 22.2 %collective-permute-start.21 = (bf16[1,512,768]{2,1,0:T(8,128)(2,1)S(1)}, bf16[1,512,768]{2,1,0:T(8,128)(2,1)S(1)}, u32[]{:S(2)}, u32[]{:S(2)}) collective-permute-start(bf16[1,512,768]{2,1,0:T(8,128)(2,1)S(1)} %constant_dynamic-slice_fusion.1), channel_id=1, source_target_pairs={{0,1},{3,2},{4,5},{7,6},{8,9},{11,10},{12,13},{15,14},{16,17},{19,... | collective-permute-start | bytes 2359304 | tf_op jit(solution)/shard_map/ppermute | solution.py:374
  299.1 50.0 %collective-permute-start.30 = (bf16[2,256,2048]{2,1,0:T(8,128)(2,1)}, bf16[2,256,2048]{2,1,0:T(8,128)(2,1)}, u32[]{:S(2)}, u32[]{:S(2)}) collective-permute-start(bf16[2,256,2048]{2,1,0:T(8,128)(2,1)} %add_convert_fusion), channel_id=1, source_target_pairs={{2,1},{6,5},{10,9},{14,13},{18,17},{22,21},{26,25},{30,29}} | collective-permute-start | bytes 6291464 | tf_op jit(solution)/shard_map/ppermute | solution.py:374
  306.4 26.0 %collective-permute-start.27 = (bf16[1,512,768]{2,1,0:T(8,128)(2,1)}, bf16[1,512,768]{2,1,0:T(8,128)(2,1)S(1)}, u32[]{:S(2)}, u32[]{:S(2)}) collective-permute-start(bf16[1,512,768]{2,1,0:T(8,128)(2,1)} %add_convert_fusion.5), channel_id=1, source_target_pairs={{0,1},{1,0},{2,3},{3,2},{4,5},{5,4},{6,7},{7,6},{8,9},{9,8},{10,11... | collective-permute-start | bytes 2359304 | tf_op jit(solution)/shard_map/ppermute | solution.py:374
  310.3 44.3 %collective-permute-start.34 = (bf16[1,256,2048]{2,1,0:T(8,128)(2,1)}, bf16[1,256,2048]{2,1,0:T(8,128)(2,1)}, u32[]{:S(2)}, u32[]{:S(2)}) collective-permute-start(bf16[1,256,2048]{2,1,0:T(8,128)(2,1)} %get-tuple-element.156), channel_id=1, source_target_pairs={{1,2},{5,6},{9,10},{13,14},{17,18},{21,22},{25,26},{29,30}} | collective-permute-start | bytes 3145736 | tf_op jit(solution)/shard_map/ppermute | solution.py:374
  315.6 46.2 %collective-permute-start.32 = (bf16[1,256,2048]{2,1,0:T(8,128)(2,1)}, bf16[1,256,2048]{2,1,0:T(8,128)(2,1)}, u32[]{:S(2)}, u32[]{:S(2)}) collective-permute-start(bf16[1,256,2048]{2,1,0:T(8,128)(2,1)} %get-tuple-element.155), channel_id=1, source_target_pairs={{1,2},{5,6},{9,10},{13,14},{17,18},{21,22},{25,26},{29,30}} | collective-permute-start | bytes 3145736 | tf_op jit(solution)/shard_map/ppermute | solution.py:374
  320.0 28.9 %collective-permute-start.23 = (bf16[1,512,768]{2,1,0:T(8,128)(2,1)}, bf16[1,512,768]{2,1,0:T(8,128)(2,1)S(1)}, u32[]{:S(2)}, u32[]{:S(2)}) collective-permute-start(bf16[1,512,768]{2,1,0:T(8,128)(2,1)} %get-tuple-element.149), channel_id=1, source_target_pairs={{0,1},{3,2},{4,5},{7,6},{8,9},{11,10},{12,13},{15,14},{16,17},{19,... | collective-permute-start | bytes 2359304 | tf_op jit(solution)/shard_map/ppermute | solution.py:374
  330.4 33.2 %copy-start.16 = (bf16[2,256,2048]{2,1,0:T(8,128)(2,1)}, bf16[2,256,2048]{2,1,0:T(8,128)(2,1)S(1)}, u32[]{:S(2)}) copy-start(bf16[2,256,2048]{2,1,0:T(8,128)(2,1)S(1)} %broadcast_select_fusion.refs_0_) | copy-start | bytes 6291460
  332.4 63.6 %collective-permute-start.19 = (f32[2048]{0:T(1024)S(1)}, f32[2048]{0:T(1024)S(1)}, u32[]{:S(2)}, u32[]{:S(2)}) collective-permute-start(f32[2048]{0:T(1024)S(1)} %add.150), channel_id=1, source_target_pairs={{0,8},{4,12},{8,0},{12,4},{16,24},{20,28},{24,16},{28,20},{1,9},{5... | collective-permute-start | bytes 24584 | tf_op jit(solution)/shard_map/ppermute | solution.py:434
  348.9 47.7 %collective-permute-start.16 = (f32[2048]{0:T(1024)S(1)}, f32[2048]{0:T(1024)S(1)}, u32[]{:S(2)}, u32[]{:S(2)}) collective-permute-start(f32[2048]{0:T(1024)S(1)} %bitcast.81), channel_id=1, source_target_pairs={{0,1},{1,0},{2,3},{3,2},{4,5},{5,4},{6,7},{7,6},{8,9},{9,8},{10,11... | collective-permute-start | bytes 24584 | tf_op jit(solution)/shard_map/ppermute | solution.py:434
  349.1 74.5 %collective-permute-start.22 = (bf16[1,512,768]{2,1,0:T(8,128)(2,1)}, bf16[1,512,768]{2,1,0:T(8,128)(2,1)S(1)}, u32[]{:S(2)}, u32[]{:S(2)}) collective-permute-start(bf16[1,512,768]{2,1,0:T(8,128)(2,1)} %get-tuple-element.148), channel_id=1, source_target_pairs={{1,2},{2,1},{5,6},{6,5},{9,10},{10,9},{13,14},{14,13},{17,18},{18,... | collective-permute-start | bytes 2359304 | tf_op jit(solution)/shard_map/ppermute | solution.py:374
  354.6 40.3 %collective-permute-start.24 = (bf16[1,512,768]{2,1,0:T(8,128)(2,1)S(1)}, bf16[1,512,768]{2,1,0:T(8,128)(2,1)S(1)}, u32[]{:S(2)}, u32[]{:S(2)}) collective-permute-start(bf16[1,512,768]{2,1,0:T(8,128)(2,1)S(1)} %add_convert_fusion.7), channel_id=1, source_target_pairs={{1,2},{2,1},{5,6},{6,5},{9,10},{10,9},{13,14},{14,13},{17,18},{18,... | collective-permute-start | bytes 2359304 | tf_op jit(solution)/shard_map/ppermute | solution.py:374
  365.2 49.3 %copy-start.25 = (f32[2048]{0:T(1024)S(1)}, f32[2048]{0:T(1024)}, u32[]{:S(2)}) copy-start(f32[2048]{0:T(1024)} %param.50) | copy-start | bytes 24580
  365.2 49.3 %copy-start.26 = (f32[2048]{0:T(1024)S(1)}, f32[2048]{0:T(1024)}, u32[]{:S(2)}) copy-start(f32[2048]{0:T(1024)} %param.51) | copy-start | bytes 24580
  365.2 50.0 %collective-permute-start.35 = (bf16[1,256,2048]{2,1,0:T(8,128)(2,1)}, bf16[1,256,2048]{2,1,0:T(8,128)(2,1)S(1)}, u32[]{:S(2)}, u32[]{:S(2)}) collective-permute-start(bf16[1,256,2048]{2,1,0:T(8,128)(2,1)} %add_convert_fusion.2), channel_id=1, source_target_pairs={{0,1},{1,0},{2,3},{3,2},{4,5},{5,4},{6,7},{7,6},{8,9},{9,8},{10,11... | collective-permute-start | bytes 3145736 | tf_op jit(solution)/shard_map/ppermute | solution.py:374
  396.0 27.6 %collective-permute-start.28 = (bf16[1,512,768]{2,1,0:T(8,128)(2,1)}, bf16[1,512,768]{2,1,0:T(8,128)(2,1)}, u32[]{:S(2)}, u32[]{:S(2)}) collective-permute-start(bf16[1,512,768]{2,1,0:T(8,128)(2,1)} %add_convert_fusion.6), channel_id=1, source_target_pairs={{0,1},{1,0},{2,3},{3,2},{4,5},{5,4},{6,7},{7,6},{8,9},{9,8},{10,11... | collective-permute-start | bytes 2359304 | tf_op jit(solution)/shard_map/ppermute | solution.py:374
  396.1 5.6 %collective-permute-start.20 = (f32[2048]{0:T(1024)S(1)}, f32[2048]{0:T(1024)S(1)}, u32[]{:S(2)}, u32[]{:S(2)}) collective-permute-start(f32[2048]{0:T(1024)S(1)} %add.151), channel_id=1, source_target_pairs={{0,16},{4,20},{8,24},{12,28},{16,0},{20,4},{24,8},{28,12},{1,17},{... | collective-permute-start | bytes 24584 | tf_op jit(solution)/shard_map/ppermute | solution.py:434
  396.6 17.9 %collective-permute-start.17 = (f32[2048]{0:T(1024)S(1)}, f32[2048]{0:T(1024)S(1)}, u32[]{:S(2)}, u32[]{:S(2)}) collective-permute-start(f32[2048]{0:T(1024)S(1)} %add.143), channel_id=1, source_target_pairs={{0,2},{1,3},{2,0},{3,1},{4,6},{5,7},{6,4},{7,5},{8,10},{9,11},{10,... | collective-permute-start | bytes 24584 | tf_op jit(solution)/shard_map/ppermute | solution.py:434
  (40 other events, 504.1 us)
Sparse Core Ops, SparseCore 0:
  67.8 35.0 reduce-scatter.4
  137.1 37.6 reduce-scatter.6
  231.4 25.3 all-gather.2
  326.1 26.7 all-gather.4

commit v5 on v4

--- a/solution.py
+++ b/solution.py
@@ -487,15 +487,18 @@
         near0 = send(x0, MID_SWAP)
         normed, normed_t = norm(tokens, gain[None])
         tab = rope_tables(length)
-        pair0, near0, normed, normed_t, tab = lax.optimization_barrier((pair0, near0, normed, normed_t, tab))
+        pair0, near0, normed, normed_t, tab, x1 = lax.optimization_barrier(
+            (pair0, near0, normed, normed_t, tab, x1)
+        )
         far0 = send(pair0, MID_SWAP)
         end_near0 = send(near0, OUTWARD)
         o_in = send(after(w_out, pair0, near0), INWARD)
         far0, end_near0 = lax.optimization_barrier((far0, end_near0))
         end_far0 = send(far0, OUTWARD)
         o_near = send(after(w_out, far0), MID_SWAP)
-        o_far = send(after(o_in, far0), MID_SWAP)
-        o_one = send(jnp.where(me == 1, w_out, o_near), OUTWARD)
+        end_far0, x1 = lax.optimization_barrier((end_far0, x1))
+        pair1 = send(x1, PAIR_SWAP)
+        near1 = send(x1, MID_SWAP)
         q_cands = [(x0, pair0, near0, far0, end_near0, end_far0)]
         q_starts = line_starts(me, w_rows)
     else:
@@ -506,26 +509,48 @@
         all_out = lax.all_gather(w_out, "fsdp", axis=0, tiled=True)
 
     scale = 1.0 / islands
-    qkv_total = lax.psum_scatter(w_qkv, "island", scatter_dimension=1, tiled=True).astype(F32)
-    out_total = lax.psum_scatter(w_out, "island", scatter_dimension=1, tiled=True).astype(F32)
+    qkv_total = lax.psum_scatter(w_qkv, "island", scatter_dimension=1, tiled=True)
+    out_total = lax.psum_scatter(w_out, "island", scatter_dimension=1, tiled=True)
     gain_total = all_sum(gain, "island", islands)
     gain_pair = nesterov(gain_global, gain_momentum, gain_total * scale)
-    qkv_pair = nesterov(qkv_global, qkv_momentum, qkv_total * scale)
-    out_pair = nesterov(out_global, out_momentum, out_total * scale)
-    qkv_whole = lax.all_gather(qkv_pair[0].astype(BF16), "island", axis=1, tiled=True)
-    out_whole = lax.all_gather(out_pair[0].astype(BF16), "island", axis=1, tiled=True)
+
+    def outer(qkv_total, out_total):
+        qkv_pair = nesterov(qkv_global, qkv_momentum, qkv_total.astype(F32) * scale)
+        out_pair = nesterov(out_global, out_momentum, out_total.astype(F32) * scale)
+        qkv_whole = lax.all_gather(qkv_pair[0].astype(BF16), "island", axis=1, tiled=True)
+        out_whole = lax.all_gather(out_pair[0].astype(BF16), "island", axis=1, tiled=True)
+        return qkv_pair, out_pair, qkv_whole, out_whole
 
     *kept0, go0, w0 = forward(q_starts, normed, cotangent, tab, q_cands[0])
     gain_sum = jnp.zeros((8, width), F32)
     if line:
         go0 = go0.reshape(2, o_rows, width)
-        o_two = send(after(o_far, go0), OUTWARD)
+        pair1, near1, go0 = lax.optimization_barrier((pair1, near1, go0))
+        far1 = send(pair1, MID_SWAP)
+        end_near1 = send(near1, OUTWARD)
         go_in0 = send(go0, [(3, 2)])
-        synced = (qkv_pair[0], qkv_pair[1], out_pair[0], out_pair[1])
-        x1 = after(x1, o_two)
-        pair1 = send(x1, PAIR_SWAP)
-        near1 = send(x1, MID_SWAP)
-        o_cands = (w_out, o_in, o_near, o_far, o_one, o_two)
+        go_last0 = send(go0[1:], [(0, 1)])
+        far1, end_near1 = lax.optimization_barrier((far1, end_near1))
+        end_far1 = send(far1, OUTWARD)
+        o_far = send(after(o_in, far1), MID_SWAP)
+        o_first = jnp.where(me == 1, w_out, o_near)
+        end_far1, o_far, o_first = lax.optimization_barrier((end_far1, o_far, o_first))
+        o_one = send(o_first, OUTWARD)
+        o_two = send(o_far, OUTWARD)
+        go_sum0 = plus(go0, go_in0)
+        go_over0 = send(go_sum0, [(2, 1)])
+        *kept1, go1, w1 = forward(
+            after(q_starts, go_sum0),
+            normed,
+            cotangent,
+            tab,
+            (x1, pair1, near1, far1, end_near1, end_far1),
+        )
+        go1 = go1.reshape(2, o_rows, width)
+        go_in1_far = send(go1[1:], [(0, 1)])
+        go_in1_near = send(go1[:1], [(0, 1)])
+        go_last1 = send(go1[:1], [(3, 2)])
+        o_three = send(after(jnp.where(me == 2, w_out, o_near), go1), OUTWARD)
         places = (
             table(me, 0, 1, -1, -1),
             table(me, -1, 0, -1, -1),
@@ -534,23 +559,25 @@
             table(me, 1, -1, -1, 1),
             table(me, -1, -1, -1, 0),
         )
-        o_starts = starts_of(o_rows, places)
-        g0, gain_sum = backward(o_starts, normed_t, w0, cotangent, tab, kept0, gain_sum, o_cands)
-        pair1, near1 = lax.optimization_barrier((pair1, near1, g0))[:2]
-        far1 = send(pair1, MID_SWAP)
-        end_near1 = send(near1, OUTWARD)
+        g0, gain_sum = backward(
+            starts_of(o_rows, places),
+            normed_t,
+            w0,
+            cotangent,
+            tab,
+            kept0,
+            after(gain_sum, go1),
+            (w_out, o_in, o_near, o_far, o_one, o_two),
+        )
+        g0, go0, go1, qkv_total, out_total = lax.optimization_barrier((g0, go0, go1, qkv_total, out_total))
+        qkv_pair, out_pair, qkv_whole, out_whole = outer(qkv_total, out_total)
+        synced = (qkv_pair[0], qkv_pair[1], out_pair[0], out_pair[1])
+        go_sum0 = plus(go0[:1], go_over0[:1])
+        go_end0 = send(go_sum0, [(1, 0)])
+        go_sum1_far = plus(go1[1:], go_in1_far)
+        go_over1_far = send(go_sum1_far, [(1, 2)])
+        go_sum1_near = plus(go1[:1], go_in1_near)
         grad0 = scatter_merged(g0, me)
-        go_over0 = send(plus(go0, go_in0), [(2, 1)])
-        far1, end_near1 = lax.optimization_barrier((far1, end_near1))
-        end_far1 = send(far1, OUTWARD)
-        o_three = send(after(jnp.where(me == 2, w_out, o_near), end_far1), OUTWARD)
-        *kept1, go1, w1 = forward(
-            after(q_starts, *synced), normed, cotangent, tab, (x1, pair1, near1, far1, end_near1, end_far1)
-        )
-        go1 = go1.reshape(2, o_rows, width)
-        go_in1_far = send(go1[1:], [(0, 1)])
-        go_in1_near = send(go1[:1], [(0, 1)])
-        o_cands = (w_out, o_in, o_near, o_far, o_three, o_two)
         places = (
             table(me, -1, -1, 0, 1),
             table(me, -1, -1, 1, -1),
@@ -560,9 +587,17 @@
             table(me, 1, -1, -1, -1),
         )
         g1, gain_sum = backward(
-            starts_of(o_rows, places), normed_t, w1, cotangent, tab, kept1, after(gain_sum, go1), o_cands
+            starts_of(o_rows, places),
+            normed_t,
+            w1,
+            cotangent,
+            tab,
+            kept1,
+            after(gain_sum, go_last0, go_last1, go_sum0, go_sum1_far, go_sum1_near, *synced),
+            (w_out, o_in, o_near, o_far, o_three, o_two),
         )
     else:
+        qkv_pair, out_pair, qkv_whole, out_whole = outer(qkv_total, out_total)
         *kept1, go1, w1 = forward(q_starts, normed, cotangent, tab, q_cands[1])
         go = jnp.concatenate([go0, go1], axis=0)
         none = jnp.zeros((1,), jnp.int32)
@@ -579,15 +614,15 @@
 
     if line:
         qkv_state = adam_pair(0, grad0, ())
-        go_over1_far = send(plus(go1[1:], go_in1_far), [(1, 2)])
-        go_over1_near = send(plus(go1[:1], go_in1_near), [(1, 2)])
-        low = me < 2
-        mine = jnp.where(low, go0, go1)
-        over1 = jnp.concatenate([go_over1_near, go_over1_far], axis=0)
-        over = jnp.where(low, go_over0, over1)
+        go_over1_near = send(go_sum1_near, [(1, 2)])
+        go_end1 = send(plus(go1[1:], go_over1_far), [(2, 3)])
         odd = me & 1
-        go_out = send(plus(block(mine, 1 - odd), block(over, 1 - odd)), PAIR_SWAP)
-        out_grad = (jnp.stack([odd, odd, odd * 0]).astype(jnp.int32), (mine, over, go_out))
+        mine = jnp.where(me < 2, go0, go1)
+        none = me * 0
+        out_grad = (
+            jnp.stack([odd, odd] + [none] * 5).astype(jnp.int32),
+            (mine, go_over0, go_over1_near, go_last0, go_last1, go_end0, go_end1),
+        )
         out_state = out_adam(out_grad, w_out, out_first[0], out_second[0], out_whole)
         grad1 = scatter_single(g1, me, (qkv_state[0],))
     else:

time: 445 us -> 477 us (1.072)
  waiting for transfers between devices: 131 us -> 146 us
  starting transfers between devices: 79.3 us -> 85.5 us
    ppermute x31 -> x34, waiting for transfers between devices: 118 us -> 140 us  [send(): return lax.ppermute(x, 'fsdp', pairs)]
    ppermute x5, waiting for transfers between devices: 12.9 us -> 6.03 us  [all_sum(): x = x + lax.ppermute(x, axis, [(i, i ^ k) for i in range(n)])]
    convert_element_type x8 -> x9, other arithmetic: 19.5 us -> 26 us  [plus(): return (a.astype(F32) + b.astype(F32)).astype(BF16)]
    slice x0 -> x2, local copies, waits for them, and re-layouts: none -> 5.53 us  [the longest x1 3.23 us: shards(): go_in1_far = send(go1[1:], [(0, 1)])]
    ppermute x31 -> x34, starting transfers between devices: 76.8 us -> 80.7 us  [send(): return lax.ppermute(x, 'fsdp', pairs)]
    unnamed x102 -> x143, local copies, waits for them, and re-layouts: 19.9 us -> 22.5 us
  transfers between devices with their start and end apart: 40 -> 43, of which waited for: 18 -> 16; matrix products, arithmetic and copies ran while one was open for 16% -> 15% of each run, Pallas kernels for 22% -> 20%
where the time goes in v5:
time: 477 us; the launch traced here: 468 us
  waiting for transfers between devices  146 us (31%)
  Pallas kernels  103 us (22%)
  starting transfers between devices  85.5 us (18%)
  local copies, waits for them, and re-layouts  53.5 us (11%)
  between operations  42.9 us (9%)
  other arithmetic  38 us (8%)
    ppermute x34, waiting for transfers between devices, send(): return lax.ppermute(x, 'fsdp', pairs)  140 us
    ppermute x34, starting transfers between devices, send(): return lax.ppermute(x, 'fsdp', pairs)  80.7 us
    pallas_call x5, Pallas kernels, call(): pl.pallas_call(kernel, out_shape=outs, grid=(1,), in_specs=specs, out_spe...  79.7 us
    convert_element_type x9, other arithmetic, plus(): return (a.astype(F32) + b.astype(F32)).astype(BF16)  26 us
    pallas_call x3, Pallas kernels, adam_call(): pl.pallas_call(functools.partial(adam_kernel, n_parts, len(held)), out_sh...  23 us
    unnamed x143, local copies, waits for them, and re-layouts  22.5 us
    dynamic_slice x20, local copies, waits for them, and re-layouts, table(): return jnp.array(values, jnp.int32)[me]  11.8 us
  transfers between devices with their start and end apart: 43, of which 16 were waited for; matrix products, arithmetic and copies ran while one was open for 15% of the time, Pallas kernels for 20%

profile of v5, /device:TPU:22, one launch (start us, length us, event | category | flops | bytes accessed | tf_op | source)
XLA Modules:
  0.0 468.2 jit_solution(9705131590251509391)
XLA Ops:
  13.3 4.1 shard_map.478
  20.2 8.9 %collective-permute-done.refs_1_ = bf16[512,768]{1,0:T(8,128)(2,1)S(1)} collective-permute-done((bf16[512,768]{1,0:T(8,128)(2,1)S(1)}, bf16[512,768]{1,0:T(8,128)(2,1)S(1)}, u32[]{:S(2)}, u32[]{:S(2)}) %collective-permute-start) | collective-permute-done | bytes 786464 | tf_op jit(solution)/shard_map/ppermute | solution.py:374
  29.1 3.2 collective-permute-done.1.refs_2_
  32.3 2.3 collective-permute-start.2
  37.8 14.7 %collective-permute-done.2.refs_3_ = bf16[512,768]{1,0:T(8,128)(2,1)} collective-permute-done((bf16[512,768]{1,0:T(8,128)(2,1)S(1)}, bf16[512,768]{1,0:T(8,128)(2,1)}, u32[]{:S(2)}, u32[]{:S(2)}) %collective-permute-start.2) | collective-permute-done | bytes 786464 | tf_op jit(solution)/shard_map/ppermute | solution.py:374
  53.6 5.3 %collective-permute-start.4 = (bf16[512,768]{1,0:T(8,128)(2,1)}, bf16[512,768]{1,0:T(8,128)(2,1)}, u32[]{:S(2)}, u32[]{:S(2)}) collective-permute-start(bf16[512,768]{1,0:T(8,128)(2,1)} %collective-permute-done.2.refs_3_), channel_id=1, source_target_pairs={{1,0},{2,3},{5,4},{6,7},{9,8},{10,11},{13,12},{14,15},{17,16},{18,... | collective-permute-start | bytes 2359304 | tf_op jit(solution)/shard_map/ppermute | solution.py:374
  60.5 12.8 %collective-permute-done.4.refs_5_ = bf16[512,768]{1,0:T(8,128)(2,1)} collective-permute-done((bf16[512,768]{1,0:T(8,128)(2,1)}, bf16[512,768]{1,0:T(8,128)(2,1)}, u32[]{:S(2)}, u32[]{:S(2)}) %collective-permute-start.4) | collective-permute-done | bytes 786464 | tf_op jit(solution)/shard_map/ppermute | solution.py:374
  73.3 2.5 collective-permute-start.5
  75.8 3.2 collective-permute-start.6
  91.6 19.3 %shard_map.479 = (bf16[512,512]{1,0:T(8,128)(2,1)S(1)}, bf16[512,128]{1,0:T(8,128)(2,1)S(1)}, bf16[512,128]{1,0:T(8,128)(2,1)S(1)}, bf16[8,256,256]{2,1,0:T(8,12...) custom-call(s32[6]{0:T(128)S(1)} %stack.67.starts, ...), custom_call_target="tpu_custom_call" | custom-call | flops 1 | bytes 1 | tf_op jit(solution)/shard_map/pallas_call | solution.py:206
  113.4 3.3 collective-permute-start.8
  116.7 5.4 %collective-permute-start.9 = (bf16[512,768]{1,0:T(8,128)(2,1)}, bf16[512,768]{1,0:T(8,128)(2,1)S(1)}, u32[]{:S(2)}, u32[]{:S(2)}) collective-permute-start(bf16[512,768]{1,0:T(8,128)(2,1)} %collective-permute-done.6.refs_2_), channel_id=1, source_target_pairs={{1,0},{2,3},{5,4},{6,7},{9,8},{10,11},{13,12},{14,15},{17,16},{18,... | collective-permute-start | bytes 2359304 | tf_op jit(solution)/shard_map/ppermute | solution.py:374
  124.1 12.1 %collective-permute-done.8.refs_3_ = bf16[512,768]{1,0:T(8,128)(2,1)} collective-permute-done((bf16[512,768]{1,0:T(8,128)(2,1)}, bf16[512,768]{1,0:T(8,128)(2,1)}, u32[]{:S(2)}, u32[]{:S(2)}) %collective-permute-start.8) | collective-permute-done | bytes 786464 | tf_op jit(solution)/shard_map/ppermute | solution.py:374
  137.0 3.3 collective-permute-start.12
  140.3 2.4 collective-permute-start.10
  142.8 15.8 %collective-permute-done.13.refs_2_ = bf16[256,2048]{1,0:T(8,128)(2,1)} collective-permute-done((bf16[256,2048]{1,0:T(8,128)(2,1)S(1)}, bf16[256,2048]{1,0:T(8,128)(2,1)}, u32[]{:S(2)}, u32[]{:S(2)}) %collective-permute-start.13) | collective-permute-done | bytes 1048608 | tf_op jit(solution)/shard_map/ppermute | solution.py:374
  158.6 2.7 broadcast_select_fusion.1
  161.3 14.9 %collective-permute-done.12.refs_3_ = bf16[256,2048]{1,0:T(8,128)(2,1)} collective-permute-done((bf16[256,2048]{1,0:T(8,128)(2,1)}, bf16[256,2048]{1,0:T(8,128)(2,1)}, u32[]{:S(2)}, u32[]{:S(2)}) %collective-permute-start.12) | collective-permute-done | bytes 1048608 | tf_op jit(solution)/shard_map/ppermute | solution.py:374
  176.3 2.4 collective-permute-start.14
  178.7 2.3 collective-permute-start.15
  181.0 3.7 add_convert_fusion
  184.7 18.7 %shard_map.480 = (bf16[512,512]{1,0:T(8,128)(2,1)S(1)}, bf16[512,128]{1,0:T(8,128)(2,1)S(1)}, bf16[512,128]{1,0:T(8,128)(2,1)S(1)}, bf16[8,256,256]{2,1,0:T(8,12...) custom-call(s32[6]{0:T(128)S(1)} %stack.67.starts, ...), custom_call_target="tpu_custom_call" | custom-call | flops 1 | bytes 1 | tf_op jit(solution)/shard_map/pallas_call | solution.py:206
  203.6 3.2 slice_bitcast_fusion
  208.4 4.6 collective-permute-start.18
  241.1 2.3 slice.56
  249.9 19.1 %shard_map.481 = (bf16[2048,768]{1,0:T(8,128)(2,1)}, f32[8,2048]{1,0:T(8,128)S(1)}) custom-call(s32[6]{0:T(128)S(1)} %stack.68.starts, bf16[2048,512]{1,0:T(8,128)(2,1)} %get-tuple-element.77.normed_t, bf16[2048,768]{1,0:T(8,128)(2,1)} %get-tuple-element.104.w_ref, bf16[512,2048]{1,0:T(8,128)(2,1)} %cot.7, f32[3,512,128]{2,1,0:T(8,128)S(1)} %pad_maximum_fusion.1.tab, ...), custom_call_target="tpu_custom_call" | custom-call | flops 1 | bytes 1 | tf_op jit(solution)/shard_map/pallas_call | solution.py:206
  269.6 2.8 constant_dynamic-slice_fusion
  273.9 2.6 fusion
  284.3 6.6 %collective-permute-start.21 = (bf16[256,2048]{1,0:T(8,128)(2,1)}, bf16[256,2048]{1,0:T(8,128)(2,1)S(1)}, u32[]{:S(2)}, u32[]{:S(2)}) collective-permute-start(bf16[256,2048]{1,0:T(8,128)(2,1)} %get-tuple-element.121), channel_id=1, source_target_pairs={{1,0},{2,3},{5,4},{6,7},{9,8},{10,11},{13,12},{14,15},{17,16},{18,... | collective-permute-start | bytes 3145736 | tf_op jit(solution)/shard_map/ppermute | solution.py:374
  290.8 3.0 add_convert_fusion.3
  293.8 5.3 %collective-permute-done.37 = bf16[1,256,2048]{2,1,0:T(8,128)(2,1)} collective-permute-done((bf16[1,256,2048]{2,1,0:T(8,128)(2,1)}, bf16[1,256,2048]{2,1,0:T(8,128)(2,1)}, u32[]{:S(2)}, u32[]{:S(2)}) %collective-permute-start.37) | collective-permute-done | bytes 1048608 | tf_op jit(solution)/shard_map/ppermute | solution.py:374
  299.1 3.7 fusion.1
  302.9 25.9 %collective-permute-done.17.refs_4_ = bf16[1,256,2048]{2,1,0:T(8,128)(2,1)S(1)} collective-permute-done((bf16[1,256,2048]{2,1,0:T(8,128)(2,1)}, bf16[1,256,2048]{2,1,0:T(8,128)(2,1)S(1)}, u32[]{:S(2)}, u32[]{:S(2)}) %collective-permute-start.17) | collective-permute-done | bytes 1048608 | tf_op jit(solution)/shard_map/ppermute | solution.py:374
  330.8 18.6 %shard_map.482 = (bf16[2048,768]{1,0:T(8,128)(2,1)}, f32[8,2048]{1,0:T(8,128)S(1)}) custom-call(s32[6]{0:T(128)S(1)} %stack.28.starts, bf16[2048,512]{1,0:T(8,128)(2,1)} %get-tuple-element.77.normed_t, bf16[2048,768]{1,0:T(8,128)(2,1)} %get-tuple-element.98.w_ref, bf16[512,2048]{1,0:T(8,128)(2,1)} %cot.7, f32[3,512,128]{2,1,0:T(8,128)S(1)} %pad_maximum_fusion.1.tab, ...), custom_call_target="tpu_custom_call" | custom-call | flops 1 | bytes 1 | tf_op jit(solution)/shard_map/pallas_call | solution.py:206
  355.3 3.4 add_convert_fusion.1
  360.7 6.3 %collective-permute-done.27 = bf16[1,512,768]{2,1,0:T(8,128)(2,1)S(1)} collective-permute-done((bf16[1,512,768]{2,1,0:T(8,128)(2,1)S(1)}, bf16[1,512,768]{2,1,0:T(8,128)(2,1)S(1)}, u32[]{:S(2)}, u32[]{:S(2)}) %collective-permute-start.27) | collective-permute-done | bytes 786464 | tf_op jit(solution)/shard_map/ppermute | solution.py:374
  367.1 2.5 add_convert_fusion.7
  376.1 8.7 %collective-permute-done.29 = bf16[1,512,768]{2,1,0:T(8,128)(2,1)} collective-permute-done((bf16[1,512,768]{2,1,0:T(8,128)(2,1)}, bf16[1,512,768]{2,1,0:T(8,128)(2,1)}, u32[]{:S(2)}, u32[]{:S(2)}) %collective-permute-start.29) | collective-permute-done | bytes 786464 | tf_op jit(solution)/shard_map/ppermute | solution.py:374
  384.7 2.4 add_convert_fusion.6
  389.2 9.0 %collective-permute-done.32.refs_1_ = bf16[2,512,768]{2,1,0:T(8,128)(2,1)S(1)} collective-permute-done((bf16[2,512,768]{2,1,0:T(8,128)(2,1)}, bf16[2,512,768]{2,1,0:T(8,128)(2,1)S(1)}, u32[]{:S(2)}, u32[]{:S(2)}) %collective-permute-start.32) | collective-permute-done | bytes 1572896 | tf_op jit(solution)/shard_map/ppermute | solution.py:374
  409.1 5.8 %collective-permute-done.22 = f32[2048]{0:T(1024)S(1)} collective-permute-done((f32[2048]{0:T(1024)S(1)}, f32[2048]{0:T(1024)S(1)}, u32[]{:S(2)}, u32[]{:S(2)}) %collective-permute-start.22) | collective-permute-done | bytes 8224 | tf_op jit(solution)/shard_map/ppermute | solution.py:434
  416.6 2.7 copy.66.refs_6_
  419.3 5.4 %collective-permute-start.38 = (bf16[1,256,2048]{2,1,0:T(8,128)(2,1)}, bf16[1,256,2048]{2,1,0:T(8,128)(2,1)}, u32[]{:S(2)}, u32[]{:S(2)}) collective-permute-start(bf16[1,256,2048]{2,1,0:T(8,128)(2,1)} %get-tuple-element.177), channel_id=1, source_target_pairs={{2,3},{6,7},{10,11},{14,15},{18,19},{22,23},{26,27},{30,31}} | collective-permute-start | bytes 3145736 | tf_op jit(solution)/shard_map/ppermute | solution.py:374
  426.2 2.5 add_convert_fusion.5
  428.7 7.6 %shard_map.483 = (bf16[512,1536]{1,0:T(8,128)(2,1)}, f32[512,1536]{1,0:T(8,128)}, f32[512,1536]{1,0:T(8,128)}) custom-call(s32[3]{0:T(128)S(1)} %pad_add_fusion.idx_ref, bf16[4,512,768]{2,1,0:T(8,128)(2,1)} %bitcast.71, bf16[2,512,768]{2,1,0:T(8,128)(2,1)S(1)} %collective-permute-done.32.refs_1_, bf16[1,512,768]{2,1,0:T(8,128)(2,1)} %collective-permute-done.33.refs_2_, ...), custom_call_target="tpu_custom_call" | custom-call | flops 20000000 | bytes 14000000 | tf_op jit(solution)/shard_map/pallas_call | solution.py:314
  436.3 4.2 collective-permute-start.28
  446.1 8.3 %shard_map.485 = (bf16[256,2048]{1,0:T(8,128)(2,1)}, f32[256,2048]{1,0:T(8,128)}, f32[256,2048]{1,0:T(8,128)}) custom-call(s32[7]{0:T(128)S(1)} %pad_add_fusion.1.idx_ref, bf16[2,256,2048]{2,1,0:T(8,128)(2,1)} %broadcast_select_fusion.refs_0_, bf16[2,256,2048]{2,1,0:T(8,128)(2,1)} %collective-permute-done.18.refs_1_, ...), custom_call_target="tpu_custom_call" | custom-call | flops 20000000 | bytes 14000000 | tf_op jit(solution)/shard_map/pallas_call | solution.py:314
  454.4 7.1 %shard_map.484 = (bf16[512,1536]{1,0:T(8,128)(2,1)}, f32[512,1536]{1,0:T(8,128)}, f32[512,1536]{1,0:T(8,128)}) custom-call(s32[3]{0:T(128)S(1)} %stack.70.idx_ref, bf16[4,512,768]{2,1,0:T(8,128)(2,1)} %bitcast.76, bf16[1,512,768]{2,1,0:T(8,128)(2,1)S(1)} %collective-permute-done.28.refs_1_, ...), custom_call_target="tpu_custom_call", output_to_operand_aliasing={{0}: (8, {}), {1}: (9, {}), {2}: (10, {})} | custom-call | flops 20000000 | bytes 14000000 | tf_op jit(solution)/shard_map/pallas_call | solution.py:314
  (258 shorter events, 88.6 us)
Async XLA Ops:
  7.2 232.1 %reduce-scatter.7.cloned.1.call-start = ((), (), s32[]{:S(2)}) async-start(), calls=%async_computation.5 | async-start | bytes 1769472
  9.8 19.3 %collective-permute-start = (bf16[512,768]{1,0:T(8,128)(2,1)S(1)}, bf16[512,768]{1,0:T(8,128)(2,1)S(1)}, u32[]{:S(2)}, u32[]{:S(2)}) collective-permute-start(bf16[512,768]{1,0:T(8,128)(2,1)S(1)} %pad_maximum_fusion.refs_0_), channel_id=1, source_target_pairs={{0,1},{1,0},{2,3},{3,2},{4,5},{5,4},{6,7},{7,6},{8,9},{9,8},{10,11... | collective-permute-start | bytes 2359304 | tf_op jit(solution)/shard_map/ppermute | solution.py:374
  11.4 20.9 %collective-permute-start.1 = (bf16[512,768]{1,0:T(8,128)(2,1)S(1)}, bf16[512,768]{1,0:T(8,128)(2,1)S(1)}, u32[]{:S(2)}, u32[]{:S(2)}) collective-permute-start(bf16[512,768]{1,0:T(8,128)(2,1)S(1)} %pad_maximum_fusion.refs_0_), channel_id=1, source_target_pairs={{1,2},{2,1},{5,6},{6,5},{9,10},{10,9},{13,14},{14,13},{17,18},{18,... | collective-permute-start | bytes 2359304 | tf_op jit(solution)/shard_map/ppermute | solution.py:374
  32.3 50.5 %copy-start.66 = (s32[4]{0:T(128)S(1)}, s32[4]{0:T(128)}, u32[]{:S(2)}) copy-start(s32[4]{0:T(128)} %constant.157.clone) | copy-start | bytes 52
  32.3 52.4 %copy-start.65 = (s32[4]{0:T(128)S(1)}, s32[4]{0:T(128)}, u32[]{:S(2)}) copy-start(s32[4]{0:T(128)} %constant.158.clone) | copy-start | bytes 52
  32.3 54.4 %copy-start = (bf16[1,256,2048]{2,1,0:T(8,128)(2,1)S(1)}, bf16[1,256,2048]{2,1,0:T(8,128)(2,1)}, u32[]{:S(2)}) copy-start(bf16[1,256,2048]{2,1,0:T(8,128)(2,1)} %param.43) | copy-start | bytes 3145732
  32.3 20.2 %collective-permute-start.2 = (bf16[512,768]{1,0:T(8,128)(2,1)S(1)}, bf16[512,768]{1,0:T(8,128)(2,1)}, u32[]{:S(2)}, u32[]{:S(2)}) collective-permute-start(bf16[512,768]{1,0:T(8,128)(2,1)S(1)} %collective-permute-done.refs_1_), channel_id=1, source_target_pairs={{1,2},{2,1},{5,6},{6,5},{9,10},{10,9},{13,14},{14,13},{17,18},{18,... | collective-permute-start | bytes 2359304 | tf_op jit(solution)/shard_map/ppermute | solution.py:374
  35.5 17.2 %collective-permute-start.3 = (bf16[512,768]{1,0:T(8,128)(2,1)S(1)}, bf16[512,768]{1,0:T(8,128)(2,1)S(1)}, u32[]{:S(2)}, u32[]{:S(2)}) collective-permute-start(bf16[512,768]{1,0:T(8,128)(2,1)S(1)} %collective-permute-done.1.refs_2_), channel_id=1, source_target_pairs={{1,0},{2,3},{5,4},{6,7},{9,8},{10,11},{13,12},{14,15},{17,16},{18,... | collective-permute-start | bytes 2359304 | tf_op jit(solution)/shard_map/ppermute | solution.py:374
  53.6 19.7 %collective-permute-start.4 = (bf16[512,768]{1,0:T(8,128)(2,1)}, bf16[512,768]{1,0:T(8,128)(2,1)}, u32[]{:S(2)}, u32[]{:S(2)}) collective-permute-start(bf16[512,768]{1,0:T(8,128)(2,1)} %collective-permute-done.2.refs_3_), channel_id=1, source_target_pairs={{1,0},{2,3},{5,4},{6,7},{9,8},{10,11},{13,12},{14,15},{17,16},{18,... | collective-permute-start | bytes 2359304 | tf_op jit(solution)/shard_map/ppermute | solution.py:374
  60.5 209.1 %reduce-scatter.5.cloned.1.call-start = ((), (), s32[]{:S(2)}) async-start(), calls=%async_computation.2 | async-start | bytes 1179648 | tf_op jit(solution)/shard_map/reduce_scatter | solution.py:513
  73.3 38.8 %collective-permute-start.5 = (bf16[512,768]{1,0:T(8,128)(2,1)}, bf16[512,768]{1,0:T(8,128)(2,1)}, u32[]{:S(2)}, u32[]{:S(2)}) collective-permute-start(bf16[512,768]{1,0:T(8,128)(2,1)} %pad_maximum_fusion.2.refs_0_), channel_id=1, source_target_pairs={{0,1},{1,0},{2,3},{3,2},{4,5},{5,4},{6,7},{7,6},{8,9},{9,8},{10,11... | collective-permute-start | bytes 2359304 | tf_op jit(solution)/shard_map/ppermute | solution.py:374
  75.8 36.4 %collective-permute-start.6 = (bf16[512,768]{1,0:T(8,128)(2,1)}, bf16[512,768]{1,0:T(8,128)(2,1)}, u32[]{:S(2)}, u32[]{:S(2)}) collective-permute-start(bf16[512,768]{1,0:T(8,128)(2,1)} %pad_maximum_fusion.2.refs_0_), channel_id=1, source_target_pairs={{1,2},{2,1},{5,6},{6,5},{9,10},{10,9},{13,14},{14,13},{17,18},{18,... | collective-permute-start | bytes 2359304 | tf_op jit(solution)/shard_map/ppermute | solution.py:374
  86.7 71.9 %copy-start.1 = (bf16[1,256,2048]{2,1,0:T(8,128)(2,1)S(1)}, bf16[1,256,2048]{2,1,0:T(8,128)(2,1)}, u32[]{:S(2)}) copy-start(bf16[1,256,2048]{2,1,0:T(8,128)(2,1)} %param.43) | copy-start | bytes 3145732
  86.7 49.4 %collective-permute-start.11 = (bf16[256,2048]{1,0:T(8,128)(2,1)S(1)}, bf16[256,2048]{1,0:T(8,128)(2,1)}, u32[]{:S(2)}, u32[]{:S(2)}) collective-permute-start(bf16[256,2048]{1,0:T(8,128)(2,1)S(1)} %bitcast.48), channel_id=1, source_target_pairs={{0,1},{3,2},{4,5},{7,6},{8,9},{11,10},{12,13},{15,14},{16,17},{19,... | collective-permute-start | bytes 3145736 | tf_op jit(solution)/shard_map/ppermute | solution.py:374
  112.1 49.2 %copy-start.18 = (bf16[512,512]{1,0:T(8,128)(2,1)}, bf16[512,512]{1,0:T(8,128)(2,1)S(1)}, u32[]{:S(2)}) copy-start(bf16[512,512]{1,0:T(8,128)(2,1)S(1)} %get-tuple-element.105.q_ref) | copy-start | bytes 1572868
  112.1 68.8 %collective-permute-start.7 = (bf16[2,256,2048]{2,1,0:T(8,128)(2,1)}, bf16[2,256,2048]{2,1,0:T(8,128)(2,1)}, u32[]{:S(2)}, u32[]{:S(2)}) collective-permute-start(bf16[2,256,2048]{2,1,0:T(8,128)(2,1)} %bitcast.63), channel_id=1, source_target_pairs={{3,2},{7,6},{11,10},{15,14},{19,18},{23,22},{27,26},{31,30}} | collective-permute-start | bytes 6291464 | tf_op jit(solution)/shard_map/ppermute | solution.py:374
  113.4 22.7 %collective-permute-start.8 = (bf16[512,768]{1,0:T(8,128)(2,1)}, bf16[512,768]{1,0:T(8,128)(2,1)}, u32[]{:S(2)}, u32[]{:S(2)}) collective-permute-start(bf16[512,768]{1,0:T(8,128)(2,1)} %collective-permute-done.5.refs_1_), channel_id=1, source_target_pairs={{1,2},{2,1},{5,6},{6,5},{9,10},{10,9},{13,14},{14,13},{17,18},{18,... | collective-permute-start | bytes 2359304 | tf_op jit(solution)/shard_map/ppermute | solution.py:374
  116.7 19.4 %collective-permute-start.9 = (bf16[512,768]{1,0:T(8,128)(2,1)}, bf16[512,768]{1,0:T(8,128)(2,1)S(1)}, u32[]{:S(2)}, u32[]{:S(2)}) collective-permute-start(bf16[512,768]{1,0:T(8,128)(2,1)} %collective-permute-done.6.refs_2_), channel_id=1, source_target_pairs={{1,0},{2,3},{5,4},{6,7},{9,8},{10,11},{13,12},{14,15},{17,16},{18,... | collective-permute-start | bytes 2359304 | tf_op jit(solution)/shard_map/ppermute | solution.py:374
  122.1 36.5 %collective-permute-start.13 = (bf16[256,2048]{1,0:T(8,128)(2,1)S(1)}, bf16[256,2048]{1,0:T(8,128)(2,1)}, u32[]{:S(2)}, u32[]{:S(2)}) collective-permute-start(bf16[256,2048]{1,0:T(8,128)(2,1)S(1)} %bitcast.49), channel_id=1, source_target_pairs={{1,2},{2,1},{5,6},{6,5},{9,10},{10,9},{13,14},{14,13},{17,18},{18,... | collective-permute-start | bytes 3145736 | tf_op jit(solution)/shard_map/ppermute | solution.py:374
  137.0 39.3 %collective-permute-start.12 = (bf16[256,2048]{1,0:T(8,128)(2,1)}, bf16[256,2048]{1,0:T(8,128)(2,1)}, u32[]{:S(2)}, u32[]{:S(2)}) collective-permute-start(bf16[256,2048]{1,0:T(8,128)(2,1)} %collective-permute-done.11.refs_1_), channel_id=1, source_target_pairs={{1,2},{2,1},{5,6},{6,5},{9,10},{10,9},{13,14},{14,13},{17,18},{18,... | collective-permute-start | bytes 3145736 | tf_op jit(solution)/shard_map/ppermute | solution.py:374
  140.3 21.0 %collective-permute-start.10 = (bf16[512,768]{1,0:T(8,128)(2,1)}, bf16[512,768]{1,0:T(8,128)(2,1)}, u32[]{:S(2)}, u32[]{:S(2)}) collective-permute-start(bf16[512,768]{1,0:T(8,128)(2,1)} %collective-permute-done.8.refs_3_), channel_id=1, source_target_pairs={{1,0},{2,3},{5,4},{6,7},{9,8},{10,11},{13,12},{14,15},{17,16},{18,... | collective-permute-start | bytes 2359304 | tf_op jit(solution)/shard_map/ppermute | solution.py:374
  142.8 273.9 %all-gather.3.cloned.1.call-start = ((), (), s32[]{:S(2)}) async-start(), calls=%async_computation.3 | async-start | bytes 1769472 | tf_op jit(solution)/shard_map/all_gather | solution.py:520
  176.3 67.8 %collective-permute-start.14 = (bf16[256,2048]{1,0:T(8,128)(2,1)}, bf16[256,2048]{1,0:T(8,128)(2,1)}, u32[]{:S(2)}, u32[]{:S(2)}) collective-permute-start(bf16[256,2048]{1,0:T(8,128)(2,1)} %get-tuple-element.113), channel_id=1, source_target_pairs={{1,0},{2,3},{5,4},{6,7},{9,8},{10,11},{13,12},{14,15},{17,16},{18,... | collective-permute-start | bytes 3145736 | tf_op jit(solution)/shard_map/ppermute | solution.py:374
  178.7 67.2 %collective-permute-start.15 = (bf16[256,2048]{1,0:T(8,128)(2,1)}, bf16[256,2048]{1,0:T(8,128)(2,1)}, u32[]{:S(2)}, u32[]{:S(2)}) collective-permute-start(bf16[256,2048]{1,0:T(8,128)(2,1)} %collective-permute-done.12.refs_3_), channel_id=1, source_target_pairs={{1,0},{2,3},{5,4},{6,7},{9,8},{10,11},{13,12},{14,15},{17,16},{18,... | collective-permute-start | bytes 3145736 | tf_op jit(solution)/shard_map/ppermute | solution.py:374
  206.8 67.1 %collective-permute-start.19 = (bf16[1,256,2048]{2,1,0:T(8,128)(2,1)}, bf16[1,256,2048]{2,1,0:T(8,128)(2,1)}, u32[]{:S(2)}, u32[]{:S(2)}) collective-permute-start(bf16[1,256,2048]{2,1,0:T(8,128)(2,1)} %get-tuple-element.181), channel_id=1, source_target_pairs={{0,1},{4,5},{8,9},{12,13},{16,17},{20,21},{24,25},{28,29}} | collective-permute-start | bytes 3145736 | tf_op jit(solution)/shard_map/ppermute | solution.py:374
  208.4 75.8 %collective-permute-start.18 = (bf16[2,256,2048]{2,1,0:T(8,128)(2,1)}, bf16[2,256,2048]{2,1,0:T(8,128)(2,1)}, u32[]{:S(2)}, u32[]{:S(2)}) collective-permute-start(bf16[2,256,2048]{2,1,0:T(8,128)(2,1)} %add_convert_fusion), channel_id=1, source_target_pairs={{2,1},{6,5},{10,9},{14,13},{18,17},{22,21},{26,25},{30,29}} | collective-permute-start | bytes 6291464 | tf_op jit(solution)/shard_map/ppermute | solution.py:374
  243.4 59.5 %collective-permute-start.16 = (bf16[1,256,2048]{2,1,0:T(8,128)(2,1)}, bf16[1,256,2048]{2,1,0:T(8,128)(2,1)S(1)}, u32[]{:S(2)}, u32[]{:S(2)}) collective-permute-start(bf16[1,256,2048]{2,1,0:T(8,128)(2,1)} %slice.56), channel_id=1, source_target_pairs={{0,1},{4,5},{8,9},{12,13},{16,17},{20,21},{24,25},{28,29}} | collective-permute-start | bytes 3145736 | tf_op jit(solution)/shard_map/ppermute | solution.py:374
  244.1 38.8 %collective-permute-start.20 = (bf16[1,256,2048]{2,1,0:T(8,128)(2,1)}, bf16[1,256,2048]{2,1,0:T(8,128)(2,1)}, u32[]{:S(2)}, u32[]{:S(2)}) collective-permute-start(bf16[1,256,2048]{2,1,0:T(8,128)(2,1)} %get-tuple-element.182), channel_id=1, source_target_pairs={{0,1},{4,5},{8,9},{12,13},{16,17},{20,21},{24,25},{28,29}} | collective-permute-start | bytes 3145736 | tf_op jit(solution)/shard_map/ppermute | solution.py:374
  272.4 82.8 %collective-permute-start.31 = (bf16[2,512,768]{2,1,0:T(8,128)(2,1)}, bf16[2,512,768]{2,1,0:T(8,128)(2,1)}, u32[]{:S(2)}, u32[]{:S(2)}) collective-permute-start(bf16[2,512,768]{2,1,0:T(8,128)(2,1)} %constant_dynamic-slice_fusion), channel_id=1, source_target_pairs={{0,1},{3,2},{4,5},{7,6},{8,9},{11,10},{12,13},{15,14},{16,17},{19,... | collective-permute-start | bytes 4718600 | tf_op jit(solution)/shard_map/ppermute | solution.py:374
  276.5 22.7 %collective-permute-start.37 = (bf16[1,256,2048]{2,1,0:T(8,128)(2,1)}, bf16[1,256,2048]{2,1,0:T(8,128)(2,1)}, u32[]{:S(2)}, u32[]{:S(2)}) collective-permute-start(bf16[1,256,2048]{2,1,0:T(8,128)(2,1)} %fusion), channel_id=1, source_target_pairs={{1,2},{5,6},{9,10},{13,14},{17,18},{21,22},{25,26},{29,30}} | collective-permute-start | bytes 3145736 | tf_op jit(solution)/shard_map/ppermute | solution.py:374
  280.7 162.3 %all-gather.5.cloned.1.call-start = ((), (), s32[]{:S(2)}) async-start(), calls=%async_computation.4 | async-start | bytes 1179648 | tf_op jit(solution)/shard_map/all_gather | solution.py:521
  283.0 45.9 %collective-permute-start.17 = (bf16[1,256,2048]{2,1,0:T(8,128)(2,1)}, bf16[1,256,2048]{2,1,0:T(8,128)(2,1)S(1)}, u32[]{:S(2)}, u32[]{:S(2)}) collective-permute-start(bf16[1,256,2048]{2,1,0:T(8,128)(2,1)} %get-tuple-element.182), channel_id=1, source_target_pairs={{3,2},{7,6},{11,10},{15,14},{19,18},{23,22},{27,26},{31,30}} | collective-permute-start | bytes 3145736 | tf_op jit(solution)/shard_map/ppermute | solution.py:374
  284.3 45.6 %collective-permute-start.21 = (bf16[256,2048]{1,0:T(8,128)(2,1)}, bf16[256,2048]{1,0:T(8,128)(2,1)S(1)}, u32[]{:S(2)}, u32[]{:S(2)}) collective-permute-start(bf16[256,2048]{1,0:T(8,128)(2,1)} %get-tuple-element.121), channel_id=1, source_target_pairs={{1,0},{2,3},{5,4},{6,7},{9,8},{10,11},{13,12},{14,15},{17,16},{18,... | collective-permute-start | bytes 3145736 | tf_op jit(solution)/shard_map/ppermute | solution.py:374
  351.3 15.8 %collective-permute-start.27 = (bf16[1,512,768]{2,1,0:T(8,128)(2,1)S(1)}, bf16[1,512,768]{2,1,0:T(8,128)(2,1)S(1)}, u32[]{:S(2)}, u32[]{:S(2)}) collective-permute-start(bf16[1,512,768]{2,1,0:T(8,128)(2,1)S(1)} %constant_dynamic-slice_fusion.1), channel_id=1, source_target_pairs={{0,1},{3,2},{4,5},{7,6},{8,9},{11,10},{12,13},{15,14},{16,17},{19,... | collective-permute-start | bytes 2359304 | tf_op jit(solution)/shard_map/ppermute | solution.py:374
  358.7 39.6 %collective-permute-start.32 = (bf16[2,512,768]{2,1,0:T(8,128)(2,1)}, bf16[2,512,768]{2,1,0:T(8,128)(2,1)S(1)}, u32[]{:S(2)}, u32[]{:S(2)}) collective-permute-start(bf16[2,512,768]{2,1,0:T(8,128)(2,1)} %add_convert_fusion.1), channel_id=1, source_target_pairs={{1,2},{2,1},{5,6},{6,5},{9,10},{10,9},{13,14},{14,13},{17,18},{18,... | collective-permute-start | bytes 4718600 | tf_op jit(solution)/shard_map/ppermute | solution.py:374
  369.6 15.2 %collective-permute-start.29 = (bf16[1,512,768]{2,1,0:T(8,128)(2,1)}, bf16[1,512,768]{2,1,0:T(8,128)(2,1)}, u32[]{:S(2)}, u32[]{:S(2)}) collective-permute-start(bf16[1,512,768]{2,1,0:T(8,128)(2,1)} %get-tuple-element.171), channel_id=1, source_target_pairs={{0,1},{3,2},{4,5},{7,6},{8,9},{11,10},{12,13},{15,14},{16,17},{19,... | collective-permute-start | bytes 2359304 | tf_op jit(solution)/shard_map/ppermute | solution.py:374
  370.8 31.0 %collective-permute-start.24 = (f32[2048]{0:T(1024)S(1)}, f32[2048]{0:T(1024)S(1)}, u32[]{:S(2)}, u32[]{:S(2)}) collective-permute-start(f32[2048]{0:T(1024)S(1)} %bitcast.57), channel_id=1, source_target_pairs={{0,4},{4,0},{8,12},{12,8},{16,20},{20,16},{24,28},{28,24},{1,5},{5... | collective-permute-start | bytes 24584 | tf_op jit(solution)/shard_map/ppermute | solution.py:434
  387.2 32.1 %collective-permute-start.30 = (bf16[1,512,768]{2,1,0:T(8,128)(2,1)}, bf16[1,512,768]{2,1,0:T(8,128)(2,1)}, u32[]{:S(2)}, u32[]{:S(2)}) collective-permute-start(bf16[1,512,768]{2,1,0:T(8,128)(2,1)} %add_convert_fusion.6), channel_id=1, source_target_pairs={{1,2},{2,1},{5,6},{6,5},{9,10},{10,9},{13,14},{14,13},{17,18},{18,... | collective-permute-start | bytes 2359304 | tf_op jit(solution)/shard_map/ppermute | solution.py:374
  400.4 24.3 %collective-permute-start.33 = (bf16[1,512,768]{2,1,0:T(8,128)(2,1)}, bf16[1,512,768]{2,1,0:T(8,128)(2,1)}, u32[]{:S(2)}, u32[]{:S(2)}) collective-permute-start(bf16[1,512,768]{2,1,0:T(8,128)(2,1)} %add_convert_fusion.4), channel_id=1, source_target_pairs={{0,1},{1,0},{2,3},{3,2},{4,5},{5,4},{6,7},{7,6},{8,9},{9,8},{10,11... | collective-permute-start | bytes 2359304 | tf_op jit(solution)/shard_map/ppermute | solution.py:374
  401.8 3.7 collective-permute-start.25
  403.2 11.8 %collective-permute-start.22 = (f32[2048]{0:T(1024)S(1)}, f32[2048]{0:T(1024)S(1)}, u32[]{:S(2)}, u32[]{:S(2)}) collective-permute-start(f32[2048]{0:T(1024)S(1)} %bitcast.90), channel_id=1, source_target_pairs={{0,1},{1,0},{2,3},{3,2},{4,5},{5,4},{6,7},{7,6},{8,9},{9,8},{10,11... | collective-permute-start | bytes 24584 | tf_op jit(solution)/shard_map/ppermute | solution.py:434
  405.5 30.8 %collective-permute-start.26 = (f32[2048]{0:T(1024)S(1)}, f32[2048]{0:T(1024)S(1)}, u32[]{:S(2)}, u32[]{:S(2)}) collective-permute-start(f32[2048]{0:T(1024)S(1)} %add.153), channel_id=1, source_target_pairs={{0,16},{4,20},{8,24},{12,28},{16,0},{20,4},{24,8},{28,12},{1,17},{... | collective-permute-start | bytes 24584 | tf_op jit(solution)/shard_map/ppermute | solution.py:434
  407.9 35.2 %collective-permute-start.35 = (bf16[1,256,2048]{2,1,0:T(8,128)(2,1)}, bf16[1,256,2048]{2,1,0:T(8,128)(2,1)}, u32[]{:S(2)}, u32[]{:S(2)}) collective-permute-start(bf16[1,256,2048]{2,1,0:T(8,128)(2,1)} %get-tuple-element.178), channel_id=1, source_target_pairs={{1,2},{5,6},{9,10},{13,14},{17,18},{21,22},{25,26},{29,30}} | collective-permute-start | bytes 3145736 | tf_op jit(solution)/shard_map/ppermute | solution.py:374
  415.0 28.1 %collective-permute-start.36 = (bf16[1,256,2048]{2,1,0:T(8,128)(2,1)}, bf16[1,256,2048]{2,1,0:T(8,128)(2,1)}, u32[]{:S(2)}, u32[]{:S(2)}) collective-permute-start(bf16[1,256,2048]{2,1,0:T(8,128)(2,1)} %add_convert_fusion.3), channel_id=1, source_target_pairs={{1,0},{5,4},{9,8},{13,12},{17,16},{21,20},{25,24},{29,28}} | collective-permute-start | bytes 3145736 | tf_op jit(solution)/shard_map/ppermute | solution.py:374
  419.3 25.5 %collective-permute-start.38 = (bf16[1,256,2048]{2,1,0:T(8,128)(2,1)}, bf16[1,256,2048]{2,1,0:T(8,128)(2,1)}, u32[]{:S(2)}, u32[]{:S(2)}) collective-permute-start(bf16[1,256,2048]{2,1,0:T(8,128)(2,1)} %get-tuple-element.177), channel_id=1, source_target_pairs={{2,3},{6,7},{10,11},{14,15},{18,19},{22,23},{26,27},{30,31}} | collective-permute-start | bytes 3145736 | tf_op jit(solution)/shard_map/ppermute | solution.py:374
  424.7 15.8 %collective-permute-start.23 = (f32[2048]{0:T(1024)S(1)}, f32[2048]{0:T(1024)S(1)}, u32[]{:S(2)}, u32[]{:S(2)}) collective-permute-start(f32[2048]{0:T(1024)S(1)} %add.145), channel_id=1, source_target_pairs={{0,2},{1,3},{2,0},{3,1},{4,6},{5,7},{6,4},{7,5},{8,10},{9,11},{10,... | collective-permute-start | bytes 24584 | tf_op jit(solution)/shard_map/ppermute | solution.py:434
  436.3 18.0 %collective-permute-start.28 = (bf16[1,512,768]{2,1,0:T(8,128)(2,1)}, bf16[1,512,768]{2,1,0:T(8,128)(2,1)S(1)}, u32[]{:S(2)}, u32[]{:S(2)}) collective-permute-start(bf16[1,512,768]{2,1,0:T(8,128)(2,1)} %get-tuple-element.170), channel_id=1, source_target_pairs={{1,2},{2,1},{5,6},{6,5},{9,10},{10,9},{13,14},{14,13},{17,18},{18,... | collective-permute-start | bytes 2359304 | tf_op jit(solution)/shard_map/ppermute | solution.py:374
  440.5 13.9 %collective-permute-start.34 = (bf16[1,512,768]{2,1,0:T(8,128)(2,1)}, bf16[1,512,768]{2,1,0:T(8,128)(2,1)}, u32[]{:S(2)}, u32[]{:S(2)}) collective-permute-start(bf16[1,512,768]{2,1,0:T(8,128)(2,1)} %add_convert_fusion.5), channel_id=1, source_target_pairs={{0,1},{1,0},{2,3},{3,2},{4,5},{5,4},{6,7},{7,6},{8,9},{9,8},{10,11... | collective-permute-start | bytes 2359304 | tf_op jit(solution)/shard_map/ppermute | solution.py:374
  (64 other events, 949.5 us)
Sparse Core Ops, SparseCore 0:
  60.6 37.5 reduce-scatter.6
  142.9 35.0 reduce-scatter.4
  280.9 28.3 all-gather.2
  376.2 25.7 all-gather.4
